TPU v7x, 32 devices: a whole 2x2x4 slice. The times are simulated.
32 devices in a mesh: dp: 8 (over z, y), bal: 4 (over x, core).
Axes of the slice: x: 2, y: 2, z: 4, core: 2. Of those that a mesh axis runs over, the one named last changes fastest.
Arguments:
- tokens: bfloat16 [4, 128, 225, 768], P(None, ('dp', 'bal')), may hold values from -6 to 6
- cotangent: bfloat16 [4, 128, 225, 768], P(None, ('dp', 'bal')), may hold values from -6 to 6
- counts: int32 [4, 128], P(None, ('dp', 'bal')), may hold values from 56 to 225, as said below
- rows: int32 [4, 128, 225], P(None, ('dp', 'bal')), may hold values from 0 to 14, as said below
- cols: int32 [4, 128, 225], P(None, ('dp', 'bal')), may hold values from 0 to 14, as said below
- present: int32 [4, 128], P(None, ('dp', 'bal')), may hold values 0 or 1
- slots: int32 [4, 128], P(None, ('dp', 'bal')), may hold values from 0 to 15, as said below
- first_gain: float32 [768], replicated, may hold values from 0.25 to 1.75
- first_shift: float32 [768], replicated, may hold values from -1.75 to 1.75
- qkv_weight: bfloat16 [768, 2304], replicated, may hold values from -0.21875 to 0.21875
- query_bias: float32 [768], replicated, may hold values from -1.75 to 1.75
- value_bias: float32 [768], replicated, may hold values from -1.75 to 1.75
- out_weight: bfloat16 [768, 768], replicated, may hold values from -0.625 to 0.625
- out_bias: float32 [768], replicated, may hold values from -1.75 to 1.75
- second_gain: float32 [768], replicated, may hold values from 0.25 to 1.75
- second_shift: float32 [768], replicated, may hold values from -1.75 to 1.75
- up_weight: bfloat16 [768, 3072], replicated, may hold values from -0.21875 to 0.21875
- up_bias: float32 [3072], replicated, may hold values from -1.75 to 1.75
- down_weight: bfloat16 [3072, 768], replicated, may hold values from -0.109375 to 0.109375
- down_bias: float32 [768], replicated, may hold values from -1.75 to 1.75
Outputs:
- block_output: bfloat16 [4, 128, 225, 768], P(None, ('dp', 'bal'))
- tokens_grad: float32 [4, 128, 225, 768], P(None, ('dp', 'bal'))
- first_gain_grad: float32 [768], replicated
- first_shift_grad: float32 [768], replicated
- qkv_weight_grad: float32 [768, 2304], P('dp')
- query_bias_grad: float32 [768], replicated
- value_bias_grad: float32 [768], replicated
- out_weight_grad: float32 [768, 768], P('dp')
- out_bias_grad: float32 [768], replicated
- second_gain_grad: float32 [768], replicated
- second_shift_grad: float32 [768], replicated
- up_weight_grad: float32 [768, 3072], P('dp')
- up_bias_grad: float32 [3072], replicated
- down_weight_grad: float32 [3072, 768], P('dp')
- down_bias_grad: float32 [768], replicated
Inputs may be any that keep to these rules, and one draw needn't show every extreme that they name: `counts`: every image has at least 56 visible patches; in every draw some image has all 225. In each image the pairs (rows, cols) over the 225 slots are the cells of a 15 x 15 grid, each once. `cols`: paired with rows as stated there. Within each aligned block of 16 images of a micro-batch the slots are a permutation of 0 to 15. Split such a block into runs of 4 images in order. For every pair of runs a and b, exactly one image of run a has a slot in [b * 4, (b + 1) * 4).
All inputs are finite; a program needn't handle non-finite values. No bound on the sum of `present` on one device may be relied on, other than what follows from the above.
Results may differ from a plain program's by a relative error of at most 0.014.
Values may be sent and summed in bfloat16 or wider, within the bound.
A program may use at most 512 MiB of HBM per device.

v0:
```python
import functools
import math

import jax
import jax.numpy as jnp
from jax import lax
from jax.experimental import pallas as pl
from jax.experimental.pallas import tpu as pltpu
from jax.sharding import PartitionSpec as P

HEADS = 12
TILE = 256
WINDOW = 256
FAR = 1e12
EPS = 1e-06
BLOCKS = 8
CHUNK = 1536
VMEM_LIMIT = 60 * 1024 * 1024

F32 = jnp.float32
BF16 = jnp.bfloat16

OFF, CNT, IMG, LIVE, PEER, SPOT, MISC = 0, 16, 32, 48, 64, 80, 96
N_FWD, N_BWD, ROWS_FWD, ROWS_BWD, N_LIVE, CORE = range(MISC, MISC + 6)
PLACES = 128

GAIN_ONE, SHIFT_ONE, QKV_B, OUT_B, GAIN_TWO, SHIFT_TWO, DOWN_B, UP_B = 0, 1, 2, 5, 6, 7, 8, 9
VECTORS = (GAIN_ONE, SHIFT_ONE, QKV_B, QKV_B + 2, OUT_B, GAIN_TWO, SHIFT_TWO, DOWN_B, UP_B)


def dot(a, b):
    return jnp.dot(a, b, preferred_element_type=F32)


def dot_bt(a, b):
    return lax.dot_general(a, b, (((1,), (1,)), ((), ())), preferred_element_type=F32)


def turned(block):
    size = 256 if block.shape[1] % 256 == 0 else 128
    row = lax.broadcasted_iota(jnp.int32, (size, size), 0)
    col = lax.broadcasted_iota(jnp.int32, (size, size), 1)
    eye = jnp.where(row == col, 1.0, 0.0).astype(BF16)
    parts = [
        dot_bt(eye, block[:, start : start + size]).astype(BF16)
        for start in range(0, block.shape[1], size)
    ]
    return parts[0] if len(parts) == 1 else jnp.concatenate(parts, axis=0)


def layer_norm(values):
    average = jnp.mean(values, axis=-1, keepdims=True)
    centred = values - average
    spread = jnp.mean(centred * centred, axis=-1, keepdims=True)
    inverse = lax.rsqrt(spread + EPS)
    return centred * inverse, inverse


def norm_back(out_grad, gain, unit, inverse):
    e = out_grad * gain
    mean_e = jnp.mean(e, axis=-1, keepdims=True)
    mean_eu = jnp.mean(e * unit, axis=-1, keepdims=True)
    return inverse * (e - mean_e - unit * mean_eu)


def gelu_parts(u):
    size = jnp.abs(u)
    t = 1.0 / (1.0 + (0.3275911 * math.sqrt(0.5)) * size)
    bell = jnp.exp(-0.5 * (u * u))
    poly = t * (
        0.5 * 0.254829592
        + t
        * (
            0.5 * -0.284496736
            + t * (0.5 * 1.421413741 + t * (0.5 * -1.453152027 + t * (0.5 * 1.061405429)))
        )
    )
    tail = poly * bell
    phi_sum = jnp.where(u >= 0, 1.0 - tail, tail)
    return phi_sum, u * bell * (1.0 / math.sqrt(2.0 * math.pi))


def put_rows(packed, off, count, block):
    rows = (block.shape[0] + 15) // 16 * 16
    if rows > block.shape[0]:
        more = jnp.zeros((rows - block.shape[0], block.shape[1]), block.dtype)
        block = jnp.concatenate([block, more], axis=0)
    ids = row_ids(0, rows)
    window = pl.ds(off, rows)
    block = jnp.where(ids < count, block, jnp.zeros_like(block))
    packed[window, :] = jnp.where(ids < (count + 15) // 16 * 16, block, packed[window, :])


def row_ids(start, rows):
    return start + lax.broadcasted_iota(jnp.int32, (rows, 1), 0)


def aligned(value, step=16):
    return pl.multiple_of(value, step)


def by_count(count, run):
    @pl.when(count <= 128)
    def _():
        run(128, 128)

    @pl.when(jnp.logical_and(count > 128, count <= 192))
    def _():
        run(192, 256)

    @pl.when(count > 192)
    def _():
        run(256, 256)


def distances(rows, cols, which, count, keys, queries):
    mine = lax.broadcasted_iota(jnp.int32, rows.shape, 0) == which
    row = jnp.sum(jnp.where(mine, rows, 0).astype(F32), axis=0, keepdims=True)
    col = jnp.sum(jnp.where(mine, cols, 0).astype(F32), axis=0, keepdims=True)
    spots = jnp.concatenate([row, col, jnp.zeros((6, row.shape[1]), F32)], axis=0)
    spots = jnp.concatenate([spots, jnp.zeros((8, WINDOW - row.shape[1]), F32)], axis=1)
    eye = jnp.where(
        lax.broadcasted_iota(jnp.int32, (keys, WINDOW), 0)
        == lax.broadcasted_iota(jnp.int32, (keys, WINDOW), 1),
        1.0,
        0.0,
    ).astype(BF16)
    turned_spots = dot_bt(eye, spots.astype(BF16))
    down = turned_spots[:, 0:1] - spots[0:1, :queries]
    across = turned_spots[:, 1:2] - spots[1:2, :queries]
    far = row_ids(0, keys) >= count
    return jnp.where(far, FAR, jnp.sqrt(down * down + across * across))


def prepare_kernel(every, counts, present, slots, me, cot, *rest):
    *lines, meta, take, vecs, send = rest
    step = pl.program_id(0)
    steps, length, images, width = pl.num_programs(0), cot.shape[1], cot.shape[2], cot.shape[3]
    group = every.shape[0]

    @pl.when(step == 0)
    def _():
        def fill(live):
            def body(img, carry):
                spot, off = carry
                m, i = img // images, img % images
                count = counts[m, i]
                mine = present[m, i] == live

                @pl.when(mine)
                def _():
                    meta[OFF + spot] = off
                    meta[CNT + spot] = count
                    meta[IMG + spot] = img
                    meta[LIVE + spot] = live
                    meta[PEER + spot] = slots[m, i] // images * steps + m
                    meta[SPOT + img] = spot

                padded = (count + 15) // 16 * 16
                return spot + mine.astype(jnp.int32), off + jnp.where(mine, padded, 0)

            return body

        meta[CORE] = me[0] % 2
        vecs[...] = jnp.zeros_like(vecs)
        for row, values in zip(VECTORS, lines):
            for n in range(values.shape[0] // width):
                piece = values[n * width : (n + 1) * width]
                vecs[row + n : row + n + 1, :] = piece.reshape(1, width)
        zero = jnp.int32(0)
        total = counts.shape[0] * images
        spot, off = lax.fori_loop(0, total, fill(1), (zero, zero))
        meta[N_LIVE] = spot
        meta[ROWS_BWD] = off
        meta[N_BWD] = (off + TILE - 1) // TILE
        spot, off = lax.fori_loop(0, total, fill(0), (spot, off))
        meta[ROWS_FWD] = off
        meta[N_FWD] = (off + TILE - 1) // TILE

        def land(n, carry):
            a, m, i = n // total, n % total // images, n % images
            slot = every[a, m, i]

            @pl.when(slot // images == me[0])
            def _():
                take[m * images + slot % images] = a * steps + m

            return carry

        lax.fori_loop(0, group * total, land, 0)

    block = jnp.swapaxes(cot[0].astype(F32), 0, 1).astype(BF16)
    for place in range(images):
        peer = take[step * images + place] // steps
        send[peer, 0, :length, :] = block[place]


def place_kernel(take, got, out):
    step = pl.program_id(0)
    length, images = out.shape[1], out.shape[2]
    steps = pl.num_programs(0)
    parts = [
        got[take[step * images + place] // steps, 0, :length, :].astype(F32)
        for place in range(images)
    ]
    out[0] = jnp.swapaxes(jnp.stack(parts, axis=0), 0, 1).astype(out.dtype)


def attend_kernel(
    meta, slopes, tokens, rows_in, cols_in, vecs, weight,
    packed_out, qkv_out, att_out, total_out,
    packed, qkv, att, gaps, sem_packed, sem_qkv, sem_att,
):
    length, per, width = tokens.shape[1], tokens.shape[2], tokens.shape[3]
    steps = pl.num_programs(0) // (per + 1)
    images = steps * per
    now = pl.program_id(0)

    def tile_copy(which, t):
        src, dst, sem = (
            (packed, packed_out, sem_packed),
            (qkv, qkv_out, sem_qkv),
            (att, att_out, sem_att),
        )[which]
        rows = pl.ds(aligned(t * TILE, TILE), TILE)
        return pltpu.make_async_copy(src.at[rows], dst.at[rows], sem.at[t])

    @pl.when(now == 0)
    def _():
        packed[...] = jnp.zeros_like(packed)

    @pl.when(now < steps)
    def _():
        block = jnp.swapaxes(tokens[0].astype(F32), 0, 1).astype(BF16)
        for i in range(per):
            spot = meta[SPOT + now * per + i]
            put_rows(packed, aligned(meta[OFF + spot]), meta[CNT + spot], block[i])

    @pl.when(now == steps - 1)
    def _():

        def project(t, carry):
            rows = pl.ds(aligned(t * TILE, TILE), TILE)
            unit, _ = layer_norm(packed[rows, :].astype(F32))
            hidden = (
                unit * vecs[GAIN_ONE : GAIN_ONE + 1] + vecs[SHIFT_ONE : SHIFT_ONE + 1]
            ).astype(BF16)
            for part in range(3):
                cols = slice(part * width, (part + 1) * width)
                bias = vecs[QKV_B + part : QKV_B + part + 1]
                qkv[rows, cols] = (dot(hidden, weight[:, cols]) + bias).astype(BF16)
            tile_copy(0, t).start()
            tile_copy(1, t).start()
            return carry

        lax.fori_loop(0, meta[N_FWD], project, 0)

    @pl.when(now >= steps)
    def _():
        spot = now - steps
        off = aligned(meta[OFF + spot])
        count = meta[CNT + spot]

        def run(keys, queries):
            which = meta[IMG + spot] % per
            gaps[:keys, :queries] = distances(rows_in[0], cols_in[0], which, count, keys, queries)
            key_seen = row_ids(0, keys) < count
            query_seen = row_ids(0, queries) < count
            left = lax.broadcasted_iota(jnp.int32, (queries, 128), 1) < 64

            def pair(p, carry):
                lanes = aligned(p * 128, 128)
                q2 = qkv[pl.ds(off, queries), pl.ds(lanes, 128)] * 0.125
                k2 = qkv[pl.ds(off, keys), pl.ds(width + lanes, 128)]
                v2 = qkv[pl.ds(off, keys), pl.ds(2 * width + lanes, 128)]
                q2 = jnp.where(query_seen, q2, jnp.zeros_like(q2))
                k2 = jnp.where(key_seen, k2, jnp.zeros_like(k2))
                v2 = jnp.where(key_seen, v2, jnp.zeros_like(v2))
                v2t = turned(v2)
                outs = []
                for half in range(2):
                    head = 2 * p + half
                    mine = left if half == 0 else jnp.logical_not(left)
                    qh = jnp.where(mine, q2, jnp.zeros_like(q2))
                    scores = dot_bt(k2, qh) - slopes[head] * gaps[:keys, :queries]
                    top = jnp.max(scores, axis=0, keepdims=True)
                    terms = jnp.exp(scores - top)
                    total = jnp.sum(terms, axis=0, keepdims=True)
                    heads_out = dot(v2t[half * 64 : half * 64 + 64], terms.astype(BF16))
                    outs.append((heads_out * (1.0 / total)).astype(BF16))
                    total_out[0, p, half : half + 1, :queries] = top + jnp.log(total)
                both = jnp.concatenate(outs, axis=0)
                att[pl.ds(off, queries), pl.ds(lanes, 128)] = turned_back(both)
                return carry

            lax.fori_loop(0, HEADS // 2, pair, 0, unroll=HEADS // 2)

        by_count(count, run)
        after = meta[OFF + jnp.minimum(spot + 1, images - 1)]
        end = jnp.where(spot == images - 1, meta[N_FWD], after // TILE)

        def send(t, carry):
            tile_copy(2, t).start()
            return carry

        lax.fori_loop(off // TILE, end, send, 0)

    @pl.when(now == pl.num_programs(0) - 1)
    def _():
        def finish(t, carry):
            for which in range(3):
                tile_copy(which, t).wait()
            return carry

        lax.fori_loop(0, meta[N_FWD], finish, 0)


def turned_back(block):
    size = block.shape[1]
    parts = []
    for start in range(0, size, 128):
        row = lax.broadcasted_iota(jnp.int32, (128, size), 0)
        col = lax.broadcasted_iota(jnp.int32, (128, size), 1)
        eye = jnp.where(row + start == col, 1.0, 0.0).astype(BF16)
        parts.append(dot_bt(eye, block).astype(BF16))
    return parts[0] if len(parts) == 1 else jnp.concatenate(parts, axis=0)


def mlp_kernel(
    chunk, length, meta, cot_in, att_in, tokens_in,
    vecs, out_w, up_w, down_w,
    y_send, mid_grad, att_grad, keep_g, send_g, vec_g, upb_g,
    up_b, held, up_acc, down_acc, out_acc, h2_s, h2t_s, dzt_s, z_s, g_s, sem,
):
    step = pl.program_id(0)
    tiles = held.shape[0] // TILE - WINDOW // TILE
    images = (pl.num_programs(0) - tiles) // 2
    per = cot_in.shape[0]
    width = cot_in.shape[3]
    hidden = up_w.shape[1]
    out_b, gain, shift, down_b = [
        vecs.at[pl.ds(n, 1)] for n in (OUT_B, GAIN_TWO, SHIFT_TWO, DOWN_B)
    ]

    @pl.when(step == 0)
    def _():
        up_acc[...] = jnp.zeros_like(up_acc)
        down_acc[...] = jnp.zeros_like(down_acc)
        out_acc[...] = jnp.zeros_like(out_acc)
        vec_g[...] = jnp.zeros_like(vec_g)
        upb_g[...] = jnp.zeros_like(upb_g)
        for n in range(hidden // width):
            up_b[0:1, n * width : (n + 1) * width] = vecs[UP_B + n : UP_B + n + 1, :]

    @pl.when(step < images)
    def _():
        for i in range(per):
            spot = meta[SPOT + step * per + i]

            @pl.when(meta[LIVE + spot] == 1)
            def _():
                put_rows(
                    held, aligned(meta[OFF + spot]), meta[CNT + spot],
                    cot_in[meta[PEER + spot] // images, 0],
                )

    def run_tile(t, both):
        rows = aligned(t * TILE, TILE)
        ids = row_ids(rows, TILE)
        att = att_in[...]
        att = jnp.where(ids < meta[ROWS_FWD], att, jnp.zeros_like(att))
        mid = tokens_in[...].astype(F32) + (dot(att, out_w[...]) + out_b[...])
        unit, inverse = layer_norm(mid)
        h2 = (unit * gain[...] + shift[...]).astype(BF16)
        h2_s[...] = h2
        z_s[...] = mid + down_b[...]
        if both:
            dz = held[pl.ds(rows, TILE), :]
            dz = jnp.where(ids < meta[ROWS_BWD], dz, jnp.zeros_like(dz))
            h2t_s[...] = turned(h2)
            dzt_s[...] = turned(dz)
            g_s[...] = jnp.zeros_like(g_s)

        def part(c, carry):
            cols = pl.ds(aligned(c * chunk, chunk), chunk)
            pre = dot(h2_s[...], up_w[:, cols]) + up_b[0:1, cols]
            share, slope = gelu_parts(pre)
            act = (pre * share).astype(BF16)
            z_s[...] += dot(act, down_w[cols, :])
            if both:
                pre_g = (dot_bt(dz, down_w[cols, :]) * (share + slope)).astype(BF16)
                up_acc[:, cols] += dot(h2t_s[...], pre_g)
                down_acc[:, cols] += dot(dzt_s[...], act)
                upb_g[0:1, cols] += jnp.sum(pre_g.astype(F32), axis=0, keepdims=True)
                g_s[...] += dot_bt(pre_g, up_w[:, cols])
            return carry

        lax.fori_loop(0, hidden // chunk, part, 0)
        held[pl.ds(rows, TILE), :] = z_s[...].astype(BF16)
        if both:
            dzf = dz.astype(F32)
            g2 = g_s[...]
            dmid = dzf + norm_back(g2, gain[...], unit, inverse)
            branch = dmid.astype(BF16)
            mid_grad[...] = dmid
            att_grad[...] = dot_bt(branch, out_w[...]).astype(BF16)
            out_acc[...] += dot(turned(att), branch)
            vec_g[0:1, :] += jnp.sum(g2 * unit, axis=0, keepdims=True)
            vec_g[1:2, :] += jnp.sum(g2, axis=0, keepdims=True)
            vec_g[2:3, :] += jnp.sum(branch.astype(F32), axis=0, keepdims=True)
            vec_g[3:4, :] += jnp.sum(dzf, axis=0, keepdims=True)

    tile = step - images

    @pl.when(jnp.logical_and(tile >= 0, tile < meta[N_BWD]))
    def _():
        run_tile(tile, True)

    @pl.when(
        jnp.logical_and(
            jnp.logical_and(tile >= meta[N_BWD], tile >= 0),
            jnp.logical_and(tile < meta[N_FWD], tile < tiles),
        )
    )
    def _():
        run_tile(tile, False)

    turn = step - images - tiles

    @pl.when(turn >= 0)
    def _():
        for i in range(per):
            spot = meta[SPOT + turn * per + i]
            block = held[pl.ds(aligned(meta[OFF + spot]), length), :]
            seen = row_ids(0, length) < meta[CNT + spot]
            y_send[meta[PEER + spot] // images, 0, :length, :] = jnp.where(
                seen, block, jnp.zeros_like(block)
            )

    @pl.when(step == pl.num_programs(0) - 1)
    def _():
        share = width // BLOCKS
        long = hidden // BLOCKS
        size = 2 * share + long // 2 + share // 2
        for turn, target in enumerate((send_g, keep_g)):
            h = meta[CORE] if turn else 1 - meta[CORE]
            side = aligned(h * (width // 2), 128)
            copies = []
            for n in range(BLOCKS):
                base = n * size
                if turn:
                    earlier[n].wait()
                for c in range(2):
                    cols = pl.ds(aligned((2 * h + c) * width, 128), width)
                    piece = up_acc[n * share : (n + 1) * share, cols]
                    held[base + c * share : base + (c + 1) * share, :] = piece.astype(BF16)
                base += 2 * share
                piece = down_acc[pl.ds(side, width // 2), n * long : (n + 1) * long]
                flipped = turned(piece.astype(BF16))
                held[base : base + long // 2, : width // 2] = flipped[: long // 2]
                held[base : base + long // 2, width // 2 :] = flipped[long // 2 :]
                base += long // 2
                rows = pl.ds(pl.multiple_of(n * share + h * (share // 2), 8), share // 2)
                held[base : base + share // 2, :] = out_acc[rows, :].astype(BF16)
                copy = pltpu.make_async_copy(
                    held.at[pl.ds(n * size, size)], target.at[n], sem.at[turn, n]
                )
                copy.start()
                copies.append(copy)
            earlier = copies
        for copy in earlier:
            copy.wait()


def attend_back_kernel(
    first, per, meta, slopes, qkv, att_grad, totals, rows_in, cols_in, *rest
):
    grads_out, grads, gaps, sem = rest[-4:]
    step = pl.program_id(0)
    width = att_grad.shape[1]
    spot = first + step
    live = spot < meta[N_LIVE]
    slot = step % 2

    def copy(at):
        rows = pl.ds(aligned(meta[OFF + first + at]), WINDOW)
        return pltpu.make_async_copy(grads.at[at % 2], grads_out.at[rows], sem.at[at % 2])

    @pl.when(live)
    def _():
        count = meta[CNT + spot]

        def run(keys, queries):
            which = meta[IMG + spot] % per
            gaps[:keys, :queries] = distances(rows_in[0], cols_in[0], which, count, keys, queries)
            key_seen = row_ids(0, keys) < count
            query_seen = row_ids(0, queries) < count
            left = lax.broadcasted_iota(jnp.int32, (queries, 128), 1) < 64

            def pair(p, carry):
                lanes = aligned(p * 128, 128)
                q2 = qkv[:queries, pl.ds(lanes, 128)] * 0.125
                k2 = qkv[:keys, pl.ds(width + lanes, 128)]
                v2 = qkv[:keys, pl.ds(2 * width + lanes, 128)]
                o2 = att_grad[:queries, pl.ds(lanes, 128)]
                q2 = jnp.where(query_seen, q2, jnp.zeros_like(q2))
                o2 = jnp.where(query_seen, o2, jnp.zeros_like(o2))
                k2 = jnp.where(key_seen, k2, jnp.zeros_like(k2))
                v2 = jnp.where(key_seen, v2, jnp.zeros_like(v2))
                k2t = turned(k2)
                dq_parts = []
                dk = dv = None
                for half in range(2):
                    head = 2 * p + half
                    mine = left if half == 0 else jnp.logical_not(left)
                    qh = jnp.where(mine, q2, jnp.zeros_like(q2))
                    oh = jnp.where(mine, o2, jnp.zeros_like(o2))
                    scores = dot_bt(k2, qh) - slopes[head] * gaps[:keys, :queries]
                    probs = jnp.exp(scores - totals[0, p, half : half + 1, :queries])
                    prob_g = dot_bt(v2, oh)
                    inner = jnp.sum(probs * prob_g, axis=0, keepdims=True)
                    score_g = (probs * (prob_g - inner)).astype(BF16)
                    dv_part = dot(probs.astype(BF16), oh)
                    dk_part = dot(score_g, qh)
                    dq_parts.append(
                        (dot(k2t[half * 64 : half * 64 + 64], score_g) * 0.125).astype(BF16)
                    )
                    dk = dk_part if dk is None else dk + dk_part
                    dv = dv_part if dv is None else dv + dv_part
                dq = turned_back(jnp.concatenate(dq_parts, axis=0))
                grads[slot, :queries, pl.ds(lanes, 128)] = dq
                grads[slot, :keys, pl.ds(width + lanes, 128)] = dk.astype(BF16)
                grads[slot, :keys, pl.ds(2 * width + lanes, 128)] = dv.astype(BF16)
                return carry

            lax.fori_loop(0, HEADS // 2, pair, 0, unroll=HEADS // 2)

        by_count(count, run)

        @pl.when(step > 0)
        def _():
            copy(step - 1).wait()

        copy(step).start()

        @pl.when(jnp.logical_or(step == pl.num_programs(0) - 1, spot == meta[N_LIVE] - 1))
        def _():
            copy(step).wait()


def qkv_grad_kernel(meta, packed_grad, tokens, vecs, keep_g, send_g, bias_g, acc, stage, sem):
    tile = pl.program_id(0)
    width = tokens.shape[1]

    @pl.when(tile == 0)
    def _():
        acc[...] = jnp.zeros_like(acc)
        bias_g[...] = jnp.zeros_like(bias_g)

    @pl.when(tile < meta[N_BWD])
    def _():
        ids = row_ids(tile * TILE, TILE)
        unit, _ = layer_norm(tokens[...].astype(F32))
        hidden = (
            unit * vecs[GAIN_ONE : GAIN_ONE + 1] + vecs[SHIFT_ONE : SHIFT_ONE + 1]
        ).astype(BF16)
        hidden_t = turned(hidden)
        for part in range(3):
            cols = slice(part * width, (part + 1) * width)
            block = packed_grad[:, cols]
            block = jnp.where(ids < meta[ROWS_BWD], block, jnp.zeros_like(block))
            acc[:, cols] += dot(hidden_t, block)
            bias_g[0:1, cols] += jnp.sum(block.astype(F32), axis=0, keepdims=True)

    @pl.when(tile == pl.num_programs(0) - 1)
    def _():
        rows = width // BLOCKS // 2
        for block in range(BLOCKS):
            for h in range(2):
                for c in range(3):
                    first = (2 * block + h) * rows
                    piece = acc[first : first + rows, c * width : (c + 1) * width]
                    stage[h, block, c * rows : (c + 1) * rows, :] = piece.astype(BF16)
        mine = meta[CORE]
        keep = pltpu.make_async_copy(stage.at[mine], keep_g, sem.at[0])
        send = pltpu.make_async_copy(stage.at[1 - mine], send_g, sem.at[1])
        keep.start()
        send.start()
        keep.wait()
        send.wait()


def token_grad_kernel(meta, packed_grad, tokens, mid_grad, vecs, weight, out, vec_g, held):
    step = pl.program_id(0)
    tiles = held.shape[0] // TILE - WINDOW // TILE
    length, images = out.shape[1], out.shape[2]

    @pl.when(step == 0)
    def _():
        vec_g[...] = jnp.zeros_like(vec_g)

    @pl.when(jnp.logical_and(step < tiles, step < meta[N_BWD]))
    def _():
        rows = aligned(step * TILE, TILE)
        ids = row_ids(rows, TILE)
        unit, inverse = layer_norm(tokens[...].astype(F32))
        block = packed_grad[...]
        block = jnp.where(ids < meta[ROWS_BWD], block, jnp.zeros_like(block))
        g1 = dot_bt(block, weight[...])
        back = norm_back(g1, vecs[GAIN_ONE : GAIN_ONE + 1], unit, inverse)
        held[pl.ds(rows, TILE), :] = mid_grad[...] + back
        vec_g[0:1, :] += jnp.sum(g1 * unit, axis=0, keepdims=True)
        vec_g[1:2, :] += jnp.sum(g1, axis=0, keepdims=True)

    @pl.when(step >= tiles)
    def _():
        parts = []
        for i in range(images):
            spot = meta[SPOT + (step - tiles) * images + i]
            off = aligned(meta[OFF + spot])
            limit = meta[CNT + spot] * meta[LIVE + spot]
            block = held[pl.ds(off, length), :]
            parts.append(jnp.where(row_ids(0, length) < limit, block, 0.0))
        out[0] = jnp.swapaxes(jnp.stack(parts, axis=0), 0, 1)


def whole(*shape):
    return pl.BlockSpec(shape, lambda *_: (0,) * len(shape), pipeline_mode=pl.Buffered(1))


def params():
    return pltpu.CompilerParams(vmem_limit_bytes=VMEM_LIMIT)


def small():
    return pl.BlockSpec(memory_space=pltpu.SMEM)


def prepare(every, counts, present, slots, me, cotangent, *vectors):
    steps, length, images, width = cotangent.shape
    group = every.shape[0]
    padded = (length + 7) // 8 * 8
    return pl.pallas_call(
        prepare_kernel,
        out_shape=(
            jax.ShapeDtypeStruct((PLACES,), jnp.int32),
            jax.ShapeDtypeStruct((steps * images,), jnp.int32),
            jax.ShapeDtypeStruct((16, width), F32),
            jax.ShapeDtypeStruct((group, steps, padded, width), BF16),
        ),
        grid=(steps,),
        in_specs=[small()] * 5
        + [pl.BlockSpec((1, length, images, width), lambda m: (m, 0, 0, 0))]
        + [whole(*vector.shape) for vector in vectors],
        out_specs=[
            small(),
            small(),
            whole(16, width),
            pl.BlockSpec((group, 1, padded, width), lambda m: (0, m, 0, 0)),
        ],
        compiler_params=params(),
    )(every, counts, present, slots, me, cotangent, *vectors)


def place(take, got, length):
    group, steps, padded, width = got.shape
    return pl.pallas_call(
        place_kernel,
        out_shape=jax.ShapeDtypeStruct((steps, length, group, width), BF16),
        grid=(steps,),
        in_specs=[small(), pl.BlockSpec((group, 1, padded, width), lambda m: (0, m, 0, 0))],
        out_specs=pl.BlockSpec((1, length, group, width), lambda m: (m, 0, 0, 0)),
        compiler_params=params(),
    )(take, got)


def first_half(meta, slopes, tokens, rows, cols, vecs, weight):
    steps, length, per, width = tokens.shape
    images = steps * per
    tiles = -(-images * ((length + 15) // 16 * 16) // TILE)
    total = tiles * TILE + WINDOW
    spots = pl.BlockSpec(
        (1, per, length),
        lambda s, meta, slopes: (meta[IMG + jnp.maximum(s - steps, 0)] // per, 0, 0),
    )
    return pl.pallas_call(
        attend_kernel,
        out_shape=(
            jax.ShapeDtypeStruct((total, width), BF16),
            jax.ShapeDtypeStruct((total, 3 * width), BF16),
            jax.ShapeDtypeStruct((total, width), BF16),
            jax.ShapeDtypeStruct((images, HEADS // 2, 8, WINDOW), F32),
        ),
        grid_spec=pltpu.PrefetchScalarGridSpec(
            num_scalar_prefetch=2,
            grid=(steps + images,),
            in_specs=[
                pl.BlockSpec(
                    (1, length, per, width),
                    lambda s, meta, slopes: (jnp.minimum(s, steps - 1), 0, 0, 0),
                ),
                spots,
                spots,
                whole(*vecs.shape),
                whole(width, 3 * width),
            ],
            out_specs=[
                pl.BlockSpec(memory_space=pl.ANY),
                pl.BlockSpec(memory_space=pl.ANY),
                pl.BlockSpec(memory_space=pl.ANY),
                pl.BlockSpec(
                    (1, HEADS // 2, 8, WINDOW),
                    lambda s, meta, slopes: (jnp.maximum(s - steps, 0), 0, 0, 0),
                ),
            ],
            scratch_shapes=[
                pltpu.VMEM((total, width), BF16),
                pltpu.VMEM((total, 3 * width), BF16),
                pltpu.VMEM((total, width), BF16),
                pltpu.VMEM((WINDOW, WINDOW), F32),
                pltpu.SemaphoreType.DMA((tiles,)),
                pltpu.SemaphoreType.DMA((tiles,)),
                pltpu.SemaphoreType.DMA((tiles,)),
            ],
        ),
        compiler_params=params(),
        cost_estimate=cost(40),
    )(meta, slopes, tokens, rows, cols, vecs, weight)


def mlp(meta, cot, att, packed, vecs, out_w, up_w, down_w, length):
    group, steps, padded, width = cot.shape
    rows = packed.shape[0]
    tiles = (rows - WINDOW) // TILE
    hidden = up_w.shape[1]
    parcel = (2 * width + hidden // 2 + width // 2) // BLOCKS
    def fwd_tile(s, meta):
        return (jnp.clip(s - steps, 0, meta[N_FWD] - 1), 0)

    def bwd_tile(s, meta):
        return (jnp.clip(s - steps, 0, jnp.maximum(meta[N_BWD] - 1, 0)), 0)

    return pl.pallas_call(
        functools.partial(mlp_kernel, CHUNK, length),
        out_shape=(
            jax.ShapeDtypeStruct(cot.shape, BF16),
            jax.ShapeDtypeStruct((rows, width), F32),
            jax.ShapeDtypeStruct((rows, width), BF16),
            jax.ShapeDtypeStruct((BLOCKS, parcel, width), BF16),
            jax.ShapeDtypeStruct((BLOCKS, parcel, width), BF16),
            jax.ShapeDtypeStruct((8, width), F32),
            jax.ShapeDtypeStruct((8, hidden), F32),
        ),
        grid_spec=pltpu.PrefetchScalarGridSpec(
            num_scalar_prefetch=1,
            grid=(2 * steps + tiles,),
            in_specs=[
                pl.BlockSpec(
                    (group, 1, padded, width), lambda s, meta: (0, jnp.minimum(s, steps - 1), 0, 0)
                ),
                pl.BlockSpec((TILE, width), fwd_tile),
                pl.BlockSpec((TILE, width), fwd_tile),
                whole(*vecs.shape),
                whole(width, width),
                whole(width, hidden),
                whole(hidden, width),
            ],
            out_specs=[
                pl.BlockSpec(
                    (group, 1, padded, width),
                    lambda s, meta: (0, jnp.clip(s - steps - tiles, 0, steps - 1), 0, 0),
                ),
                pl.BlockSpec((TILE, width), bwd_tile),
                pl.BlockSpec((TILE, width), bwd_tile),
                pl.BlockSpec(memory_space=pl.ANY),
                pl.BlockSpec(memory_space=pl.ANY),
                whole(8, width),
                whole(8, hidden),
            ],
            scratch_shapes=[
                pltpu.VMEM((8, hidden), F32),
                pltpu.VMEM((rows, width), BF16),
                pltpu.VMEM((width, hidden), F32),
                pltpu.VMEM((width, hidden), F32),
                pltpu.VMEM((width, width), F32),
                pltpu.VMEM((TILE, width), BF16),
                pltpu.VMEM((width, TILE), BF16),
                pltpu.VMEM((width, TILE), BF16),
                pltpu.VMEM((TILE, width), F32),
                pltpu.VMEM((TILE, width), F32),
                pltpu.SemaphoreType.DMA((2, BLOCKS)),
            ],
        ),
        compiler_params=params(),
        cost_estimate=cost(110),
    )(meta, cot, att, packed, vecs, out_w, up_w, down_w)


def attend_back(first, count, expected, meta, slopes, qkv, att_grad, totals, rows_in, cols_in, earlier):
    total, wide = qkv.shape
    width = wide // 3
    per, length = rows_in.shape[1:]

    def spot_of(s, meta):
        return jnp.clip(first + s, 0, jnp.maximum(meta[N_LIVE] - 1, 0))

    def by_offset(s, meta, slopes):
        return (aligned(meta[OFF + spot_of(s, meta)]), 0)

    spots = pl.BlockSpec(
        (1, per, length),
        lambda s, meta, slopes: (meta[IMG + spot_of(s, meta)] // per, 0, 0),
    )
    anywhere = pl.BlockSpec(memory_space=pl.ANY)
    return pl.pallas_call(
        functools.partial(attend_back_kernel, first, per),
        out_shape=jax.ShapeDtypeStruct((total, wide), BF16),
        grid_spec=pltpu.PrefetchScalarGridSpec(
            num_scalar_prefetch=2,
            grid=(count,),
            in_specs=[
                pl.BlockSpec((pl.Element(WINDOW), pl.Element(wide)), by_offset),
                pl.BlockSpec((pl.Element(WINDOW), pl.Element(width)), by_offset),
                pl.BlockSpec(
                    (1, HEADS // 2, 8, WINDOW),
                    lambda s, meta, slopes: (spot_of(s, meta), 0, 0, 0),
                ),
                spots,
                spots,
            ]
            + [anywhere] * len(earlier),
            out_specs=anywhere,
            scratch_shapes=[
                pltpu.VMEM((2, WINDOW, wide), BF16),
                pltpu.VMEM((WINDOW, WINDOW), F32),
                pltpu.SemaphoreType.DMA((2,)),
            ],
        ),
        input_output_aliases={7: 0} if earlier else {},
        compiler_params=params(),
        cost_estimate=cost(expected),
    )(meta, slopes, qkv, att_grad, totals, rows_in, cols_in, *earlier)


def bwd_tile(s, meta):
    return (jnp.clip(s, 0, jnp.maximum(meta[N_BWD] - 1, 0)), 0)


def qkv_grad(meta, packed_grad, packed, vecs):
    rows, width = packed.shape
    parcel = 3 * width // 2 // BLOCKS
    tiles = (rows - WINDOW) // TILE
    return pl.pallas_call(
        qkv_grad_kernel,
        out_shape=(
            jax.ShapeDtypeStruct((BLOCKS, parcel, width), BF16),
            jax.ShapeDtypeStruct((BLOCKS, parcel, width), BF16),
            jax.ShapeDtypeStruct((8, 3 * width), F32),
        ),
        grid_spec=pltpu.PrefetchScalarGridSpec(
            num_scalar_prefetch=1,
            grid=(tiles,),
            in_specs=[
                pl.BlockSpec((TILE, 3 * width), bwd_tile),
                pl.BlockSpec((TILE, width), bwd_tile),
                whole(*vecs.shape),
            ],
            out_specs=[
                pl.BlockSpec(memory_space=pl.ANY),
                pl.BlockSpec(memory_space=pl.ANY),
                whole(8, 3 * width),
            ],
            scratch_shapes=[
                pltpu.VMEM((width, 3 * width), F32),
                pltpu.VMEM((2, BLOCKS, parcel, width), BF16),
                pltpu.SemaphoreType.DMA((2,)),
            ],
        ),
        compiler_params=params(),
        cost_estimate=cost(15),
    )(meta, packed_grad, packed, vecs)


def token_grad(meta, packed_grad, packed, mid_grad, vecs, weight, steps, length, images):
    rows, width = packed.shape
    tiles = (rows - WINDOW) // TILE
    return pl.pallas_call(
        token_grad_kernel,
        out_shape=(
            jax.ShapeDtypeStruct((steps, length, images, width), F32),
            jax.ShapeDtypeStruct((8, width), F32),
        ),
        grid_spec=pltpu.PrefetchScalarGridSpec(
            num_scalar_prefetch=1,
            grid=(tiles + steps,),
            in_specs=[
                pl.BlockSpec((TILE, 3 * width), bwd_tile),
                pl.BlockSpec((TILE, width), bwd_tile),
                pl.BlockSpec((TILE, width), bwd_tile),
                whole(*vecs.shape),
                whole(width, 3 * width),
            ],
            out_specs=[
                pl.BlockSpec(
                    (1, length, images, width),
                    lambda s, meta: (jnp.clip(s - tiles, 0, steps - 1), 0, 0, 0),
                ),
                whole(8, width),
            ],
            scratch_shapes=[pltpu.VMEM((rows, width), F32)],
        ),
        compiler_params=params(),
        cost_estimate=cost(20),
    )(meta, packed_grad, packed, mid_grad, vecs, weight)


def cost(microseconds):
    return pl.CostEstimate(
        flops=int(microseconds * 1e9), bytes_accessed=int(microseconds * 1e5), transcendentals=0
    )


def swap(block, axis, bit):
    size = lax.axis_size(axis)
    return lax.ppermute(block, axis, [(n, n ^ bit) for n in range(size)])


def bit_of(axis, bit):
    return lax.axis_index(axis) // bit % 2


def added(a, b):
    return (a.astype(F32) + b.astype(F32)).astype(BF16)


def unpacked(mine, other, shapes):
    swapped = bit_of("bal", 1) == 1
    first = jnp.where(swapped, other, mine)
    second = jnp.where(swapped, mine, other)
    lead, width = mine.shape[:-2], mine.shape[-1]
    out, at = [], 0
    for rows, columns, kind in shapes:
        wide = columns // width
        part = rows * wide // 2
        held = [half[..., at : at + part, :] for half in (first, second)]
        if kind == "rows":
            size = rows // 2
            parts = [
                jnp.concatenate(
                    [half[..., c * size : (c + 1) * size, :] for c in range(wide)], axis=-1
                )
                for half in held
            ]
            out.append(jnp.concatenate(parts, axis=-2))
        elif kind == "columns":
            parts = [
                half[..., c * rows : (c + 1) * rows, :] for half in held for c in range(wide // 2)
            ]
            out.append(jnp.concatenate(parts, axis=-1))
        else:
            size = width // 2
            tops = [half[..., :size] for half in held]
            bottoms = [half[..., size:] for half in held]
            out.append(
                jnp.concatenate(
                    [jnp.concatenate(tops, axis=-1), jnp.concatenate(bottoms, axis=-1)], axis=-2
                )
            )
        at += part
    return [matrix.reshape(lead[:-1] + (-1, matrix.shape[-1])) if lead else matrix for matrix in out]


def spread_sum(keep, send, shapes):
    return [
        lax.psum(lax.psum_scatter(matrix, "dp", scatter_dimension=0, tiled=True), "bal").astype(F32)
        for matrix in unpacked(keep, send, shapes)
    ]


def start_fold(block, bit):
    block = block.reshape((-1, 2) + block.shape[-2:])
    mine = bit_of("dp", bit)
    keep = lax.dynamic_index_in_dim(block, mine, 1, keepdims=False)
    send = lax.dynamic_index_in_dim(block, 1 - mine, 1, keepdims=False)
    return keep, swap(send, "dp", bit)


def fold(block, bit):
    return added(*start_fold(block, bit))


def after(value, *others):
    return lax.optimization_barrier((value,) + others)[0]


def doubled(block, round_no):
    bits = []
    for axis in ("bal", "dp"):
        bit = 1
        while bit < lax.axis_size(axis):
            bits.append((axis, bit))
            bit *= 2
    if round_no is None:
        return len(bits)
    axis, bit = bits[round_no]
    return block + swap(block, axis, bit)


def per_device(
    tokens,
    cotangent,
    counts,
    rows,
    cols,
    present,
    slots,
    first_gain,
    first_shift,
    qkv_weight,
    query_bias,
    value_bias,
    out_weight,
    out_bias,
    second_gain,
    second_shift,
    up_weight,
    up_bias,
    down_weight,
    down_bias,
):
    steps, images, length, width = tokens.shape
    hidden = up_weight.shape[1]
    group = lax.axis_size("bal")
    total = steps * images
    slopes = jnp.exp2(-8.0 * (jnp.arange(16, dtype=F32) + 1.0) / HEADS)

    def exchange(blocks):
        flat = blocks.reshape(group, -1, width)
        return lax.all_to_all(flat, "bal", split_axis=0, concat_axis=0, tiled=True)

    def turn(array):
        return jnp.transpose(array, (0, 2, 1, 3))

    meta, take, vecs, cot_send = prepare(
        lax.all_gather(slots, "bal"), counts, present, slots,
        lax.axis_index("bal").astype(jnp.int32).reshape(1), turn(cotangent),
        first_gain, first_shift, query_bias, value_bias, out_bias, second_gain, second_shift,
        down_bias, up_bias,
    )
    cot_home = exchange(cot_send).reshape(group, steps, -1, width)
    packed, qkv, att, totals = first_half(meta, slopes, turn(tokens), rows, cols, vecs, qkv_weight)
    y_send, mid_grad, att_grad, keep_two, send_two, vec_two, upb_g = mlp(
        meta, cot_home, att, packed, vecs, out_weight, up_weight, down_weight, length
    )
    y_got = exchange(y_send)

    share, long = width // BLOCKS, hidden // BLOCKS
    shapes_two = ((share, hidden, "columns"), (long, width, "side"), (share, width, "rows"))
    shapes_one = ((share, 3 * width, "rows"),)
    direct = lax.axis_size("dp") == BLOCKS

    def back(first, count, expected, table, earlier):
        return attend_back(
            first, count, expected, table, slopes, qkv, att_grad, totals, rows, cols, earlier
        )

    lead = max(images // 2, 1)
    packed_grad = back(0, lead, 15, meta, ())
    table = meta
    if direct:
        sum_two = added(after(keep_two, packed_grad), swap(send_two, "bal", 1))
        share_two = lax.psum_scatter(sum_two, "dp", scatter_dimension=0, tiled=True)[0]
        table = after(meta, sum_two)
    packed_grad = back(lead, total - lead, 500, table, (packed_grad,))
    keep_one, send_one, bias_g = qkv_grad(after(table, y_got), packed_grad, packed, vecs)
    output = place(after(take, keep_one), y_got.reshape(group, steps, -1, width), length)
    table = after(table, output)
    if direct:
        sum_one = added(keep_one, swap(send_one, "bal", 1))
        table = after(table, sum_one)
    input_grad, vec_one = token_grad(
        table, packed_grad, packed, mid_grad, vecs, qkv_weight, steps, length, images
    )
    vectors = jnp.concatenate(
        [
            vec_one[:2].reshape(-1), bias_g[0, :width], bias_g[0, 2 * width :],
            vec_two[:4].reshape(-1), upb_g[0],
        ]
    )
    rounds = doubled(vectors, None)
    if direct:
        half_one = fold(sum_one, 1)
        keep, crossing = start_fold(half_one, 2)
        across = swap(share_two, "bal", 2)
        for n in range(3):
            vectors = doubled(vectors, n)
        block = added(after(keep, vectors), crossing)
        keep, crossing = start_fold(block, 4)
        vectors = after(vectors, block)
        for n in range(3, rounds):
            vectors = doubled(vectors, n)
        full_two = added(after(share_two, vectors), across)
        other_two = swap(full_two, "bal", 1)
        up_rows, down_rows, out_rows = [
            matrix.astype(F32) for matrix in unpacked(full_two, other_two, shapes_two)
        ]
        block = added(after(keep, full_two), crossing).reshape(sum_one.shape[-2:])
        full_one = added(block, swap(block, "bal", 2))
        (qkv_rows,) = [
            matrix.astype(F32)
            for matrix in unpacked(full_one, swap(full_one, "bal", 1), shapes_one)
        ]
    else:
        (qkv_rows,) = spread_sum(keep_one, send_one, shapes_one)
        up_rows, down_rows, out_rows = spread_sum(keep_two, send_two, shapes_two)
        for n in range(rounds):
            vectors = doubled(vectors, n)

    def vector(n):
        return vectors[n * width : (n + 1) * width]

    return (
        turn(output),
        turn(input_grad),
        vector(0),
        vector(1),
        qkv_rows,
        vector(2),
        vector(3),
        out_rows,
        vector(6),
        vector(4),
        vector(5),
        up_rows,
        vectors[8 * width :],
        down_rows,
        vector(7),
    )


def solution(mesh):
    images = P(None, ("dp", "bal"), None, None)
    spots = P(None, ("dp", "bal"), None)
    flags = P(None, ("dp", "bal"))
    matrix = P("dp", None)
    return jax.shard_map(
        per_device,
        mesh=mesh,
        in_specs=(images, images, flags, spots, spots, flags, flags) + (P(),) * 13,
        out_specs=(
            images, images, P(), P(), matrix, P(), P(), matrix, P(), P(), P(), matrix, P(), matrix, P(),
        ),
        check_vma=False,
    )
```

profile of v0, /device:TPU:0, one launch (start us, length us, event | category | flops | bytes accessed | tf_op | source)
XLA Modules:
  0.0 457.9 jit_solution(9092250576873938719)
XLA Ops:
  7.2 8.0 %all-gather.1.every = s32[4,4,4]{2,1,0:T(4,128)} all-gather(s32[1,4,4]{2,1,0:T(4,128)} %bitcast.39), channel_id=2, replica_groups=mesh['dp'=8,'bal'=4] {'bal'}, dimensions={0}, use_global_device_ids=true | all-gather | bytes 320 | tf_op jit(solution)/shard_map/all_gather | solution.py:1045
  15.2 9.9 %shard_map.307 = (s32[128]{0:T(128)}, s32[16]{0:T(128)}, f32[16,768]{1,0:T(8,128)}, bf16[4,4,232,768]{3,2,1,0:T(8,128)(2,1)}) custom-call(s32[4,4,4]{2,1,0:T(4,128)} %all-gather.1.every, s32[4,4]{1,0:T(4,128)} %counts.1, s32[4,4]{1,0:T(4,128)} %present.1, s32[4,4]{1,0:T(4,128)} %slots.1, s32[1]{0:T(128)} %bitcast.1.me, bf16[4,225,4,768]{3,2,1,0:T(4,128)(2,1)} %bitcast.34, ...), custom_call_target="tpu_custom_call" | custom-call | tf_op jit(solution)/shard_map/pallas_call | solution.py:643
  25.0 5.1 %all-to-all-start = ((bf16[4,928,768]{2,1,0:T(8,128)(2,1)}), bf16[4,928,768]{2,1,0:T(8,128)(2,1)}, u32[]{:S(2)}, u32[]{:S(2)}) async-start(bf16[4,928,768]{2,1,0:T(8,128)(2,1)} %bitcast.32), calls=%async_computation | async-start | bytes 11403264 | tf_op jit(solution)/shard_map/all_to_all | solution.py:1039
  30.1 0.5 multiply_exponential_fusion.slopes
  30.7 83.2 %shard_map.308 = (bf16[4096,768]{1,0:T(8,128)(2,1)}, bf16[4096,2304]{1,0:T(8,128)(2,1)}, bf16[4096,768]{1,0:T(8,128)(2,1)}, f32[16,6,8,256]{3,2,1,0:T(8,128)}) custom-call(s32[128]{0:T(128)} %get-tuple-element.64.meta, f32[16]{0:T(128)} %multiply_exponential_fusion.slopes, bf16[4,225,4,768]{3,2,1,0:T(4,128)(2,1)} %bitcast.40, s32[4,4,225]{2,1,0:T(4,128)} %rows_in.5, ...), custom_call_target="tpu_custom_call" | custom-call | flops 40000000000 | bytes 4000000 | tf_op jit(solution)/shard_map/pallas_call | solution.py:686
  113.9 115.9 %shard_map.309 = (bf16[4,4,232,768]{3,2,1,0:T(8,128)(2,1)}, f32[4096,768]{1,0:T(8,128)}, bf16[4096,768]{1,0:T(8,128)(2,1)}, bf16[8,432,768]{2,1,0:T(8,128)(2,1)}...) custom-call(s32[128]{0:T(128)} %get-tuple-element.64.meta, ...), custom_call_target="tpu_custom_call" | custom-call | flops 109999996928 | bytes 11000000 | tf_op jit(solution)/shard_map/pallas_call | solution.py:743
  229.8 9.4 %all-to-all-start.1 = ((bf16[4,928,768]{2,1,0:T(8,128)(2,1)}), bf16[4,928,768]{2,1,0:T(8,128)(2,1)}, u32[]{:S(2)}, u32[]{:S(2)}) async-start(bf16[4,928,768]{2,1,0:T(8,128)(2,1)} %bitcast.31), calls=%async_computation.1 | async-start | bytes 11403264 | tf_op jit(solution)/shard_map/all_to_all | solution.py:1039
  239.3 12.2 %shard_map.310.rest_0_ = bf16[4096,2304]{1,0:T(8,128)(2,1)} custom-call(s32[128]{0:T(128)} %get-tuple-element.64.meta, f32[16]{0:T(128)} %multiply_exponential_fusion.slopes, bf16[4096,2304]{1,0:T(8,128)(2,1)} %get-tuple-element.52.qkv, bf16[4096,768]{1,0:T(8,128)(2,1)} %get-tuple-element.53.att_grad, f32[16,6,8,256]{3,2,1,0:T(8,128)} %get-tuple-element.54.totals, ...), custom_call_target="tpu_custom_call" | custom-call | flops 15000000512 | bytes 1500000 | tf_op jit(solution)/shard_map/pallas_call | solution.py:815
  251.5 7.8 %add_convert_fusion = bf16[8,432,768]{2,1,0:T(8,128)(2,1)} fusion(bf16[8,432,768]{2,1,0:T(8,128)(2,1)} %collective-permute-done, bf16[8,432,768]{2,1,0:T(8,128)(2,1)} %get-tuple-element.55), kind=kLoop, calls=%fused_computation | loop fusion | flops 10616832 | bytes 15925248 | tf_op jit(solution)/shard_map/convert_element_type | solution.py:933
  259.3 38.2 %shard_map.311.packed_grad = bf16[4096,2304]{1,0:T(8,128)(2,1)} custom-call(s32[128]{0:T(128)} %get-tuple-element.64.meta, f32[16]{0:T(128)} %multiply_exponential_fusion.slopes, bf16[4096,2304]{1,0:T(8,128)(2,1)} %get-tuple-element.52.qkv, bf16[4096,768]{1,0:T(8,128)(2,1)} %get-tuple-element.53.att_grad, ...), custom_call_target="tpu_custom_call", output_to_operand_aliasing={{}: (7, {})} | custom-call | flops 499999997952 | bytes 50000000 | tf_op jit(solution)/shard_map/pallas_call | solution.py:815
  297.4 8.3 %all-to-all-done.1 = bf16[4,928,768]{2,1,0:T(8,128)(2,1)} async-done(((bf16[4,928,768]{2,1,0:T(8,128)(2,1)}), bf16[4,928,768]{2,1,0:T(8,128)(2,1)}, u32[]{:S(2)}, u32[]{:S(2)}) %all-to-all-start.1) | async-done | bytes 5701664 | tf_op jit(solution)/shard_map/all_to_all | solution.py:1039
  305.7 17.2 %shard_map.312 = (bf16[8,144,768]{2,1,0:T(8,128)(2,1)}, bf16[8,144,768]{2,1,0:T(8,128)(2,1)}, f32[8,2304]{1,0:T(8,128)}) custom-call(s32[128]{0:T(128)} %get-tuple-element.64.meta, bf16[4096,2304]{1,0:T(8,128)(2,1)} %shard_map.311.packed_grad, bf16[4096,768]{1,0:T(8,128)(2,1)} %get-tuple-element.50.tokens_in.tokens, f32[16,768]{1,0:T(8,128)} %get-tuple-element.48.vecs), custom_call_target="tpu_custom_call" | custom-call | flops 15000000512 | bytes 1500000 | tf_op jit(solution)/shard_map/pallas_call | solution.py:853
  323.1 0.6 reshape.73
  323.7 0.9 slice.106
  324.6 7.5 %shard_map.313 = bf16[4,225,4,768]{3,2,1,0:T(4,128)(2,1)} custom-call(s32[16]{0:T(128)} %get-tuple-element.61.take, bf16[4,4,232,768]{3,2,1,0:T(8,128)(2,1)} %bitcast.7.got), custom_call_target="tpu_custom_call" | custom-call | tf_op jit(solution)/shard_map/pallas_call | solution.py:667
  332.1 1.4 slice_reduce_fusion
  333.5 1.9 add_convert_fusion.1
  335.5 31.1 %collective-permute-start.5 = (bf16[4,144,768]{2,1,0:T(8,128)(2,1)S(1)}, bf16[4,144,768]{2,1,0:T(8,128)(2,1)S(1)}, u32[]{:S(2)}, u32[]{:S(2)}) collective-permute-start(bf16[4,144,768]{2,1,0:T(8,128)(2,1)S(1)} %dynamic-slice_bitcast_fusion), channel_id=1, source_target_pairs={{0,4},{4,0},{8,12},{12,8},{16,20},{20,16},{24,28},{28,24},{1,5},{5... | collective-permute-start | bytes 2654216 | tf_op jit(solution)/shard_map/ppermute | solution.py:925
  366.5 20.0 %shard_map.314 = (f32[4,225,4,768]{3,2,1,0:T(4,128)}, f32[8,768]{1,0:T(8,128)}) custom-call(s32[128]{0:T(128)} %get-tuple-element.64.meta, bf16[4096,2304]{1,0:T(8,128)(2,1)} %shard_map.311.packed_grad, bf16[4096,768]{1,0:T(8,128)(2,1)} %get-tuple-element.50.tokens_in.tokens, f32[4096,768]{1,0:T(8,128)} %get-tuple-element.65.mid_grad, ...), custom_call_target="tpu_custom_call" | custom-call | flops 20000000000 | bytes 2000000 | tf_op jit(solution)/shard_map/pallas_call | solution.py:887
  386.5 1.3 slice.102
  387.8 1.3 reshape.72
  389.1 1.3 constant_dynamic-update-slice_fusion.4
  390.5 1.3 constant_dynamic-update-slice_fusion.3
  391.8 0.2 fusion
  392.1 1.3 constant_dynamic-update-slice_fusion.2
  393.5 0.6 constant_dynamic-update-slice_fusion.1
  394.1 0.6 constant_dynamic-update-slice_fusion
  394.8 1.3 collective-permute-done.2
  396.1 0.8 add.90
  396.9 2.0 collective-permute-start.3
  398.9 12.5 %collective-permute-done.3 = f32[9216]{0:T(1024)S(1)} collective-permute-done((f32[9216]{0:T(1024)S(1)}, f32[9216]{0:T(1024)S(1)}, u32[]{:S(2)}, u32[]{:S(2)}) %collective-permute-start.3) | collective-permute-done | bytes 36896 | tf_op jit(solution)/shard_map/ppermute | solution.py:925
  411.4 3.9 collective-permute-done.4
  415.5 1.8 collective-permute-start.7
  417.3 2.2 collective-permute-done.7
  419.5 7.9 %collective-permute-start.8 = (f32[9216]{0:T(1024)S(1)}, f32[9216]{0:T(1024)S(1)}, u32[]{:S(2)}, u32[]{:S(2)}) collective-permute-start(f32[9216]{0:T(1024)S(1)} %add.101), channel_id=1, source_target_pairs={{0,16},{4,20},{8,24},{12,28},{16,0},{20,4},{24,8},{28,12},{1,17},{... | collective-permute-start | bytes 110600 | tf_op jit(solution)/shard_map/ppermute | solution.py:925
  427.5 3.9 collective-permute-done.8
  431.6 6.4 %collective-permute-done.10 = bf16[1,144,768]{2,1,0:T(8,128)(2,1)S(1)} collective-permute-done((bf16[1,144,768]{2,1,0:T(8,128)(2,1)S(1)}, bf16[1,144,768]{2,1,0:T(8,128)(2,1)S(1)}, u32[]{:S(2)}, u32[]{:S(2)}) %collective-permute-start.10) | collective-permute-done | bytes 221216 | tf_op jit(solution)/shard_map/ppermute | solution.py:925
  438.0 0.7 collective-permute-start.11
  438.8 0.6 slice.151
  439.4 5.2 %collective-permute-done.11 = bf16[144,768]{1,0:T(8,128)(2,1)S(1)} collective-permute-done((bf16[144,768]{1,0:T(8,128)(2,1)S(1)}, bf16[144,768]{1,0:T(8,128)(2,1)S(1)}, u32[]{:S(2)}, u32[]{:S(2)}) %collective-permute-start.11) | collective-permute-done | bytes 221216 | tf_op jit(solution)/shard_map/ppermute | solution.py:925
  444.7 0.6 fusion.8
  445.3 0.5 collective-permute-start.13
  445.8 0.3 collective-permute-done.12
  446.2 1.0 maximum_convert_fusion.2
  447.2 0.3 collective-permute-done.13
  447.9 0.7 maximum_convert_fusion.3
  448.6 1.1 maximum_convert_fusion.1
  449.7 1.1 maximum_convert_fusion
  (45 shorter events, 1.5 us)
Async XLA Ops:
  25.0 88.9 %all-to-all-start = ((bf16[4,928,768]{2,1,0:T(8,128)(2,1)}), bf16[4,928,768]{2,1,0:T(8,128)(2,1)}, u32[]{:S(2)}, u32[]{:S(2)}) async-start(bf16[4,928,768]{2,1,0:T(8,128)(2,1)} %bitcast.32), calls=%async_computation | async-start | bytes 11403264 | tf_op jit(solution)/shard_map/all_to_all | solution.py:1039
  229.8 21.7 %collective-permute-start = (bf16[8,432,768]{2,1,0:T(8,128)(2,1)}, bf16[8,432,768]{2,1,0:T(8,128)(2,1)}, u32[]{:S(2)}, u32[]{:S(2)}) collective-permute-start(bf16[8,432,768]{2,1,0:T(8,128)(2,1)} %get-tuple-element.56), channel_id=1, source_target_pairs={{0,1},{1,0},{2,3},{3,2},{4,5},{5,4},{6,7},{7,6},{8,9},{9,8},{10,11... | collective-permute-start | bytes 15925256 | tf_op jit(solution)/shard_map/ppermute | solution.py:925
  229.8 75.9 %all-to-all-start.1 = ((bf16[4,928,768]{2,1,0:T(8,128)(2,1)}), bf16[4,928,768]{2,1,0:T(8,128)(2,1)}, u32[]{:S(2)}, u32[]{:S(2)}) async-start(bf16[4,928,768]{2,1,0:T(8,128)(2,1)} %bitcast.31), calls=%async_computation.1 | async-start | bytes 11403264 | tf_op jit(solution)/shard_map/all_to_all | solution.py:1039
  239.3 154.2 %reduce-scatter.2.cloned.1.call-start = ((), (), s32[]{:S(2)}) async-start(), calls=%async_computation.3 | async-start | bytes 5971968 | tf_op jit(solution)/shard_map/reduce_scatter | solution.py:1072
  297.4 25.7 %copy-start.3 = (f32[8,768]{1,0:T(8,128)S(1)}, f32[8,768]{1,0:T(8,128)}, u32[]{:S(2)}) copy-start(f32[8,768]{1,0:T(8,128)} %get-tuple-element.69) | copy-start | bytes 73732
  322.9 10.5 %collective-permute-start.1 = (bf16[8,144,768]{2,1,0:T(8,128)(2,1)}, bf16[8,144,768]{2,1,0:T(8,128)(2,1)}, u32[]{:S(2)}, u32[]{:S(2)}) collective-permute-start(bf16[8,144,768]{2,1,0:T(8,128)(2,1)} %get-tuple-element.63), channel_id=1, source_target_pairs={{0,1},{1,0},{2,3},{3,2},{4,5},{5,4},{6,7},{7,6},{8,9},{9,8},{10,11... | collective-permute-start | bytes 5308424 | tf_op jit(solution)/shard_map/ppermute | solution.py:925
  324.6 8.8 %copy-start = (bf16[8,144,768]{2,1,0:T(8,128)(2,1)S(1)}, bf16[8,144,768]{2,1,0:T(8,128)(2,1)}, u32[]{:S(2)}) copy-start(bf16[8,144,768]{2,1,0:T(8,128)(2,1)} %get-tuple-element.60) | copy-start | bytes 5308420
  335.5 56.3 %collective-permute-start.5 = (bf16[4,144,768]{2,1,0:T(8,128)(2,1)S(1)}, bf16[4,144,768]{2,1,0:T(8,128)(2,1)S(1)}, u32[]{:S(2)}, u32[]{:S(2)}) collective-permute-start(bf16[4,144,768]{2,1,0:T(8,128)(2,1)S(1)} %dynamic-slice_bitcast_fusion), channel_id=1, source_target_pairs={{0,4},{4,0},{8,12},{12,8},{16,20},{20,16},{24,28},{28,24},{1,5},{5... | collective-permute-start | bytes 2654216 | tf_op jit(solution)/shard_map/ppermute | solution.py:925
  391.8 1.7 copy-start.2
  392.1 23.3 %collective-permute-start.6 = (bf16[2,144,768]{2,1,0:T(8,128)(2,1)S(1)}, bf16[2,144,768]{2,1,0:T(8,128)(2,1)S(1)}, u32[]{:S(2)}, u32[]{:S(2)}) collective-permute-start(bf16[2,144,768]{2,1,0:T(8,128)(2,1)S(1)} %get-tuple-element.80), channel_id=1, source_target_pairs={{0,8},{4,12},{8,0},{12,4},{16,24},{20,28},{24,16},{28,20},{1,9},{5... | collective-permute-start | bytes 1327112 | tf_op jit(solution)/shard_map/ppermute | solution.py:925
  393.4 38.0 %copy-start.1 = (bf16[1,432,768]{2,1,0:T(8,128)(2,1)S(1)}, bf16[1,432,768]{2,1,0:T(8,128)(2,1)}, u32[]{:S(2)}) copy-start(bf16[1,432,768]{2,1,0:T(8,128)(2,1)} %reduce-scatter.2.cloned.1.call-done) | copy-start | bytes 1990660
  393.4 37.9 %collective-permute-start.9 = (bf16[432,768]{1,0:T(8,128)(2,1)}, bf16[432,768]{1,0:T(8,128)(2,1)S(1)}, u32[]{:S(2)}, u32[]{:S(2)}) collective-permute-start(bf16[432,768]{1,0:T(8,128)(2,1)} %bitcast.36), channel_id=1, source_target_pairs={{0,2},{1,3},{2,0},{3,1},{4,6},{5,7},{6,4},{7,5},{8,10},{9,11},{10,... | collective-permute-start | bytes 1990664 | tf_op jit(solution)/shard_map/ppermute | solution.py:925
  394.7 1.4 collective-permute-start.2
  396.9 14.5 %collective-permute-start.3 = (f32[9216]{0:T(1024)S(1)}, f32[9216]{0:T(1024)S(1)}, u32[]{:S(2)}, u32[]{:S(2)}) collective-permute-start(f32[9216]{0:T(1024)S(1)} %add.90), channel_id=1, source_target_pairs={{0,2},{1,3},{2,0},{3,1},{4,6},{5,7},{6,4},{7,5},{8,10},{9,11},{10,... | collective-permute-start | bytes 110600 | tf_op jit(solution)/shard_map/ppermute | solution.py:925
  411.4 4.0 collective-permute-start.4
  415.5 4.0 collective-permute-start.7
  419.5 11.9 %collective-permute-start.8 = (f32[9216]{0:T(1024)S(1)}, f32[9216]{0:T(1024)S(1)}, u32[]{:S(2)}, u32[]{:S(2)}) collective-permute-start(f32[9216]{0:T(1024)S(1)} %add.101), channel_id=1, source_target_pairs={{0,16},{4,20},{8,24},{12,28},{16,0},{20,4},{24,8},{28,12},{1,17},{... | collective-permute-start | bytes 110600 | tf_op jit(solution)/shard_map/ppermute | solution.py:925
  427.4 10.5 %collective-permute-start.10 = (bf16[1,144,768]{2,1,0:T(8,128)(2,1)S(1)}, bf16[1,144,768]{2,1,0:T(8,128)(2,1)S(1)}, u32[]{:S(2)}, u32[]{:S(2)}) collective-permute-start(bf16[1,144,768]{2,1,0:T(8,128)(2,1)S(1)} %get-tuple-element.92), channel_id=1, source_target_pairs={{0,16},{4,20},{8,24},{12,28},{16,0},{20,4},{24,8},{28,12},{1,17},{... | collective-permute-start | bytes 663560 | tf_op jit(solution)/shard_map/ppermute | solution.py:925
  438.0 6.5 %collective-permute-start.11 = (bf16[144,768]{1,0:T(8,128)(2,1)S(1)}, bf16[144,768]{1,0:T(8,128)(2,1)S(1)}, u32[]{:S(2)}, u32[]{:S(2)}) collective-permute-start(bf16[144,768]{1,0:T(8,128)(2,1)S(1)} %fusion.1), channel_id=1, source_target_pairs={{0,2},{1,3},{2,0},{3,1},{4,6},{5,7},{6,4},{7,5},{8,10},{9,11},{10,... | collective-permute-start | bytes 663560 | tf_op jit(solution)/shard_map/ppermute | solution.py:925
  444.6 1.5 collective-permute-start.12
  445.3 2.2 collective-permute-start.13
Sparse Core Ops, SparseCore 0:
  259.4 124.5 reduce-scatter.1
where the time goes:
time: 461 us; the launch traced here: 458 us
  Pallas kernels  304 us (66%)
  starting transfers between devices  59 us (13%)
  waiting for transfers between devices  44.4 us (10%)
  other arithmetic  15.7 us (3%)
  between operations  14.6 us (3%)
  local copies, waits for them, and re-layouts  12.2 us (3%)
  blocking collectives  7.98 us (2%)
    pallas_call x1, Pallas kernels, mlp(): pl.pallas_call(functools.partial(mlp_kernel, CHUNK, length), out_shape=(j...  116 us
    pallas_call x1, Pallas kernels, first_half(): pl.pallas_call(attend_kernel, out_shape=(jax.ShapeDtypeStruct((total, wid...  83.2 us
    pallas_call x2, Pallas kernels, attend_back(): pl.pallas_call(functools.partial(attend_back_kernel, first, per), out_sha...  50.4 us
    ppermute x14, starting transfers between devices, swap(): return lax.ppermute(block, axis, [(n, n ^ bit) for n in range(size)])  44.5 us
    ppermute x14, waiting for transfers between devices, swap(): return lax.ppermute(block, axis, [(n, n ^ bit) for n in range(size)])  36.1 us
    pallas_call x1, Pallas kernels, token_grad(): pl.pallas_call(token_grad_kernel, out_shape=(jax.ShapeDtypeStruct((steps,...  20 us
    pallas_call x1, Pallas kernels, qkv_grad(): pl.pallas_call(qkv_grad_kernel, out_shape=(jax.ShapeDtypeStruct((BLOCKS,...  17.2 us
    all_to_all x2, starting transfers between devices, exchange(): return lax.all_to_all(flat, 'bal', split_axis=0, concat_axis=0, tiled=True)  14.6 us
  transfers between devices with their start and end apart: 17, of which 10 were waited for; matrix products, arithmetic and copies ran while one was open for 5% of the time, Pallas kernels for 39%

commit v1 on v0

--- a/solution.py
+++ b/solution.py
@@ -37,15 +37,7 @@
 
 
 def turned(block):
-    size = 256 if block.shape[1] % 256 == 0 else 128
-    row = lax.broadcasted_iota(jnp.int32, (size, size), 0)
-    col = lax.broadcasted_iota(jnp.int32, (size, size), 1)
-    eye = jnp.where(row == col, 1.0, 0.0).astype(BF16)
-    parts = [
-        dot_bt(eye, block[:, start : start + size]).astype(BF16)
-        for start in range(0, block.shape[1], size)
-    ]
-    return parts[0] if len(parts) == 1 else jnp.concatenate(parts, axis=0)
+    return block.astype(F32).T.astype(BF16)
 
 
 def layer_norm(values):
@@ -266,7 +258,7 @@
             gaps[:keys, :queries] = distances(rows_in[0], cols_in[0], which, count, keys, queries)
             key_seen = row_ids(0, keys) < count
             query_seen = row_ids(0, queries) < count
-            left = lax.broadcasted_iota(jnp.int32, (queries, 128), 1) < 64
+            left = lax.broadcasted_iota(jnp.int32, (keys, 128), 1) < 64
 
             def pair(p, carry):
                 lanes = aligned(p * 128, 128)
@@ -276,21 +268,21 @@
                 q2 = jnp.where(query_seen, q2, jnp.zeros_like(q2))
                 k2 = jnp.where(key_seen, k2, jnp.zeros_like(k2))
                 v2 = jnp.where(key_seen, v2, jnp.zeros_like(v2))
-                v2t = turned(v2)
+                v2t = v2.astype(F32).T.astype(BF16)
+                raw = dot_bt(by_head(k2, left), q2)
                 outs = []
                 for half in range(2):
                     head = 2 * p + half
-                    mine = left if half == 0 else jnp.logical_not(left)
-                    qh = jnp.where(mine, q2, jnp.zeros_like(q2))
-                    scores = dot_bt(k2, qh) - slopes[head] * gaps[:keys, :queries]
+                    scores = raw[half * keys : (half + 1) * keys]
+                    scores = scores - slopes[head] * gaps[:keys, :queries]
                     top = jnp.max(scores, axis=0, keepdims=True)
                     terms = jnp.exp(scores - top)
                     total = jnp.sum(terms, axis=0, keepdims=True)
                     heads_out = dot(v2t[half * 64 : half * 64 + 64], terms.astype(BF16))
-                    outs.append((heads_out * (1.0 / total)).astype(BF16))
+                    outs.append(heads_out * (1.0 / total))
                     total_out[0, p, half : half + 1, :queries] = top + jnp.log(total)
                 both = jnp.concatenate(outs, axis=0)
-                att[pl.ds(off, queries), pl.ds(lanes, 128)] = turned_back(both)
+                att[pl.ds(off, queries), pl.ds(lanes, 128)] = both.T.astype(BF16)
                 return carry
 
             lax.fori_loop(0, HEADS // 2, pair, 0, unroll=HEADS // 2)
@@ -315,15 +307,9 @@
         lax.fori_loop(0, meta[N_FWD], finish, 0)
 
 
-def turned_back(block):
-    size = block.shape[1]
-    parts = []
-    for start in range(0, size, 128):
-        row = lax.broadcasted_iota(jnp.int32, (128, size), 0)
-        col = lax.broadcasted_iota(jnp.int32, (128, size), 1)
-        eye = jnp.where(row + start == col, 1.0, 0.0).astype(BF16)
-        parts.append(dot_bt(eye, block).astype(BF16))
-    return parts[0] if len(parts) == 1 else jnp.concatenate(parts, axis=0)
+def by_head(block, left):
+    none = jnp.zeros_like(block)
+    return jnp.concatenate([jnp.where(left, block, none), jnp.where(left, none, block)], axis=0)
 
 
 def mlp_kernel(
@@ -495,7 +481,7 @@
             gaps[:keys, :queries] = distances(rows_in[0], cols_in[0], which, count, keys, queries)
             key_seen = row_ids(0, keys) < count
             query_seen = row_ids(0, queries) < count
-            left = lax.broadcasted_iota(jnp.int32, (queries, 128), 1) < 64
+            left = lax.broadcasted_iota(jnp.int32, (keys, 128), 1) < 64
 
             def pair(p, carry):
                 lanes = aligned(p * 128, 128)
@@ -507,27 +493,26 @@
                 o2 = jnp.where(query_seen, o2, jnp.zeros_like(o2))
                 k2 = jnp.where(key_seen, k2, jnp.zeros_like(k2))
                 v2 = jnp.where(key_seen, v2, jnp.zeros_like(v2))
-                k2t = turned(k2)
-                dq_parts = []
-                dk = dv = None
+                k2t = k2.astype(F32).T.astype(BF16)
+                raw = dot_bt(by_head(k2, left), q2)
+                raw_g = dot_bt(by_head(v2, left), o2)
+                dq_parts, probs_low, score_low = [], [], []
                 for half in range(2):
                     head = 2 * p + half
-                    mine = left if half == 0 else jnp.logical_not(left)
-                    qh = jnp.where(mine, q2, jnp.zeros_like(q2))
-                    oh = jnp.where(mine, o2, jnp.zeros_like(o2))
-                    scores = dot_bt(k2, qh) - slopes[head] * gaps[:keys, :queries]
+                    rows = slice(half * keys, (half + 1) * keys)
+                    scores = raw[rows] - slopes[head] * gaps[:keys, :queries]
                     probs = jnp.exp(scores - totals[0, p, half : half + 1, :queries])
-                    prob_g = dot_bt(v2, oh)
+                    prob_g = raw_g[rows]
                     inner = jnp.sum(probs * prob_g, axis=0, keepdims=True)
                     score_g = (probs * (prob_g - inner)).astype(BF16)
-                    dv_part = dot(probs.astype(BF16), oh)
-                    dk_part = dot(score_g, qh)
-                    dq_parts.append(
-                        (dot(k2t[half * 64 : half * 64 + 64], score_g) * 0.125).astype(BF16)
-                    )
-                    dk = dk_part if dk is None else dk + dk_part
-                    dv = dv_part if dv is None else dv + dv_part
-                dq = turned_back(jnp.concatenate(dq_parts, axis=0))
+                    dq_parts.append(dot(k2t[half * 64 : half * 64 + 64], score_g) * 0.125)
+                    probs_low.append(probs.astype(BF16))
+                    score_low.append(score_g)
+                dv = dot(jnp.concatenate(probs_low, axis=0), o2)
+                dk = dot(jnp.concatenate(score_low, axis=0), q2)
+                dv = jnp.where(left, dv[:keys], dv[keys:])
+                dk = jnp.where(left, dk[:keys], dk[keys:])
+                dq = jnp.concatenate(dq_parts, axis=0).T.astype(BF16)
                 grads[slot, :queries, pl.ds(lanes, 128)] = dq
                 grads[slot, :keys, pl.ds(width + lanes, 128)] = dk.astype(BF16)
                 grads[slot, :keys, pl.ds(2 * width + lanes, 128)] = dv.astype(BF16)
@@ -590,14 +575,22 @@
         send.wait()
 
 
-def token_grad_kernel(meta, packed_grad, tokens, mid_grad, vecs, weight, out, vec_g, held):
+def token_grad_kernel(
+    meta, packed_grad, tokens, mid_grad, vecs, weight, bias_g, vec_two, upb_g, out, vec_g, held
+):
     step = pl.program_id(0)
     tiles = held.shape[0] // TILE - WINDOW // TILE
     length, images = out.shape[1], out.shape[2]
 
     @pl.when(step == 0)
     def _():
+        width = vec_g.shape[1]
         vec_g[...] = jnp.zeros_like(vec_g)
+        vec_g[2:3, :] = bias_g[0:1, :width]
+        vec_g[3:4, :] = bias_g[0:1, 2 * width :]
+        vec_g[4:8, :] = vec_two[0:4, :]
+        for n in range(upb_g.shape[1] // width):
+            vec_g[8 + n : 9 + n, :] = upb_g[0:1, n * width : (n + 1) * width]
 
     @pl.when(jnp.logical_and(step < tiles, step < meta[N_BWD]))
     def _():
@@ -881,14 +874,16 @@
     )(meta, packed_grad, packed, vecs)
 
 
-def token_grad(meta, packed_grad, packed, mid_grad, vecs, weight, steps, length, images):
+def token_grad(
+    meta, packed_grad, packed, mid_grad, vecs, weight, bias_g, vec_two, upb_g, steps, length, images
+):
     rows, width = packed.shape
     tiles = (rows - WINDOW) // TILE
     return pl.pallas_call(
         token_grad_kernel,
         out_shape=(
             jax.ShapeDtypeStruct((steps, length, images, width), F32),
-            jax.ShapeDtypeStruct((8, width), F32),
+            jax.ShapeDtypeStruct((16, width), F32),
         ),
         grid_spec=pltpu.PrefetchScalarGridSpec(
             num_scalar_prefetch=1,
@@ -899,19 +894,22 @@
                 pl.BlockSpec((TILE, width), bwd_tile),
                 whole(*vecs.shape),
                 whole(width, 3 * width),
+                whole(*bias_g.shape),
+                whole(*vec_two.shape),
+                whole(*upb_g.shape),
             ],
             out_specs=[
                 pl.BlockSpec(
                     (1, length, images, width),
                     lambda s, meta: (jnp.clip(s - tiles, 0, steps - 1), 0, 0, 0),
                 ),
-                whole(8, width),
+                whole(16, width),
             ],
             scratch_shapes=[pltpu.VMEM((rows, width), F32)],
         ),
         compiler_params=params(),
         cost_estimate=cost(20),
-    )(meta, packed_grad, packed, mid_grad, vecs, weight)
+    )(meta, packed_grad, packed, mid_grad, vecs, weight, bias_g, vec_two, upb_g)
 
 
 def cost(microseconds):
@@ -985,21 +983,17 @@
     return keep, swap(send, "dp", bit)
 
 
-def fold(block, bit):
-    return added(*start_fold(block, bit))
-
-
 def after(value, *others):
     return lax.optimization_barrier((value,) + others)[0]
 
 
 def doubled(block, round_no):
-    bits = []
-    for axis in ("bal", "dp"):
-        bit = 1
-        while bit < lax.axis_size(axis):
-            bits.append((axis, bit))
-            bit *= 2
+    bits = [("bal", 1)]
+    bit = 1
+    while bit < lax.axis_size("dp"):
+        bits.append(("dp", bit))
+        bit *= 2
+    bits.append(("bal", 2))
     if round_no is None:
         return len(bits)
     axis, bit = bits[round_no]
@@ -1072,43 +1066,39 @@
         share_two = lax.psum_scatter(sum_two, "dp", scatter_dimension=0, tiled=True)[0]
         table = after(meta, sum_two)
     packed_grad = back(lead, total - lead, 500, table, (packed_grad,))
-    keep_one, send_one, bias_g = qkv_grad(after(table, y_got), packed_grad, packed, vecs)
+    keep_one, send_one, bias_g = qkv_grad(table, packed_grad, packed, vecs)
     output = place(after(take, keep_one), y_got.reshape(group, steps, -1, width), length)
     table = after(table, output)
     if direct:
         sum_one = added(keep_one, swap(send_one, "bal", 1))
+        keep_y, crossing_y = start_fold(sum_one, 1)
         table = after(table, sum_one)
-    input_grad, vec_one = token_grad(
-        table, packed_grad, packed, mid_grad, vecs, qkv_weight, steps, length, images
-    )
-    vectors = jnp.concatenate(
-        [
-            vec_one[:2].reshape(-1), bias_g[0, :width], bias_g[0, 2 * width :],
-            vec_two[:4].reshape(-1), upb_g[0],
-        ]
+    input_grad, vectors = token_grad(
+        table, packed_grad, packed, mid_grad, vecs, qkv_weight, bias_g, vec_two, upb_g,
+        steps, length, images,
     )
     rounds = doubled(vectors, None)
     if direct:
-        half_one = fold(sum_one, 1)
+        half_one = added(after(keep_y, vectors), crossing_y)
         keep, crossing = start_fold(half_one, 2)
-        across = swap(share_two, "bal", 2)
-        for n in range(3):
+        for n in range(rounds - 2):
             vectors = doubled(vectors, n)
         block = added(after(keep, vectors), crossing)
         keep, crossing = start_fold(block, 4)
-        vectors = after(vectors, block)
-        for n in range(3, rounds):
-            vectors = doubled(vectors, n)
-        full_two = added(after(share_two, vectors), across)
-        other_two = swap(full_two, "bal", 1)
-        up_rows, down_rows, out_rows = [
-            matrix.astype(F32) for matrix in unpacked(full_two, other_two, shapes_two)
-        ]
-        block = added(after(keep, full_two), crossing).reshape(sum_one.shape[-2:])
-        full_one = added(block, swap(block, "bal", 2))
+        vectors = doubled(after(vectors, block), rounds - 2)
+        block = added(after(keep, vectors), crossing).reshape(sum_one.shape[-2:])
+        across_one = swap(block, "bal", 2)
+        across_two = swap(after(share_two, block), "bal", 2)
+        vectors = doubled(after(vectors, block), rounds - 1)
+        full_one = added(after(block, vectors), across_one)
+        full_two = added(after(share_two, full_one), across_two)
         (qkv_rows,) = [
             matrix.astype(F32)
             for matrix in unpacked(full_one, swap(full_one, "bal", 1), shapes_one)
+        ]
+        up_rows, down_rows, out_rows = [
+            matrix.astype(F32)
+            for matrix in unpacked(full_two, swap(full_two, "bal", 1), shapes_two)
         ]
     else:
         (qkv_rows,) = spread_sum(keep_one, send_one, shapes_one)
@@ -1117,7 +1107,7 @@
             vectors = doubled(vectors, n)
 
     def vector(n):
-        return vectors[n * width : (n + 1) * width]
+        return vectors[n]
 
     return (
         turn(output),
@@ -1132,7 +1122,7 @@
         vector(4),
         vector(5),
         up_rows,
-        vectors[8 * width :],
+        vectors[8 : 8 + hidden // width].reshape(-1),
         down_rows,
         vector(7),
     )

time: 461 us -> 435 us (0.944)
  waiting for transfers between devices: 44.4 us -> 78.7 us
  Pallas kernels: 304 us -> 280 us
  starting transfers between devices: 59 us -> 37.1 us
  local copies, waits for them, and re-layouts: 12.2 us -> 1.69 us
    pallas_call x1, Pallas kernels: 83.2 us -> 53.1 us  [first_half(): pl.pallas_call(attend_kernel, out_shape=(jax.ShapeDtypeStruct((total, wid...]
    ppermute x14, waiting for transfers between devices: 36.1 us -> 64.7 us  [swap(): return lax.ppermute(block, axis, [(n, n ^ bit) for n in range(size)])]
    ppermute x14, starting transfers between devices: 44.5 us -> 26.8 us  [swap(): return lax.ppermute(block, axis, [(n, n ^ bit) for n in range(size)])]
    pallas_call x1, Pallas kernels: 116 us -> 125 us  [mlp(): pl.pallas_call(functools.partial(mlp_kernel, CHUNK, length), out_shape=(j...]
    pallas_call x2, Pallas kernels: 50.4 us -> 43.1 us  [attend_back(): pl.pallas_call(functools.partial(attend_back_kernel, first, per), out_sha...]
    all_to_all x2, waiting for transfers between devices: 8.29 us -> 14 us  [exchange(): return lax.all_to_all(flat, 'bal', split_axis=0, concat_axis=0, tiled=True)]
  transfers between devices with their start and end apart: 17 -> 17, of which waited for: 10 -> 9; matrix products, arithmetic and copies ran while one was open for 5% -> 3% of each run, Pallas kernels for 39% -> 33%
where the time goes in v1:
time: 435 us
  Pallas kernels  280 us (64%)
  waiting for transfers between devices  78.7 us (18%)
  starting transfers between devices  37.1 us (9%)
  between operations  14.6 us (3%)
  other arithmetic  14.4 us (3%)
  blocking collectives  7.95 us (2%)
    pallas_call x1, Pallas kernels, mlp(): pl.pallas_call(functools.partial(mlp_kernel, CHUNK, length), out_shape=(j...  125 us
    ppermute x14, waiting for transfers between devices, swap(): return lax.ppermute(block, axis, [(n, n ^ bit) for n in range(size)])  64.7 us
    pallas_call x1, Pallas kernels, first_half(): pl.pallas_call(attend_kernel, out_shape=(jax.ShapeDtypeStruct((total, wid...  53.1 us
    pallas_call x2, Pallas kernels, attend_back(): pl.pallas_call(functools.partial(attend_back_kernel, first, per), out_sha...  43.1 us
    ppermute x14, starting transfers between devices, swap(): return lax.ppermute(block, axis, [(n, n ^ bit) for n in range(size)])  26.8 us
    pallas_call x1, Pallas kernels, token_grad(): pl.pallas_call(token_grad_kernel, out_shape=(jax.ShapeDtypeStruct((steps,...  23.2 us
    pallas_call x1, Pallas kernels, qkv_grad(): pl.pallas_call(qkv_grad_kernel, out_shape=(jax.ShapeDtypeStruct((BLOCKS,...  19.1 us
    all_to_all x2, waiting for transfers between devices, exchange(): return lax.all_to_all(flat, 'bal', split_axis=0, concat_axis=0, tiled=True)  14 us
  transfers between devices with their start and end apart: 17, of which 9 were waited for; matrix products, arithmetic and copies ran while one was open for 3% of the time, Pallas kernels for 33%

profile of v1, /device:TPU:0, one launch (start us, length us, event | category | flops | bytes accessed | tf_op | source)
XLA Modules:
  0.0 434.9 jit_solution(14361336762965322439)
XLA Ops:
  7.2 8.0 %all-gather.1.every = s32[4,4,4]{2,1,0:T(4,128)} all-gather(s32[1,4,4]{2,1,0:T(4,128)} %bitcast.31), channel_id=2, replica_groups=mesh['dp'=8,'bal'=4] {'bal'}, dimensions={0}, use_global_device_ids=true | all-gather | bytes 320 | tf_op jit(solution)/shard_map/all_gather | solution.py:1039
  15.1 9.9 %shard_map.307 = (s32[128]{0:T(128)}, s32[16]{0:T(128)}, f32[16,768]{1,0:T(8,128)}, bf16[4,4,232,768]{3,2,1,0:T(8,128)(2,1)}) custom-call(s32[4,4,4]{2,1,0:T(4,128)} %all-gather.1.every, s32[4,4]{1,0:T(4,128)} %counts.1, s32[4,4]{1,0:T(4,128)} %present.1, s32[4,4]{1,0:T(4,128)} %slots.1, s32[1]{0:T(128)} %bitcast.1.me, bf16[4,225,4,768]{3,2,1,0:T(4,128)(2,1)} %bitcast.27, ...), custom_call_target="tpu_custom_call" | custom-call | tf_op jit(solution)/shard_map/pallas_call | solution.py:636
  25.0 5.1 %all-to-all-start = ((bf16[4,928,768]{2,1,0:T(8,128)(2,1)}), bf16[4,928,768]{2,1,0:T(8,128)(2,1)}, u32[]{:S(2)}, u32[]{:S(2)}) async-start(bf16[4,928,768]{2,1,0:T(8,128)(2,1)} %bitcast.25), calls=%async_computation | async-start | bytes 11403264 | tf_op jit(solution)/shard_map/all_to_all | solution.py:1033
  30.1 0.5 multiply_exponential_fusion.slopes
  30.7 53.1 %shard_map.308 = (bf16[4096,768]{1,0:T(8,128)(2,1)}, bf16[4096,2304]{1,0:T(8,128)(2,1)}, bf16[4096,768]{1,0:T(8,128)(2,1)}, f32[16,6,8,256]{3,2,1,0:T(8,128)}) custom-call(s32[128]{0:T(128)} %get-tuple-element.66.meta, f32[16]{0:T(128)} %multiply_exponential_fusion.slopes, bf16[4,225,4,768]{3,2,1,0:T(4,128)(2,1)} %bitcast.32, s32[4,4,225]{2,1,0:T(4,128)} %rows_in.5, ...), custom_call_target="tpu_custom_call" | custom-call | flops 40000000000 | bytes 4000000 | tf_op jit(solution)/shard_map/pallas_call | solution.py:679
  83.8 10.7 %all-to-all-done = bf16[4,928,768]{2,1,0:T(8,128)(2,1)} async-done(((bf16[4,928,768]{2,1,0:T(8,128)(2,1)}), bf16[4,928,768]{2,1,0:T(8,128)(2,1)}, u32[]{:S(2)}, u32[]{:S(2)}) %all-to-all-start) | async-done | bytes 5701664 | tf_op jit(solution)/shard_map/all_to_all | solution.py:1033
  94.5 124.9 %shard_map.309 = (bf16[4,4,232,768]{3,2,1,0:T(8,128)(2,1)}, f32[4096,768]{1,0:T(8,128)}, bf16[4096,768]{1,0:T(8,128)(2,1)}, bf16[8,432,768]{2,1,0:T(8,128)(2,1)}...) custom-call(s32[128]{0:T(128)} %get-tuple-element.66.meta, ...), custom_call_target="tpu_custom_call" | custom-call | flops 109999996928 | bytes 11000000 | tf_op jit(solution)/shard_map/pallas_call | solution.py:736
  219.4 0.1 collective-permute-start
  219.5 8.9 %shard_map.310.rest_0_ = bf16[4096,2304]{1,0:T(8,128)(2,1)} custom-call(s32[128]{0:T(128)} %get-tuple-element.66.meta, f32[16]{0:T(128)} %multiply_exponential_fusion.slopes, bf16[4096,2304]{1,0:T(8,128)(2,1)} %get-tuple-element.55.qkv, bf16[4096,768]{1,0:T(8,128)(2,1)} %get-tuple-element.56.att_grad, f32[16,6,8,256]{3,2,1,0:T(8,128)} %get-tuple-element.57.totals, ...), custom_call_target="tpu_custom_call" | custom-call | flops 15000000512 | bytes 1500000 | tf_op jit(solution)/shard_map/pallas_call | solution.py:808
  228.5 5.2 %all-to-all-start.1 = ((bf16[4,928,768]{2,1,0:T(8,128)(2,1)}), bf16[4,928,768]{2,1,0:T(8,128)(2,1)}, u32[]{:S(2)}, u32[]{:S(2)}) async-start(bf16[4,928,768]{2,1,0:T(8,128)(2,1)} %bitcast.24), calls=%async_computation.1 | async-start | bytes 11403264 | tf_op jit(solution)/shard_map/all_to_all | solution.py:1033
  233.7 7.7 %add_convert_fusion = bf16[8,432,768]{2,1,0:T(8,128)(2,1)} fusion(bf16[8,432,768]{2,1,0:T(8,128)(2,1)} %collective-permute-done, bf16[8,432,768]{2,1,0:T(8,128)(2,1)} %get-tuple-element.58), kind=kLoop, calls=%fused_computation | loop fusion | flops 10616832 | bytes 15925248 | tf_op jit(solution)/shard_map/convert_element_type | solution.py:931
  241.5 34.1 %shard_map.311.packed_grad = bf16[4096,2304]{1,0:T(8,128)(2,1)} custom-call(s32[128]{0:T(128)} %get-tuple-element.66.meta, f32[16]{0:T(128)} %multiply_exponential_fusion.slopes, bf16[4096,2304]{1,0:T(8,128)(2,1)} %get-tuple-element.55.qkv, bf16[4096,768]{1,0:T(8,128)(2,1)} %get-tuple-element.56.att_grad, ...), custom_call_target="tpu_custom_call", output_to_operand_aliasing={{}: (7, {})} | custom-call | flops 499999997952 | bytes 50000000 | tf_op jit(solution)/shard_map/pallas_call | solution.py:808
  275.6 19.1 %shard_map.312 = (bf16[8,144,768]{2,1,0:T(8,128)(2,1)}, bf16[8,144,768]{2,1,0:T(8,128)(2,1)}, f32[8,2304]{1,0:T(8,128)}) custom-call(s32[128]{0:T(128)} %get-tuple-element.66.meta, bf16[4096,2304]{1,0:T(8,128)(2,1)} %shard_map.311.packed_grad, bf16[4096,768]{1,0:T(8,128)(2,1)} %get-tuple-element.53.tokens_in.tokens, f32[16,768]{1,0:T(8,128)} %get-tuple-element.51.vecs), custom_call_target="tpu_custom_call" | custom-call | flops 15000000512 | bytes 1500000 | tf_op jit(solution)/shard_map/pallas_call | solution.py:846
  294.7 0.1 collective-permute-start.1
  294.8 3.2 all-to-all-done.1
  298.0 7.2 %shard_map.313 = bf16[4,225,4,768]{3,2,1,0:T(4,128)(2,1)} custom-call(s32[16]{0:T(128)} %get-tuple-element.62.take, bf16[4,4,232,768]{3,2,1,0:T(8,128)(2,1)} %bitcast.7.got), custom_call_target="tpu_custom_call" | custom-call | tf_op jit(solution)/shard_map/pallas_call | solution.py:660
  305.3 0.4 add_convert_fusion.1
  305.7 0.1 dynamic-slice_bitcast_fusion.1
  305.8 0.3 collective-permute-start.5
  306.2 23.2 %shard_map.314 = (f32[4,225,4,768]{3,2,1,0:T(4,128)}, f32[16,768]{1,0:T(8,128)}) custom-call(s32[128]{0:T(128)} %get-tuple-element.66.meta, bf16[4096,2304]{1,0:T(8,128)(2,1)} %shard_map.311.packed_grad, bf16[4096,768]{1,0:T(8,128)(2,1)} %get-tuple-element.53.tokens_in.tokens, f32[4096,768]{1,0:T(8,128)} %get-tuple-element.67.mid_grad, ...), custom_call_target="tpu_custom_call" | custom-call | flops 20000000000 | bytes 2000000 | tf_op jit(solution)/shard_map/pallas_call | solution.py:882
  329.4 11.6 %collective-permute-done.5 = bf16[4,144,768]{2,1,0:T(8,128)(2,1)S(1)} collective-permute-done((bf16[4,144,768]{2,1,0:T(8,128)(2,1)S(1)}, bf16[4,144,768]{2,1,0:T(8,128)(2,1)S(1)}, u32[]{:S(2)}, u32[]{:S(2)}) %collective-permute-start.5) | collective-permute-done | bytes 884768 | tf_op jit(solution)/shard_map/ppermute | solution.py:923
  341.0 0.2 add_convert_fusion.2
  341.2 0.1 dynamic-slice_bitcast_fusion.3
  341.3 4.0 collective-permute-start.6
  345.2 1.2 collective-permute-done.2
  346.5 1.8 collective-permute-start.3
  348.3 2.6 collective-permute-done.3
  350.9 19.2 %collective-permute-done.4 = f32[16,768]{1,0:T(8,128)S(1)} collective-permute-done((f32[16,768]{1,0:T(8,128)S(1)}, f32[16,768]{1,0:T(8,128)S(1)}, u32[]{:S(2)}, u32[]{:S(2)}) %collective-permute-start.4) | collective-permute-done | bytes 49184 | tf_op jit(solution)/shard_map/ppermute | solution.py:923
  370.1 0.1 add_convert_fusion.4
  370.3 9.6 %collective-permute-start.8 = (bf16[1,144,768]{2,1,0:T(8,128)(2,1)S(1)}, bf16[1,144,768]{2,1,0:T(8,128)(2,1)S(1)}, u32[]{:S(2)}, u32[]{:S(2)}) collective-permute-start(bf16[1,144,768]{2,1,0:T(8,128)(2,1)S(1)} %get-tuple-element.106), channel_id=1, source_target_pairs={{0,16},{4,20},{8,24},{12,28},{16,0},{20,4},{24,8},{28,12},{1,17},{... | collective-permute-start | bytes 663560 | tf_op jit(solution)/shard_map/ppermute | solution.py:923
  379.9 0.1 collective-permute-start.7
  379.9 10.4 %collective-permute-done.7 = f32[16,768]{1,0:T(8,128)S(1)} collective-permute-done((f32[16,768]{1,0:T(8,128)S(1)}, f32[16,768]{1,0:T(8,128)S(1)}, u32[]{:S(2)}, u32[]{:S(2)}) %collective-permute-start.7) | collective-permute-done | bytes 49184 | tf_op jit(solution)/shard_map/ppermute | solution.py:923
  390.4 8.2 %collective-permute-start.12 = (bf16[432,768]{1,0:T(8,128)(2,1)}, bf16[432,768]{1,0:T(8,128)(2,1)S(1)}, u32[]{:S(2)}, u32[]{:S(2)}) collective-permute-start(bf16[432,768]{1,0:T(8,128)(2,1)} %bitcast.29), channel_id=1, source_target_pairs={{0,2},{1,3},{2,0},{3,1},{4,6},{5,7},{6,4},{7,5},{8,10},{9,11},{10,... | collective-permute-start | bytes 1990664 | tf_op jit(solution)/shard_map/ppermute | solution.py:923
  398.6 0.1 collective-permute-start.10
  398.7 1.9 collective-permute-start.9
  400.7 19.0 %collective-permute-done.9 = f32[16,768]{1,0:T(8,128)S(1)} collective-permute-done((f32[16,768]{1,0:T(8,128)S(1)}, f32[16,768]{1,0:T(8,128)S(1)}, u32[]{:S(2)}, u32[]{:S(2)}) %collective-permute-start.9) | collective-permute-done | bytes 49184 | tf_op jit(solution)/shard_map/ppermute | solution.py:923
  419.6 0.6 reshape.70
  420.3 0.7 slice_reduce_fusion
  421.0 0.1 collective-permute-start.11
  421.1 1.2 add_convert_fusion.3
  422.3 0.6 collective-permute-start.13
  422.9 1.0 maximum_convert_fusion.2
  423.9 0.7 collective-permute-done.13
  424.6 0.1 broadcast_select_fusion.1
  424.8 0.1 fusion.1
  424.9 0.7 maximum_convert_fusion.3
  425.6 1.1 maximum_convert_fusion
  426.7 1.1 maximum_convert_fusion.1
  (30 shorter events, 0.4 us)
Async XLA Ops:
  25.0 69.5 %all-to-all-start = ((bf16[4,928,768]{2,1,0:T(8,128)(2,1)}), bf16[4,928,768]{2,1,0:T(8,128)(2,1)}, u32[]{:S(2)}, u32[]{:S(2)}) async-start(bf16[4,928,768]{2,1,0:T(8,128)(2,1)} %bitcast.25), calls=%async_computation | async-start | bytes 11403264 | tf_op jit(solution)/shard_map/all_to_all | solution.py:1033
  219.4 14.3 %collective-permute-start = (bf16[8,432,768]{2,1,0:T(8,128)(2,1)}, bf16[8,432,768]{2,1,0:T(8,128)(2,1)}, u32[]{:S(2)}, u32[]{:S(2)}) collective-permute-start(bf16[8,432,768]{2,1,0:T(8,128)(2,1)} %get-tuple-element.59), channel_id=1, source_target_pairs={{0,1},{1,0},{2,3},{3,2},{4,5},{5,4},{6,7},{7,6},{8,9},{9,8},{10,11... | collective-permute-start | bytes 15925256 | tf_op jit(solution)/shard_map/ppermute | solution.py:923
  228.5 69.6 %all-to-all-start.1 = ((bf16[4,928,768]{2,1,0:T(8,128)(2,1)}), bf16[4,928,768]{2,1,0:T(8,128)(2,1)}, u32[]{:S(2)}, u32[]{:S(2)}) async-start(bf16[4,928,768]{2,1,0:T(8,128)(2,1)} %bitcast.24), calls=%async_computation.1 | async-start | bytes 11403264 | tf_op jit(solution)/shard_map/all_to_all | solution.py:1033
  233.7 156.8 %reduce-scatter.2.cloned.1.call-start = ((), (), s32[]{:S(2)}) async-start(), calls=%async_computation.3 | async-start | bytes 5971968 | tf_op jit(solution)/shard_map/reduce_scatter | solution.py:1066
  294.7 10.6 %collective-permute-start.1 = (bf16[8,144,768]{2,1,0:T(8,128)(2,1)}, bf16[8,144,768]{2,1,0:T(8,128)(2,1)S(1)}, u32[]{:S(2)}, u32[]{:S(2)}) collective-permute-start(bf16[8,144,768]{2,1,0:T(8,128)(2,1)} %get-tuple-element.65), channel_id=1, source_target_pairs={{0,1},{1,0},{2,3},{3,2},{4,5},{5,4},{6,7},{7,6},{8,9},{9,8},{10,11... | collective-permute-start | bytes 5308424 | tf_op jit(solution)/shard_map/ppermute | solution.py:923
  298.0 7.2 %copy-start = (bf16[8,144,768]{2,1,0:T(8,128)(2,1)S(1)}, bf16[8,144,768]{2,1,0:T(8,128)(2,1)}, u32[]{:S(2)}) copy-start(bf16[8,144,768]{2,1,0:T(8,128)(2,1)} %get-tuple-element.61) | copy-start | bytes 5308420
  305.8 35.2 %collective-permute-start.5 = (bf16[4,144,768]{2,1,0:T(8,128)(2,1)S(1)}, bf16[4,144,768]{2,1,0:T(8,128)(2,1)S(1)}, u32[]{:S(2)}, u32[]{:S(2)}) collective-permute-start(bf16[4,144,768]{2,1,0:T(8,128)(2,1)S(1)} %get-tuple-element.90), channel_id=1, source_target_pairs={{0,4},{4,0},{8,12},{12,8},{16,20},{20,16},{24,28},{28,24},{1,5},{5... | collective-permute-start | bytes 2654216 | tf_op jit(solution)/shard_map/ppermute | solution.py:923
  329.4 15.9 %copy-start.1 = (f32[16,768]{1,0:T(8,128)S(1)}, f32[16,768]{1,0:T(8,128)}, u32[]{:S(2)}) copy-start(f32[16,768]{1,0:T(8,128)} %get-tuple-element.72) | copy-start | bytes 147460
  341.3 28.8 %collective-permute-start.6 = (bf16[2,144,768]{2,1,0:T(8,128)(2,1)S(1)}, bf16[2,144,768]{2,1,0:T(8,128)(2,1)S(1)}, u32[]{:S(2)}, u32[]{:S(2)}) collective-permute-start(bf16[2,144,768]{2,1,0:T(8,128)(2,1)S(1)} %get-tuple-element.94), channel_id=1, source_target_pairs={{0,8},{4,12},{8,0},{12,4},{16,24},{20,28},{24,16},{28,20},{1,9},{5... | collective-permute-start | bytes 1327112 | tf_op jit(solution)/shard_map/ppermute | solution.py:923
  345.2 1.2 collective-permute-start.2
  346.5 4.4 %collective-permute-start.3 = (f32[16,768]{1,0:T(8,128)S(1)}, f32[16,768]{1,0:T(8,128)S(1)}, u32[]{:S(2)}, u32[]{:S(2)}) collective-permute-start(f32[16,768]{1,0:T(8,128)S(1)} %add.90), channel_id=1, source_target_pairs={{0,4},{4,0},{8,12},{12,8},{16,20},{20,16},{24,28},{28,24},{1,5},{5... | collective-permute-start | bytes 147464 | tf_op jit(solution)/shard_map/ppermute | solution.py:923
  350.8 19.2 %collective-permute-start.4 = (f32[16,768]{1,0:T(8,128)S(1)}, f32[16,768]{1,0:T(8,128)S(1)}, u32[]{:S(2)}, u32[]{:S(2)}) collective-permute-start(f32[16,768]{1,0:T(8,128)S(1)} %add.91), channel_id=1, source_target_pairs={{0,8},{4,12},{8,0},{12,4},{16,24},{20,28},{24,16},{28,20},{1,9},{5... | collective-permute-start | bytes 147464 | tf_op jit(solution)/shard_map/ppermute | solution.py:923
  370.3 20.1 %collective-permute-start.8 = (bf16[1,144,768]{2,1,0:T(8,128)(2,1)S(1)}, bf16[1,144,768]{2,1,0:T(8,128)(2,1)S(1)}, u32[]{:S(2)}, u32[]{:S(2)}) collective-permute-start(bf16[1,144,768]{2,1,0:T(8,128)(2,1)S(1)} %get-tuple-element.106), channel_id=1, source_target_pairs={{0,16},{4,20},{8,24},{12,28},{16,0},{20,4},{24,8},{28,12},{1,17},{... | collective-permute-start | bytes 663560 | tf_op jit(solution)/shard_map/ppermute | solution.py:923
  379.9 10.5 %collective-permute-start.7 = (f32[16,768]{1,0:T(8,128)S(1)}, f32[16,768]{1,0:T(8,128)S(1)}, u32[]{:S(2)}, u32[]{:S(2)}) collective-permute-start(f32[16,768]{1,0:T(8,128)S(1)} %add.92), channel_id=1, source_target_pairs={{0,16},{4,20},{8,24},{12,28},{16,0},{20,4},{24,8},{28,12},{1,17},{... | collective-permute-start | bytes 147464 | tf_op jit(solution)/shard_map/ppermute | solution.py:923
  390.4 30.6 %collective-permute-start.12 = (bf16[432,768]{1,0:T(8,128)(2,1)}, bf16[432,768]{1,0:T(8,128)(2,1)S(1)}, u32[]{:S(2)}, u32[]{:S(2)}) collective-permute-start(bf16[432,768]{1,0:T(8,128)(2,1)} %bitcast.29), channel_id=1, source_target_pairs={{0,2},{1,3},{2,0},{3,1},{4,6},{5,7},{6,4},{7,5},{8,10},{9,11},{10,... | collective-permute-start | bytes 1990664 | tf_op jit(solution)/shard_map/ppermute | solution.py:923
  398.6 22.3 %collective-permute-start.10 = (bf16[144,768]{1,0:T(8,128)(2,1)S(1)}, bf16[144,768]{1,0:T(8,128)(2,1)S(1)}, u32[]{:S(2)}, u32[]{:S(2)}) collective-permute-start(bf16[144,768]{1,0:T(8,128)(2,1)S(1)} %fusion), channel_id=1, source_target_pairs={{0,2},{1,3},{2,0},{3,1},{4,6},{5,7},{6,4},{7,5},{8,10},{9,11},{10,... | collective-permute-start | bytes 663560 | tf_op jit(solution)/shard_map/ppermute | solution.py:923
  398.7 20.9 %collective-permute-start.9 = (f32[16,768]{1,0:T(8,128)S(1)}, f32[16,768]{1,0:T(8,128)S(1)}, u32[]{:S(2)}, u32[]{:S(2)}) collective-permute-start(f32[16,768]{1,0:T(8,128)S(1)} %add.101), channel_id=1, source_target_pairs={{0,2},{1,3},{2,0},{3,1},{4,6},{5,7},{6,4},{7,5},{8,10},{9,11},{10,... | collective-permute-start | bytes 147464 | tf_op jit(solution)/shard_map/ppermute | solution.py:923
  421.0 1.9 collective-permute-start.11
  422.3 2.3 collective-permute-start.13
Sparse Core Ops, SparseCore 0:
  241.6 143.1 reduce-scatter.1

commit v2 on v1

--- a/solution.py
+++ b/solution.py
@@ -14,7 +14,7 @@
 FAR = 1e12
 EPS = 1e-06
 BLOCKS = 8
-CHUNK = 1536
+CHUNK = 1024
 VMEM_LIMIT = 60 * 1024 * 1024
 
 F32 = jnp.float32
@@ -58,7 +58,7 @@
 def gelu_parts(u):
     size = jnp.abs(u)
     t = 1.0 / (1.0 + (0.3275911 * math.sqrt(0.5)) * size)
-    bell = jnp.exp(-0.5 * (u * u))
+    bell = jnp.exp2((-0.5 * math.log2(math.e)) * (u * u))
     poly = t * (
         0.5 * 0.254829592
         + t
@@ -124,12 +124,11 @@
     return jnp.where(far, FAR, jnp.sqrt(down * down + across * across))
 
 
-def prepare_kernel(every, counts, present, slots, me, cot, *rest):
-    *lines, meta, take, vecs, send = rest
+def prepare_kernel(group, counts, present, slots, me, cot, *rest):
+    *rest, meta, take, vecs, send = rest
+    every, lines = (slots,) + tuple(rest[: group - 1]), rest[group - 1 :]
     step = pl.program_id(0)
     steps, length, images, width = pl.num_programs(0), cot.shape[1], cot.shape[2], cot.shape[3]
-    group = every.shape[0]
-
     @pl.when(step == 0)
     def _():
         def fill(live):
@@ -169,17 +168,20 @@
         meta[ROWS_FWD] = off
         meta[N_FWD] = (off + TILE - 1) // TILE
 
-        def land(n, carry):
-            a, m, i = n // total, n % total // images, n % images
-            slot = every[a, m, i]
-
-            @pl.when(slot // images == me[0])
-            def _():
-                take[m * images + slot % images] = a * steps + m
-
-            return carry
-
-        lax.fori_loop(0, group * total, land, 0)
+        for back, theirs in enumerate(every):
+            a = (me[0] + group - back) % group
+
+            def land(n, carry):
+                m, i = n // images, n % images
+                slot = theirs[m, i]
+
+                @pl.when(slot // images == me[0])
+                def _():
+                    take[m * images + slot % images] = a * steps + m
+
+                return carry
+
+            lax.fori_loop(0, total, land, 0)
 
     block = jnp.swapaxes(cot[0].astype(F32), 0, 1).astype(BF16)
     for place in range(images):
@@ -314,9 +316,10 @@
 
 def mlp_kernel(
     chunk, length, meta, cot_in, att_in, tokens_in,
-    vecs, out_w, up_w, down_w,
+    vecs, out_hbm, up_hbm, down_hbm,
     y_send, mid_grad, att_grad, keep_g, send_g, vec_g, upb_g,
-    up_b, held, up_acc, down_acc, out_acc, h2_s, h2t_s, dzt_s, z_s, g_s, sem,
+    up_b, held, up_acc, down_acc, out_acc, h2_s, h2t_s, dzt_s, z_s, g_s,
+    out_w, up_w, down_w, sem, sem_w,
 ):
     step = pl.program_id(0)
     tiles = held.shape[0] // TILE - WINDOW // TILE
@@ -328,8 +331,14 @@
         vecs.at[pl.ds(n, 1)] for n in (OUT_B, GAIN_TWO, SHIFT_TWO, DOWN_B)
     ]
 
+    def weight_copies():
+        pairs = ((out_hbm, out_w), (up_hbm, up_w), (down_hbm, down_w))
+        return [pltpu.make_async_copy(a, b, sem_w.at[n]) for n, (a, b) in enumerate(pairs)]
+
     @pl.when(step == 0)
     def _():
+        for copy in weight_copies():
+            copy.start()
         up_acc[...] = jnp.zeros_like(up_acc)
         down_acc[...] = jnp.zeros_like(down_acc)
         out_acc[...] = jnp.zeros_like(out_acc)
@@ -349,6 +358,11 @@
                     held, aligned(meta[OFF + spot]), meta[CNT + spot],
                     cot_in[meta[PEER + spot] // images, 0],
                 )
+
+    @pl.when(step == images)
+    def _():
+        for copy in weight_copies():
+            copy.wait()
 
     def run_tile(t, both):
         rows = aligned(t * TILE, TILE)
@@ -381,7 +395,7 @@
                 g_s[...] += dot_bt(pre_g, up_w[:, cols])
             return carry
 
-        lax.fori_loop(0, hidden // chunk, part, 0)
+        lax.fori_loop(0, hidden // chunk, part, 0, unroll=True)
         held[pl.ds(rows, TILE), :] = z_s[...].astype(BF16)
         if both:
             dzf = dz.astype(F32)
@@ -629,12 +643,12 @@
     return pl.BlockSpec(memory_space=pltpu.SMEM)
 
 
-def prepare(every, counts, present, slots, me, cotangent, *vectors):
+def prepare(others, counts, present, slots, me, cotangent, *vectors):
     steps, length, images, width = cotangent.shape
-    group = every.shape[0]
+    group = len(others) + 1
     padded = (length + 7) // 8 * 8
     return pl.pallas_call(
-        prepare_kernel,
+        functools.partial(prepare_kernel, group),
         out_shape=(
             jax.ShapeDtypeStruct((PLACES,), jnp.int32),
             jax.ShapeDtypeStruct((steps * images,), jnp.int32),
@@ -642,8 +656,9 @@
             jax.ShapeDtypeStruct((group, steps, padded, width), BF16),
         ),
         grid=(steps,),
-        in_specs=[small()] * 5
+        in_specs=[small()] * 4
         + [pl.BlockSpec((1, length, images, width), lambda m: (m, 0, 0, 0))]
+        + [small()] * len(others)
         + [whole(*vector.shape) for vector in vectors],
         out_specs=[
             small(),
@@ -652,7 +667,7 @@
             pl.BlockSpec((group, 1, padded, width), lambda m: (0, m, 0, 0)),
         ],
         compiler_params=params(),
-    )(every, counts, present, slots, me, cotangent, *vectors)
+    )(counts, present, slots, me, cotangent, *others, *vectors)
 
 
 def place(take, got, length):
@@ -754,9 +769,9 @@
                 pl.BlockSpec((TILE, width), fwd_tile),
                 pl.BlockSpec((TILE, width), fwd_tile),
                 whole(*vecs.shape),
-                whole(width, width),
-                whole(width, hidden),
-                whole(hidden, width),
+                pl.BlockSpec(memory_space=pl.ANY),
+                pl.BlockSpec(memory_space=pl.ANY),
+                pl.BlockSpec(memory_space=pl.ANY),
             ],
             out_specs=[
                 pl.BlockSpec(
@@ -781,7 +796,11 @@
                 pltpu.VMEM((width, TILE), BF16),
                 pltpu.VMEM((TILE, width), F32),
                 pltpu.VMEM((TILE, width), F32),
+                pltpu.VMEM((width, width), BF16),
+                pltpu.VMEM((width, hidden), BF16),
+                pltpu.VMEM((hidden, width), BF16),
                 pltpu.SemaphoreType.DMA((2, BLOCKS)),
+                pltpu.SemaphoreType.DMA((3,)),
             ],
         ),
         compiler_params=params(),
@@ -1036,7 +1055,11 @@
         return jnp.transpose(array, (0, 2, 1, 3))
 
     meta, take, vecs, cot_send = prepare(
-        lax.all_gather(slots, "bal"), counts, present, slots,
+        [
+            lax.ppermute(slots, "bal", [(a, (a + k) % group) for a in range(group)])
+            for k in range(1, group)
+        ],
+        counts, present, slots,
         lax.axis_index("bal").astype(jnp.int32).reshape(1), turn(cotangent),
         first_gain, first_shift, query_bias, value_bias, out_bias, second_gain, second_shift,
         down_bias, up_bias,
@@ -1046,8 +1069,6 @@
     y_send, mid_grad, att_grad, keep_two, send_two, vec_two, upb_g = mlp(
         meta, cot_home, att, packed, vecs, out_weight, up_weight, down_weight, length
     )
-    y_got = exchange(y_send)
-
     share, long = width // BLOCKS, hidden // BLOCKS
     shapes_two = ((share, hidden, "columns"), (long, width, "side"), (share, width, "rows"))
     shapes_one = ((share, 3 * width, "rows"),)
@@ -1065,6 +1086,8 @@
         sum_two = added(after(keep_two, packed_grad), swap(send_two, "bal", 1))
         share_two = lax.psum_scatter(sum_two, "dp", scatter_dimension=0, tiled=True)[0]
         table = after(meta, sum_two)
+        y_send = after(y_send, sum_two)
+    y_got = exchange(y_send)
     packed_grad = back(lead, total - lead, 500, table, (packed_grad,))
     keep_one, send_one, bias_g = qkv_grad(table, packed_grad, packed, vecs)
     output = place(after(take, keep_one), y_got.reshape(group, steps, -1, width), length)

time: 435 us -> 434 us (level); the launches traced: 435 us -> 426 us
  starting transfers between devices: 37.1 us -> 75.8 us
  Pallas kernels: 280 us -> 249 us
  waiting for transfers between devices: 78.7 us -> 67.7 us
  blocking collectives: 7.95 us -> 0 us
    ppermute x14, starting transfers between devices: 26.8 us -> 60.8 us  [swap(): return lax.ppermute(block, axis, [(n, n ^ bit) for n in range(size)])]
    pallas_call x1, Pallas kernels: 125 us -> 114 us  [mlp(): pl.pallas_call(functools.partial(mlp_kernel, CHUNK, length), out_shape=(j...]
    pallas_call x2, Pallas kernels: 43.1 us -> 32.7 us  [attend_back(): pl.pallas_call(functools.partial(attend_back_kernel, first, per), out_sha...]
    ppermute x14, waiting for transfers between devices: 64.7 us -> 54.8 us  [swap(): return lax.ppermute(block, axis, [(n, n ^ bit) for n in range(size)])]
    all_gather x1 -> x0, blocking collectives: 7.95 us -> none  [per_device(): lax.all_gather(slots, 'bal')]
    ppermute x0 -> x3, starting transfers between devices: none -> 4.46 us  [per_device(): lax.ppermute(slots, 'bal', [(a, (a + k) % group) for a in range(group)])]
    pallas_call x1, Pallas kernels: 23.2 us -> 18.8 us  [token_grad(): pl.pallas_call(token_grad_kernel, out_shape=(jax.ShapeDtypeStruct((steps,...]
  transfers between devices with their start and end apart: 17 -> 20, of which waited for: 9 -> 11; matrix products, arithmetic and copies ran while one was open for 3% -> 2% of each run, Pallas kernels for 33% -> 30%
where the time goes in v2:
time: 434 us; the launch traced here: 426 us
  Pallas kernels  249 us (57%)
  starting transfers between devices  75.8 us (17%)
  waiting for transfers between devices  67.7 us (16%)
  other arithmetic  16 us (4%)
  between operations  14.5 us (3%)
    pallas_call x1, Pallas kernels, mlp(): pl.pallas_call(functools.partial(mlp_kernel, CHUNK, length), out_shape=(j...  114 us
    ppermute x14, starting transfers between devices, swap(): return lax.ppermute(block, axis, [(n, n ^ bit) for n in range(size)])  60.8 us
    ppermute x14, waiting for transfers between devices, swap(): return lax.ppermute(block, axis, [(n, n ^ bit) for n in range(size)])  54.8 us
    pallas_call x1, Pallas kernels, first_half(): pl.pallas_call(attend_kernel, out_shape=(jax.ShapeDtypeStruct((total, wid...  52.5 us
    pallas_call x2, Pallas kernels, attend_back(): pl.pallas_call(functools.partial(attend_back_kernel, first, per), out_sha...  32.7 us
    pallas_call x1, Pallas kernels, token_grad(): pl.pallas_call(token_grad_kernel, out_shape=(jax.ShapeDtypeStruct((steps,...  18.8 us
    pallas_call x1, Pallas kernels, qkv_grad(): pl.pallas_call(qkv_grad_kernel, out_shape=(jax.ShapeDtypeStruct((BLOCKS,...  14.7 us
    convert_element_type x6, other arithmetic, added(): return (a.astype(F32) + b.astype(F32)).astype(BF16)  11.4 us
  transfers between devices with their start and end apart: 20, of which 11 were waited for; matrix products, arithmetic and copies ran while one was open for 2% of the time, Pallas kernels for 30%

profile of v2, /device:TPU:0, one launch (start us, length us, event | category | flops | bytes accessed | tf_op | source)
XLA Modules:
  0.0 425.6 jit_solution(11726988552990053924)
XLA Ops:
  7.2 0.5 collective-permute-start
  7.7 2.6 collective-permute-start.1
  10.3 1.4 collective-permute-start.2
  11.6 0.4 collective-permute-done.1.rest_1_
  12.0 1.1 collective-permute-done.2.rest_2_
  13.2 0.6 copy-done.3
  13.7 9.5 %shard_map.307 = (s32[128]{0:T(128)}, s32[16]{0:T(128)}, f32[16,768]{1,0:T(8,128)}, bf16[4,4,232,768]{3,2,1,0:T(8,128)(2,1)}) custom-call(s32[4,4]{1,0:T(4,128)} %counts.1, s32[4,4]{1,0:T(4,128)} %present.1, s32[4,4]{1,0:T(4,128)} %slots.1, s32[1]{0:T(128)} %bitcast.me, bf16[4,225,4,768]{3,2,1,0:T(4,128)(2,1)} %bitcast.26, s32[4,4]{1,0:T(4,128)} %copy-done.1, ...), custom_call_target="tpu_custom_call" | custom-call | tf_op jit(solution)/shard_map/pallas_call | solution.py:650
  23.3 5.1 %all-to-all-start = ((bf16[4,928,768]{2,1,0:T(8,128)(2,1)}), bf16[4,928,768]{2,1,0:T(8,128)(2,1)}, u32[]{:S(2)}, u32[]{:S(2)}) async-start(bf16[4,928,768]{2,1,0:T(8,128)(2,1)} %bitcast.24), calls=%async_computation | async-start | bytes 11403264 | tf_op jit(solution)/shard_map/all_to_all | solution.py:1052
  28.5 0.5 multiply_exponential_fusion.slopes
  29.0 52.5 %shard_map.308 = (bf16[4096,768]{1,0:T(8,128)(2,1)}, bf16[4096,2304]{1,0:T(8,128)(2,1)}, bf16[4096,768]{1,0:T(8,128)(2,1)}, f32[16,6,8,256]{3,2,1,0:T(8,128)}) custom-call(s32[128]{0:T(128)} %get-tuple-element.68.meta, f32[16]{0:T(128)} %multiply_exponential_fusion.slopes, bf16[4,225,4,768]{3,2,1,0:T(4,128)(2,1)} %bitcast.30, s32[4,4,225]{2,1,0:T(4,128)} %rows_in.5, ...), custom_call_target="tpu_custom_call" | custom-call | flops 40000000000 | bytes 4000000 | tf_op jit(solution)/shard_map/pallas_call | solution.py:694
  81.5 11.3 %all-to-all-done = bf16[4,928,768]{2,1,0:T(8,128)(2,1)} async-done(((bf16[4,928,768]{2,1,0:T(8,128)(2,1)}), bf16[4,928,768]{2,1,0:T(8,128)(2,1)}, u32[]{:S(2)}, u32[]{:S(2)}) %all-to-all-start) | async-done | bytes 5701664 | tf_op jit(solution)/shard_map/all_to_all | solution.py:1052
  92.8 114.1 %shard_map.309 = (bf16[4,4,232,768]{3,2,1,0:T(8,128)(2,1)}, f32[4096,768]{1,0:T(8,128)}, bf16[4096,768]{1,0:T(8,128)(2,1)}, bf16[8,432,768]{2,1,0:T(8,128)(2,1)}...) custom-call(s32[128]{0:T(128)} %get-tuple-element.68.meta, ...), custom_call_target="tpu_custom_call" | custom-call | flops 109999996928 | bytes 11000000 | tf_op jit(solution)/shard_map/pallas_call | solution.py:751
  206.9 11.8 %collective-permute-start.3 = (bf16[8,432,768]{2,1,0:T(8,128)(2,1)}, bf16[8,432,768]{2,1,0:T(8,128)(2,1)}, u32[]{:S(2)}, u32[]{:S(2)}) collective-permute-start(bf16[8,432,768]{2,1,0:T(8,128)(2,1)} %get-tuple-element.60), channel_id=1, source_target_pairs={{0,1},{1,0},{2,3},{3,2},{4,5},{5,4},{6,7},{7,6},{8,9},{9,8},{10,11... | collective-permute-start | bytes 15925256 | tf_op jit(solution)/shard_map/ppermute | solution.py:942
  218.6 7.8 %shard_map.310.rest_0_ = bf16[4096,2304]{1,0:T(8,128)(2,1)} custom-call(s32[128]{0:T(128)} %get-tuple-element.68.meta, f32[16]{0:T(128)} %multiply_exponential_fusion.slopes, bf16[4096,2304]{1,0:T(8,128)(2,1)} %get-tuple-element.56.qkv, bf16[4096,768]{1,0:T(8,128)(2,1)} %get-tuple-element.57.att_grad, f32[16,6,8,256]{3,2,1,0:T(8,128)} %get-tuple-element.58.totals, ...), custom_call_target="tpu_custom_call" | custom-call | flops 15000000512 | bytes 1500000 | tf_op jit(solution)/shard_map/pallas_call | solution.py:827
  226.5 0.9 collective-permute-done.3
  227.4 7.8 %add_convert_fusion = bf16[8,432,768]{2,1,0:T(8,128)(2,1)} fusion(bf16[8,432,768]{2,1,0:T(8,128)(2,1)} %collective-permute-done.3, bf16[8,432,768]{2,1,0:T(8,128)(2,1)} %get-tuple-element.59), kind=kLoop, calls=%fused_computation | loop fusion | flops 10616832 | bytes 15925248 | tf_op jit(solution)/shard_map/convert_element_type | solution.py:950
  235.2 5.4 %all-to-all-start.1 = ((bf16[4,928,768]{2,1,0:T(8,128)(2,1)}), bf16[4,928,768]{2,1,0:T(8,128)(2,1)}, u32[]{:S(2)}, u32[]{:S(2)}) async-start(bf16[4,928,768]{2,1,0:T(8,128)(2,1)} %bitcast.23), calls=%async_computation.1 | async-start | bytes 11403264 | tf_op jit(solution)/shard_map/all_to_all | solution.py:1052
  240.6 24.9 %shard_map.311.packed_grad = bf16[4096,2304]{1,0:T(8,128)(2,1)} custom-call(s32[128]{0:T(128)} %get-tuple-element.68.meta, f32[16]{0:T(128)} %multiply_exponential_fusion.slopes, bf16[4096,2304]{1,0:T(8,128)(2,1)} %get-tuple-element.56.qkv, bf16[4096,768]{1,0:T(8,128)(2,1)} %get-tuple-element.57.att_grad, ...), custom_call_target="tpu_custom_call", output_to_operand_aliasing={{}: (7, {})} | custom-call | flops 499999997952 | bytes 50000000 | tf_op jit(solution)/shard_map/pallas_call | solution.py:827
  265.5 14.7 %shard_map.312 = (bf16[8,144,768]{2,1,0:T(8,128)(2,1)}, bf16[8,144,768]{2,1,0:T(8,128)(2,1)}, f32[8,2304]{1,0:T(8,128)}) custom-call(s32[128]{0:T(128)} %get-tuple-element.68.meta, bf16[4096,2304]{1,0:T(8,128)(2,1)} %shard_map.311.packed_grad, bf16[4096,768]{1,0:T(8,128)(2,1)} %get-tuple-element.54.tokens_in.tokens, f32[16,768]{1,0:T(8,128)} %get-tuple-element.52.vecs), custom_call_target="tpu_custom_call" | custom-call | flops 15000000512 | bytes 1500000 | tf_op jit(solution)/shard_map/pallas_call | solution.py:865
  280.2 10.9 %collective-permute-start.4 = (bf16[8,144,768]{2,1,0:T(8,128)(2,1)}, bf16[8,144,768]{2,1,0:T(8,128)(2,1)S(1)}, u32[]{:S(2)}, u32[]{:S(2)}) collective-permute-start(bf16[8,144,768]{2,1,0:T(8,128)(2,1)} %get-tuple-element.67), channel_id=1, source_target_pairs={{0,1},{1,0},{2,3},{3,2},{4,5},{5,4},{6,7},{7,6},{8,9},{9,8},{10,11... | collective-permute-start | bytes 5308424 | tf_op jit(solution)/shard_map/ppermute | solution.py:942
  291.1 3.5 collective-permute-done.4
  294.6 1.9 add_convert_fusion.1
  296.7 21.4 %collective-permute-start.8 = (bf16[4,144,768]{2,1,0:T(8,128)(2,1)S(1)}, bf16[4,144,768]{2,1,0:T(8,128)(2,1)S(1)}, u32[]{:S(2)}, u32[]{:S(2)}) collective-permute-start(bf16[4,144,768]{2,1,0:T(8,128)(2,1)S(1)} %get-tuple-element.92), channel_id=1, source_target_pairs={{0,4},{4,0},{8,12},{12,8},{16,20},{20,16},{24,28},{28,24},{1,5},{5... | collective-permute-start | bytes 2654216 | tf_op jit(solution)/shard_map/ppermute | solution.py:942
  318.0 7.0 %shard_map.313 = bf16[4,225,4,768]{3,2,1,0:T(4,128)(2,1)} custom-call(s32[16]{0:T(128)} %get-tuple-element.63.take, bf16[4,4,232,768]{3,2,1,0:T(8,128)(2,1)} %bitcast.6.got), custom_call_target="tpu_custom_call" | custom-call | tf_op jit(solution)/shard_map/pallas_call | solution.py:675
  325.0 18.8 %shard_map.314 = (f32[4,225,4,768]{3,2,1,0:T(4,128)}, f32[16,768]{1,0:T(8,128)}) custom-call(s32[128]{0:T(128)} %get-tuple-element.68.meta, bf16[4096,2304]{1,0:T(8,128)(2,1)} %shard_map.311.packed_grad, bf16[4096,768]{1,0:T(8,128)(2,1)} %get-tuple-element.54.tokens_in.tokens, f32[4096,768]{1,0:T(8,128)} %get-tuple-element.69.mid_grad, ...), custom_call_target="tpu_custom_call" | custom-call | flops 20000000000 | bytes 2000000 | tf_op jit(solution)/shard_map/pallas_call | solution.py:901
  344.2 2.9 collective-permute-start.9
  347.1 0.7 collective-permute-start.5
  347.8 0.9 collective-permute-done.5
  348.7 4.8 %collective-permute-start.6 = (f32[16,768]{1,0:T(8,128)S(1)}, f32[16,768]{1,0:T(8,128)S(1)}, u32[]{:S(2)}, u32[]{:S(2)}) collective-permute-start(f32[16,768]{1,0:T(8,128)S(1)} %add.90), channel_id=1, source_target_pairs={{0,4},{4,0},{8,12},{12,8},{16,20},{20,16},{24,28},{28,24},{1,5},{5... | collective-permute-start | bytes 147464 | tf_op jit(solution)/shard_map/ppermute | solution.py:942
  353.5 2.3 collective-permute-done.6
  355.8 1.4 collective-permute-start.7
  357.2 14.8 %collective-permute-done.7 = f32[16,768]{1,0:T(8,128)S(1)} collective-permute-done((f32[16,768]{1,0:T(8,128)S(1)}, f32[16,768]{1,0:T(8,128)S(1)}, u32[]{:S(2)}, u32[]{:S(2)}) %collective-permute-start.7) | collective-permute-done | bytes 49184 | tf_op jit(solution)/shard_map/ppermute | solution.py:942
  372.2 2.6 collective-permute-start.11
  374.8 0.4 collective-permute-start.10
  375.2 12.2 %collective-permute-done.10 = f32[16,768]{1,0:T(8,128)S(1)} collective-permute-done((f32[16,768]{1,0:T(8,128)S(1)}, f32[16,768]{1,0:T(8,128)S(1)}, u32[]{:S(2)}, u32[]{:S(2)}) %collective-permute-start.10) | collective-permute-done | bytes 49184 | tf_op jit(solution)/shard_map/ppermute | solution.py:942
  387.5 1.4 collective-permute-start.15
  388.9 0.7 collective-permute-start.13
  389.6 1.3 collective-permute-start.12
  390.9 19.5 %collective-permute-done.12 = f32[16,768]{1,0:T(8,128)S(1)} collective-permute-done((f32[16,768]{1,0:T(8,128)S(1)}, f32[16,768]{1,0:T(8,128)S(1)}, u32[]{:S(2)}, u32[]{:S(2)}) %collective-permute-start.12) | collective-permute-done | bytes 49184 | tf_op jit(solution)/shard_map/ppermute | solution.py:942
  410.4 0.6 reshape.70
  411.0 0.7 slice_reduce_fusion
  411.8 1.2 add_convert_fusion.3
  413.1 0.6 collective-permute-start.16
  413.7 1.0 maximum_convert_fusion.2
  414.7 0.7 collective-permute-done.16
  415.6 0.7 maximum_convert_fusion.3
  416.4 1.1 maximum_convert_fusion
  417.5 1.1 maximum_convert_fusion.1
  (39 shorter events, 1.2 us)
Async XLA Ops:
  7.2 4.5 %collective-permute-start = (s32[4,4]{1,0:T(4,128)}, s32[4,4]{1,0:T(4,128)S(1)}, u32[]{:S(2)}, u32[]{:S(2)}) collective-permute-start(s32[4,4]{1,0:T(4,128)} %slots.1), channel_id=1, source_target_pairs={{0,1},{1,2},{2,3},{3,0},{4,5},{5,6},{6,7},{7,4},{8,9},{9,10},{10,1... | collective-permute-start | bytes 200 | tf_op jit(solution)/shard_map/ppermute | solution.py:1059
  7.7 4.3 %collective-permute-start.1 = (s32[4,4]{1,0:T(4,128)}, s32[4,4]{1,0:T(4,128)S(1)}, u32[]{:S(2)}, u32[]{:S(2)}) collective-permute-start(s32[4,4]{1,0:T(4,128)} %slots.1), channel_id=1, source_target_pairs={{0,2},{1,3},{2,0},{3,1},{4,6},{5,7},{6,4},{7,5},{8,10},{9,11},{10,... | collective-permute-start | bytes 200 | tf_op jit(solution)/shard_map/ppermute | solution.py:1059
  10.3 2.9 collective-permute-start.2
  11.6 1.5 copy-start.1
  12.0 1.1 copy-start.2
  13.2 0.6 copy-start.3
  23.3 69.5 %all-to-all-start = ((bf16[4,928,768]{2,1,0:T(8,128)(2,1)}), bf16[4,928,768]{2,1,0:T(8,128)(2,1)}, u32[]{:S(2)}, u32[]{:S(2)}) async-start(bf16[4,928,768]{2,1,0:T(8,128)(2,1)} %bitcast.24), calls=%async_computation | async-start | bytes 11403264 | tf_op jit(solution)/shard_map/all_to_all | solution.py:1052
  28.4 359.1 %reduce-scatter.2.cloned.1.call-start = ((), (), s32[]{:S(2)}) async-start(), calls=%async_computation.3 | async-start | bytes 5971968 | tf_op jit(solution)/shard_map/reduce_scatter | solution.py:1087
  206.9 20.5 %collective-permute-start.3 = (bf16[8,432,768]{2,1,0:T(8,128)(2,1)}, bf16[8,432,768]{2,1,0:T(8,128)(2,1)}, u32[]{:S(2)}, u32[]{:S(2)}) collective-permute-start(bf16[8,432,768]{2,1,0:T(8,128)(2,1)} %get-tuple-element.60), channel_id=1, source_target_pairs={{0,1},{1,0},{2,3},{3,2},{4,5},{5,4},{6,7},{7,6},{8,9},{9,8},{10,11... | collective-permute-start | bytes 15925256 | tf_op jit(solution)/shard_map/ppermute | solution.py:942
  235.2 82.8 %all-to-all-start.1 = ((bf16[4,928,768]{2,1,0:T(8,128)(2,1)}), bf16[4,928,768]{2,1,0:T(8,128)(2,1)}, u32[]{:S(2)}, u32[]{:S(2)}) async-start(bf16[4,928,768]{2,1,0:T(8,128)(2,1)} %bitcast.23), calls=%async_computation.1 | async-start | bytes 11403264 | tf_op jit(solution)/shard_map/all_to_all | solution.py:1052
  280.2 14.4 %collective-permute-start.4 = (bf16[8,144,768]{2,1,0:T(8,128)(2,1)}, bf16[8,144,768]{2,1,0:T(8,128)(2,1)S(1)}, u32[]{:S(2)}, u32[]{:S(2)}) collective-permute-start(bf16[8,144,768]{2,1,0:T(8,128)(2,1)} %get-tuple-element.67), channel_id=1, source_target_pairs={{0,1},{1,0},{2,3},{3,2},{4,5},{5,4},{6,7},{7,6},{8,9},{9,8},{10,11... | collective-permute-start | bytes 5308424 | tf_op jit(solution)/shard_map/ppermute | solution.py:942
  296.7 47.2 %collective-permute-start.8 = (bf16[4,144,768]{2,1,0:T(8,128)(2,1)S(1)}, bf16[4,144,768]{2,1,0:T(8,128)(2,1)S(1)}, u32[]{:S(2)}, u32[]{:S(2)}) collective-permute-start(bf16[4,144,768]{2,1,0:T(8,128)(2,1)S(1)} %get-tuple-element.92), channel_id=1, source_target_pairs={{0,4},{4,0},{8,12},{12,8},{16,20},{20,16},{24,28},{28,24},{1,5},{5... | collective-permute-start | bytes 2654216 | tf_op jit(solution)/shard_map/ppermute | solution.py:942
  343.9 3.2 copy-start
  344.2 27.9 %collective-permute-start.9 = (bf16[2,144,768]{2,1,0:T(8,128)(2,1)S(1)}, bf16[2,144,768]{2,1,0:T(8,128)(2,1)S(1)}, u32[]{:S(2)}, u32[]{:S(2)}) collective-permute-start(bf16[2,144,768]{2,1,0:T(8,128)(2,1)S(1)} %get-tuple-element.96), channel_id=1, source_target_pairs={{0,8},{4,12},{8,0},{12,4},{16,24},{20,28},{24,16},{28,20},{1,9},{5... | collective-permute-start | bytes 1327112 | tf_op jit(solution)/shard_map/ppermute | solution.py:942
  347.1 1.6 collective-permute-start.5
  348.7 7.1 %collective-permute-start.6 = (f32[16,768]{1,0:T(8,128)S(1)}, f32[16,768]{1,0:T(8,128)S(1)}, u32[]{:S(2)}, u32[]{:S(2)}) collective-permute-start(f32[16,768]{1,0:T(8,128)S(1)} %add.90), channel_id=1, source_target_pairs={{0,4},{4,0},{8,12},{12,8},{16,20},{20,16},{24,28},{28,24},{1,5},{5... | collective-permute-start | bytes 147464 | tf_op jit(solution)/shard_map/ppermute | solution.py:942
  355.8 16.2 %collective-permute-start.7 = (f32[16,768]{1,0:T(8,128)S(1)}, f32[16,768]{1,0:T(8,128)S(1)}, u32[]{:S(2)}, u32[]{:S(2)}) collective-permute-start(f32[16,768]{1,0:T(8,128)S(1)} %add.91), channel_id=1, source_target_pairs={{0,8},{4,12},{8,0},{12,4},{16,24},{20,28},{24,16},{28,20},{1,9},{5... | collective-permute-start | bytes 147464 | tf_op jit(solution)/shard_map/ppermute | solution.py:942
  372.2 15.2 %collective-permute-start.11 = (bf16[1,144,768]{2,1,0:T(8,128)(2,1)S(1)}, bf16[1,144,768]{2,1,0:T(8,128)(2,1)S(1)}, u32[]{:S(2)}, u32[]{:S(2)}) collective-permute-start(bf16[1,144,768]{2,1,0:T(8,128)(2,1)S(1)} %get-tuple-element.108), channel_id=1, source_target_pairs={{0,16},{4,20},{8,24},{12,28},{16,0},{20,4},{24,8},{28,12},{1,17},{... | collective-permute-start | bytes 663560 | tf_op jit(solution)/shard_map/ppermute | solution.py:942
  374.8 12.5 %collective-permute-start.10 = (f32[16,768]{1,0:T(8,128)S(1)}, f32[16,768]{1,0:T(8,128)S(1)}, u32[]{:S(2)}, u32[]{:S(2)}) collective-permute-start(f32[16,768]{1,0:T(8,128)S(1)} %add.92), channel_id=1, source_target_pairs={{0,16},{4,20},{8,24},{12,28},{16,0},{20,4},{24,8},{28,12},{1,17},{... | collective-permute-start | bytes 147464 | tf_op jit(solution)/shard_map/ppermute | solution.py:942
  387.5 24.3 %collective-permute-start.15 = (bf16[432,768]{1,0:T(8,128)(2,1)}, bf16[432,768]{1,0:T(8,128)(2,1)S(1)}, u32[]{:S(2)}, u32[]{:S(2)}) collective-permute-start(bf16[432,768]{1,0:T(8,128)(2,1)} %bitcast.28), channel_id=1, source_target_pairs={{0,2},{1,3},{2,0},{3,1},{4,6},{5,7},{6,4},{7,5},{8,10},{9,11},{10,... | collective-permute-start | bytes 1990664 | tf_op jit(solution)/shard_map/ppermute | solution.py:942
  388.9 22.8 %collective-permute-start.13 = (bf16[144,768]{1,0:T(8,128)(2,1)S(1)}, bf16[144,768]{1,0:T(8,128)(2,1)S(1)}, u32[]{:S(2)}, u32[]{:S(2)}) collective-permute-start(bf16[144,768]{1,0:T(8,128)(2,1)S(1)} %fusion), channel_id=1, source_target_pairs={{0,2},{1,3},{2,0},{3,1},{4,6},{5,7},{6,4},{7,5},{8,10},{9,11},{10,... | collective-permute-start | bytes 663560 | tf_op jit(solution)/shard_map/ppermute | solution.py:942
  389.6 20.8 %collective-permute-start.12 = (f32[16,768]{1,0:T(8,128)S(1)}, f32[16,768]{1,0:T(8,128)S(1)}, u32[]{:S(2)}, u32[]{:S(2)}) collective-permute-start(f32[16,768]{1,0:T(8,128)S(1)} %add.101), channel_id=1, source_target_pairs={{0,2},{1,3},{2,0},{3,1},{4,6},{5,7},{6,4},{7,5},{8,10},{9,11},{10,... | collective-permute-start | bytes 147464 | tf_op jit(solution)/shard_map/ppermute | solution.py:942
  411.7 1.9 collective-permute-start.14
  413.1 2.3 collective-permute-start.16
Sparse Core Ops, SparseCore 0:
  235.3 135.9 reduce-scatter.1

commit v3 on v2

--- a/solution.py
+++ b/solution.py
@@ -1007,12 +1007,11 @@
 
 
 def doubled(block, round_no):
-    bits = [("bal", 1)]
+    bits = [("bal", 1), ("bal", 2)]
     bit = 1
     while bit < lax.axis_size("dp"):
         bits.append(("dp", bit))
         bit *= 2
-    bits.append(("bal", 2))
     if round_no is None:
         return len(bits)
     axis, bit = bits[round_no]
@@ -1109,9 +1108,9 @@
         block = added(after(keep, vectors), crossing)
         keep, crossing = start_fold(block, 4)
         vectors = doubled(after(vectors, block), rounds - 2)
-        block = added(after(keep, vectors), crossing).reshape(sum_one.shape[-2:])
+        across_two = swap(share_two, "bal", 2)
+        block = added(after(keep, vectors, share_two), crossing).reshape(sum_one.shape[-2:])
         across_one = swap(block, "bal", 2)
-        across_two = swap(after(share_two, block), "bal", 2)
         vectors = doubled(after(vectors, block), rounds - 1)
         full_one = added(after(block, vectors), across_one)
         full_two = added(after(share_two, full_one), across_two)

time: 434 us -> 426 us (0.982); the launches traced: 426 us -> 425 us
  Pallas kernels: 249 us -> 296 us
  waiting for transfers between devices: 67.7 us -> 40.5 us
  starting transfers between devices: 75.8 us -> 55.7 us
    ppermute x14, waiting for transfers between devices: 54.8 us -> 27.3 us  [swap(): return lax.ppermute(block, axis, [(n, n ^ bit) for n in range(size)])]
    pallas_call x1, Pallas kernels: 114 us -> 137 us  [mlp(): pl.pallas_call(functools.partial(mlp_kernel, CHUNK, length), out_shape=(j...]
    ppermute x14, starting transfers between devices: 60.8 us -> 40.7 us  [swap(): return lax.ppermute(block, axis, [(n, n ^ bit) for n in range(size)])]
    pallas_call x2, Pallas kernels: 32.7 us -> 42.7 us  [attend_back(): pl.pallas_call(functools.partial(attend_back_kernel, first, per), out_sha...]
    pallas_call x1, Pallas kernels: 52.5 us -> 58.1 us  [first_half(): pl.pallas_call(attend_kernel, out_shape=(jax.ShapeDtypeStruct((total, wid...]
    pallas_call x1, Pallas kernels: 14.7 us -> 19.1 us  [qkv_grad(): pl.pallas_call(qkv_grad_kernel, out_shape=(jax.ShapeDtypeStruct((BLOCKS,...]
  transfers between devices with their start and end apart: 20 -> 20, of which waited for: 11 -> 12; matrix products, arithmetic and copies ran while one was open for 2% -> 1% of each run, Pallas kernels for 30% -> 35%
where the time goes in v3:
time: 426 us; the launch traced here: 425 us
  Pallas kernels  296 us (69%)
  starting transfers between devices  55.7 us (13%)
  waiting for transfers between devices  40.5 us (10%)
  other arithmetic  14.9 us (3%)
  between operations  14.6 us (3%)
    pallas_call x1, Pallas kernels, mlp(): pl.pallas_call(functools.partial(mlp_kernel, CHUNK, length), out_shape=(j...  137 us
    pallas_call x1, Pallas kernels, first_half(): pl.pallas_call(attend_kernel, out_shape=(jax.ShapeDtypeStruct((total, wid...  58.1 us
    pallas_call x2, Pallas kernels, attend_back(): pl.pallas_call(functools.partial(attend_back_kernel, first, per), out_sha...  42.7 us
    ppermute x14, starting transfers between devices, swap(): return lax.ppermute(block, axis, [(n, n ^ bit) for n in range(size)])  40.7 us
    ppermute x14, waiting for transfers between devices, swap(): return lax.ppermute(block, axis, [(n, n ^ bit) for n in range(size)])  27.3 us
    pallas_call x1, Pallas kernels, token_grad(): pl.pallas_call(token_grad_kernel, out_shape=(jax.ShapeDtypeStruct((steps,...  23.1 us
    pallas_call x1, Pallas kernels, qkv_grad(): pl.pallas_call(qkv_grad_kernel, out_shape=(jax.ShapeDtypeStruct((BLOCKS,...  19.1 us
    all_to_all x2, waiting for transfers between devices, exchange(): return lax.all_to_all(flat, 'bal', split_axis=0, concat_axis=0, tiled=True)  11.7 us
  transfers between devices with their start and end apart: 20, of which 12 were waited for; matrix products, arithmetic and copies ran while one was open for 1% of the time, Pallas kernels for 35%

profile of v3, /device:TPU:0, one launch (start us, length us, event | category | flops | bytes accessed | tf_op | source)
XLA Modules:
  0.0 424.8 jit_solution(6958500245099607831)
XLA Ops:
  7.2 0.5 collective-permute-start
  7.7 2.6 collective-permute-start.1
  10.3 1.4 collective-permute-start.2
  11.6 0.4 collective-permute-done.1.rest_1_
  12.0 1.1 collective-permute-done.2.rest_2_
  13.2 0.6 copy-done.4
  13.7 9.6 %shard_map.307 = (s32[128]{0:T(128)}, s32[16]{0:T(128)}, f32[16,768]{1,0:T(8,128)}, bf16[4,4,232,768]{3,2,1,0:T(8,128)(2,1)}) custom-call(s32[4,4]{1,0:T(4,128)} %counts.1, s32[4,4]{1,0:T(4,128)} %present.1, s32[4,4]{1,0:T(4,128)} %slots.1, s32[1]{0:T(128)} %bitcast.me, bf16[4,225,4,768]{3,2,1,0:T(4,128)(2,1)} %bitcast.26, s32[4,4]{1,0:T(4,128)} %copy-done.2, ...), custom_call_target="tpu_custom_call" | custom-call | tf_op jit(solution)/shard_map/pallas_call | solution.py:650
  23.3 5.1 %all-to-all-start = ((bf16[4,928,768]{2,1,0:T(8,128)(2,1)}), bf16[4,928,768]{2,1,0:T(8,128)(2,1)}, u32[]{:S(2)}, u32[]{:S(2)}) async-start(bf16[4,928,768]{2,1,0:T(8,128)(2,1)} %bitcast.24), calls=%async_computation | async-start | bytes 11403264 | tf_op jit(solution)/shard_map/all_to_all | solution.py:1051
  28.5 0.5 multiply_exponential_fusion.slopes
  29.0 58.1 %shard_map.308 = (bf16[4096,768]{1,0:T(8,128)(2,1)}, bf16[4096,2304]{1,0:T(8,128)(2,1)}, bf16[4096,768]{1,0:T(8,128)(2,1)}, f32[16,6,8,256]{3,2,1,0:T(8,128)}) custom-call(s32[128]{0:T(128)} %get-tuple-element.67.meta, f32[16]{0:T(128)} %multiply_exponential_fusion.slopes, bf16[4,225,4,768]{3,2,1,0:T(4,128)(2,1)} %bitcast.30, s32[4,4,225]{2,1,0:T(4,128)} %rows_in.5, ...), custom_call_target="tpu_custom_call" | custom-call | flops 40000000000 | bytes 4000000 | tf_op jit(solution)/shard_map/pallas_call | solution.py:694
  87.1 5.7 %all-to-all-done = bf16[4,928,768]{2,1,0:T(8,128)(2,1)} async-done(((bf16[4,928,768]{2,1,0:T(8,128)(2,1)}), bf16[4,928,768]{2,1,0:T(8,128)(2,1)}, u32[]{:S(2)}, u32[]{:S(2)}) %all-to-all-start) | async-done | bytes 5701664 | tf_op jit(solution)/shard_map/all_to_all | solution.py:1051
  92.8 136.8 %shard_map.309 = (bf16[4,4,232,768]{3,2,1,0:T(8,128)(2,1)}, f32[4096,768]{1,0:T(8,128)}, bf16[4096,768]{1,0:T(8,128)(2,1)}, bf16[8,432,768]{2,1,0:T(8,128)(2,1)}...) custom-call(s32[128]{0:T(128)} %get-tuple-element.67.meta, ...), custom_call_target="tpu_custom_call" | custom-call | flops 109999996928 | bytes 11000000 | tf_op jit(solution)/shard_map/pallas_call | solution.py:751
  229.6 9.5 %shard_map.310.rest_0_ = bf16[4096,2304]{1,0:T(8,128)(2,1)} custom-call(s32[128]{0:T(128)} %get-tuple-element.67.meta, f32[16]{0:T(128)} %multiply_exponential_fusion.slopes, bf16[4096,2304]{1,0:T(8,128)(2,1)} %get-tuple-element.55.qkv, bf16[4096,768]{1,0:T(8,128)(2,1)} %get-tuple-element.56.att_grad, f32[16,6,8,256]{3,2,1,0:T(8,128)} %get-tuple-element.57.totals, ...), custom_call_target="tpu_custom_call" | custom-call | flops 15000000512 | bytes 1500000 | tf_op jit(solution)/shard_map/pallas_call | solution.py:827
  239.2 7.8 %add_convert_fusion = bf16[8,432,768]{2,1,0:T(8,128)(2,1)} fusion(bf16[8,432,768]{2,1,0:T(8,128)(2,1)} %collective-permute-done.3, bf16[8,432,768]{2,1,0:T(8,128)(2,1)} %get-tuple-element.58), kind=kLoop, calls=%fused_computation | loop fusion | flops 10616832 | bytes 15925248 | tf_op jit(solution)/shard_map/convert_element_type | solution.py:950
  247.1 5.3 %all-to-all-start.1 = ((bf16[4,928,768]{2,1,0:T(8,128)(2,1)}), bf16[4,928,768]{2,1,0:T(8,128)(2,1)}, u32[]{:S(2)}, u32[]{:S(2)}) async-start(bf16[4,928,768]{2,1,0:T(8,128)(2,1)} %bitcast.23), calls=%async_computation.1 | async-start | bytes 11403264 | tf_op jit(solution)/shard_map/all_to_all | solution.py:1051
  252.4 33.1 %shard_map.311.packed_grad = bf16[4096,2304]{1,0:T(8,128)(2,1)} custom-call(s32[128]{0:T(128)} %get-tuple-element.67.meta, f32[16]{0:T(128)} %multiply_exponential_fusion.slopes, bf16[4096,2304]{1,0:T(8,128)(2,1)} %get-tuple-element.55.qkv, bf16[4096,768]{1,0:T(8,128)(2,1)} %get-tuple-element.56.att_grad, ...), custom_call_target="tpu_custom_call", output_to_operand_aliasing={{}: (7, {})} | custom-call | flops 499999997952 | bytes 50000000 | tf_op jit(solution)/shard_map/pallas_call | solution.py:827
  285.5 19.1 %shard_map.312 = (bf16[8,144,768]{2,1,0:T(8,128)(2,1)}, bf16[8,144,768]{2,1,0:T(8,128)(2,1)}, f32[8,2304]{1,0:T(8,128)}) custom-call(s32[128]{0:T(128)} %get-tuple-element.67.meta, bf16[4096,2304]{1,0:T(8,128)(2,1)} %shard_map.311.packed_grad, bf16[4096,768]{1,0:T(8,128)(2,1)} %get-tuple-element.53.tokens_in.tokens, f32[16,768]{1,0:T(8,128)} %get-tuple-element.51.vecs), custom_call_target="tpu_custom_call" | custom-call | flops 15000000512 | bytes 1500000 | tf_op jit(solution)/shard_map/pallas_call | solution.py:865
  304.8 3.8 collective-permute-done.4
  308.6 1.9 add_convert_fusion.1
  310.6 0.1 dynamic-slice_bitcast_fusion.1
  310.8 6.0 %all-to-all-done.1 = bf16[4,928,768]{2,1,0:T(8,128)(2,1)} async-done(((bf16[4,928,768]{2,1,0:T(8,128)(2,1)}), bf16[4,928,768]{2,1,0:T(8,128)(2,1)}, u32[]{:S(2)}, u32[]{:S(2)}) %all-to-all-start.1) | async-done | bytes 5701664 | tf_op jit(solution)/shard_map/all_to_all | solution.py:1051
  316.8 7.0 %shard_map.313 = bf16[4,225,4,768]{3,2,1,0:T(4,128)(2,1)} custom-call(s32[16]{0:T(128)} %get-tuple-element.62.take, bf16[4,4,232,768]{3,2,1,0:T(8,128)(2,1)} %bitcast.6.got), custom_call_target="tpu_custom_call" | custom-call | tf_op jit(solution)/shard_map/pallas_call | solution.py:675
  323.8 23.1 %shard_map.314 = (f32[4,225,4,768]{3,2,1,0:T(4,128)}, f32[16,768]{1,0:T(8,128)}) custom-call(s32[128]{0:T(128)} %get-tuple-element.67.meta, bf16[4096,2304]{1,0:T(8,128)(2,1)} %shard_map.311.packed_grad, bf16[4096,768]{1,0:T(8,128)(2,1)} %get-tuple-element.53.tokens_in.tokens, f32[4096,768]{1,0:T(8,128)} %get-tuple-element.68.mid_grad, ...), custom_call_target="tpu_custom_call" | custom-call | flops 20000000000 | bytes 2000000 | tf_op jit(solution)/shard_map/pallas_call | solution.py:901
  346.9 0.2 add_convert_fusion.2
  347.3 0.4 copy-done.1
  347.7 1.2 collective-permute-done.5
  348.9 18.0 %collective-permute-start.6 = (f32[16,768]{1,0:T(8,128)S(1)}, f32[16,768]{1,0:T(8,128)S(1)}, u32[]{:S(2)}, u32[]{:S(2)}) collective-permute-start(f32[16,768]{1,0:T(8,128)S(1)} %add.90), channel_id=1, source_target_pairs={{0,2},{1,3},{2,0},{3,1},{4,6},{5,7},{6,4},{7,5},{8,10},{9,11},{10,... | collective-permute-start | bytes 147464 | tf_op jit(solution)/shard_map/ppermute | solution.py:942
  366.9 2.3 collective-permute-done.6
  369.3 6.8 %collective-permute-start.7 = (f32[16,768]{1,0:T(8,128)S(1)}, f32[16,768]{1,0:T(8,128)S(1)}, u32[]{:S(2)}, u32[]{:S(2)}) collective-permute-start(f32[16,768]{1,0:T(8,128)S(1)} %add.91), channel_id=1, source_target_pairs={{0,4},{4,0},{8,12},{12,8},{16,20},{20,16},{24,28},{28,24},{1,5},{5... | collective-permute-start | bytes 147464 | tf_op jit(solution)/shard_map/ppermute | solution.py:942
  376.0 2.1 collective-permute-done.7
  378.1 0.1 add_convert_fusion.4
  378.4 0.5 collective-permute-start.10
  378.9 4.9 %collective-permute-done.10 = f32[16,768]{1,0:T(8,128)S(1)} collective-permute-done((f32[16,768]{1,0:T(8,128)S(1)}, f32[16,768]{1,0:T(8,128)S(1)}, u32[]{:S(2)}, u32[]{:S(2)}) %collective-permute-start.10) | collective-permute-done | bytes 49184 | tf_op jit(solution)/shard_map/ppermute | solution.py:942
  383.8 8.4 %collective-permute-start.15 = (bf16[432,768]{1,0:T(8,128)(2,1)}, bf16[432,768]{1,0:T(8,128)(2,1)S(1)}, u32[]{:S(2)}, u32[]{:S(2)}) collective-permute-start(bf16[432,768]{1,0:T(8,128)(2,1)} %bitcast.28), channel_id=1, source_target_pairs={{0,2},{1,3},{2,0},{3,1},{4,6},{5,7},{6,4},{7,5},{8,10},{9,11},{10,... | collective-permute-start | bytes 1990664 | tf_op jit(solution)/shard_map/ppermute | solution.py:942
  392.3 6.0 %collective-permute-start.13 = (bf16[144,768]{1,0:T(8,128)(2,1)S(1)}, bf16[144,768]{1,0:T(8,128)(2,1)S(1)}, u32[]{:S(2)}, u32[]{:S(2)}) collective-permute-start(bf16[144,768]{1,0:T(8,128)(2,1)S(1)} %fusion), channel_id=1, source_target_pairs={{0,2},{1,3},{2,0},{3,1},{4,6},{5,7},{6,4},{7,5},{8,10},{9,11},{10,... | collective-permute-start | bytes 663560 | tf_op jit(solution)/shard_map/ppermute | solution.py:942
  398.3 5.0 %collective-permute-done.12 = f32[16,768]{1,0:T(8,128)S(1)} collective-permute-done((f32[16,768]{1,0:T(8,128)S(1)}, f32[16,768]{1,0:T(8,128)S(1)}, u32[]{:S(2)}, u32[]{:S(2)}) %collective-permute-start.12) | collective-permute-done | bytes 49184 | tf_op jit(solution)/shard_map/ppermute | solution.py:942
  403.3 0.6 reshape.70
  403.9 0.7 slice_reduce_fusion
  404.6 7.3 %collective-permute-done.13 = bf16[144,768]{1,0:T(8,128)(2,1)S(1)} collective-permute-done((bf16[144,768]{1,0:T(8,128)(2,1)S(1)}, bf16[144,768]{1,0:T(8,128)(2,1)S(1)}, u32[]{:S(2)}, u32[]{:S(2)}) %collective-permute-start.13) | collective-permute-done | bytes 221216 | tf_op jit(solution)/shard_map/ppermute | solution.py:942
  412.0 0.2 add_convert_fusion.3
  412.2 0.5 collective-permute-start.16
  412.7 0.7 collective-permute-done.14
  413.5 1.0 maximum_convert_fusion.2
  414.5 0.1 broadcast_select_fusion.1
  414.7 0.1 fusion.1
  414.8 0.7 maximum_convert_fusion.3
  415.5 1.1 maximum_convert_fusion
  416.6 1.1 maximum_convert_fusion.1
  (41 shorter events, 0.9 us)
Async XLA Ops:
  7.2 4.5 %collective-permute-start = (s32[4,4]{1,0:T(4,128)}, s32[4,4]{1,0:T(4,128)S(1)}, u32[]{:S(2)}, u32[]{:S(2)}) collective-permute-start(s32[4,4]{1,0:T(4,128)} %slots.1), channel_id=1, source_target_pairs={{0,1},{1,2},{2,3},{3,0},{4,5},{5,6},{6,7},{7,4},{8,9},{9,10},{10,1... | collective-permute-start | bytes 200 | tf_op jit(solution)/shard_map/ppermute | solution.py:1058
  7.7 4.3 %collective-permute-start.1 = (s32[4,4]{1,0:T(4,128)}, s32[4,4]{1,0:T(4,128)S(1)}, u32[]{:S(2)}, u32[]{:S(2)}) collective-permute-start(s32[4,4]{1,0:T(4,128)} %slots.1), channel_id=1, source_target_pairs={{0,2},{1,3},{2,0},{3,1},{4,6},{5,7},{6,4},{7,5},{8,10},{9,11},{10,... | collective-permute-start | bytes 200 | tf_op jit(solution)/shard_map/ppermute | solution.py:1058
  10.3 2.9 collective-permute-start.2
  11.6 1.5 copy-start.2
  12.0 1.1 copy-start.3
  13.2 0.6 copy-start.4
  23.3 69.5 %all-to-all-start = ((bf16[4,928,768]{2,1,0:T(8,128)(2,1)}), bf16[4,928,768]{2,1,0:T(8,128)(2,1)}, u32[]{:S(2)}, u32[]{:S(2)}) async-start(bf16[4,928,768]{2,1,0:T(8,128)(2,1)} %bitcast.24), calls=%async_computation | async-start | bytes 11403264 | tf_op jit(solution)/shard_map/all_to_all | solution.py:1051
  28.4 355.3 %reduce-scatter.2.cloned.1.call-start = ((), (), s32[]{:S(2)}) async-start(), calls=%async_computation.3 | async-start | bytes 5971968 | tf_op jit(solution)/shard_map/reduce_scatter | solution.py:1086
  229.6 9.6 %collective-permute-start.3 = (bf16[8,432,768]{2,1,0:T(8,128)(2,1)}, bf16[8,432,768]{2,1,0:T(8,128)(2,1)}, u32[]{:S(2)}, u32[]{:S(2)}) collective-permute-start(bf16[8,432,768]{2,1,0:T(8,128)(2,1)} %get-tuple-element.59), channel_id=1, source_target_pairs={{0,1},{1,0},{2,3},{3,2},{4,5},{5,4},{6,7},{7,6},{8,9},{9,8},{10,11... | collective-permute-start | bytes 15925256 | tf_op jit(solution)/shard_map/ppermute | solution.py:942
  247.1 69.7 %all-to-all-start.1 = ((bf16[4,928,768]{2,1,0:T(8,128)(2,1)}), bf16[4,928,768]{2,1,0:T(8,128)(2,1)}, u32[]{:S(2)}, u32[]{:S(2)}) async-start(bf16[4,928,768]{2,1,0:T(8,128)(2,1)} %bitcast.23), calls=%async_computation.1 | async-start | bytes 11403264 | tf_op jit(solution)/shard_map/all_to_all | solution.py:1051
  304.7 4.0 collective-permute-start.4
  310.7 36.2 %collective-permute-start.8 = (bf16[4,144,768]{2,1,0:T(8,128)(2,1)S(1)}, bf16[4,144,768]{2,1,0:T(8,128)(2,1)S(1)}, u32[]{:S(2)}, u32[]{:S(2)}) collective-permute-start(bf16[4,144,768]{2,1,0:T(8,128)(2,1)S(1)} %get-tuple-element.90), channel_id=1, source_target_pairs={{0,4},{4,0},{8,12},{12,8},{16,20},{20,16},{24,28},{28,24},{1,5},{5... | collective-permute-start | bytes 2654216 | tf_op jit(solution)/shard_map/ppermute | solution.py:942
  346.9 0.8 copy-start.1
  347.2 30.9 %collective-permute-start.9 = (bf16[2,144,768]{2,1,0:T(8,128)(2,1)S(1)}, bf16[2,144,768]{2,1,0:T(8,128)(2,1)S(1)}, u32[]{:S(2)}, u32[]{:S(2)}) collective-permute-start(bf16[2,144,768]{2,1,0:T(8,128)(2,1)S(1)} %get-tuple-element.94), channel_id=1, source_target_pairs={{0,8},{4,12},{8,0},{12,4},{16,24},{20,28},{24,16},{28,20},{1,9},{5... | collective-permute-start | bytes 1327112 | tf_op jit(solution)/shard_map/ppermute | solution.py:942
  347.7 1.2 collective-permute-start.5
  348.9 20.3 %collective-permute-start.6 = (f32[16,768]{1,0:T(8,128)S(1)}, f32[16,768]{1,0:T(8,128)S(1)}, u32[]{:S(2)}, u32[]{:S(2)}) collective-permute-start(f32[16,768]{1,0:T(8,128)S(1)} %add.90), channel_id=1, source_target_pairs={{0,2},{1,3},{2,0},{3,1},{4,6},{5,7},{6,4},{7,5},{8,10},{9,11},{10,... | collective-permute-start | bytes 147464 | tf_op jit(solution)/shard_map/ppermute | solution.py:942
  369.3 8.8 %collective-permute-start.7 = (f32[16,768]{1,0:T(8,128)S(1)}, f32[16,768]{1,0:T(8,128)S(1)}, u32[]{:S(2)}, u32[]{:S(2)}) collective-permute-start(f32[16,768]{1,0:T(8,128)S(1)} %add.91), channel_id=1, source_target_pairs={{0,4},{4,0},{8,12},{12,8},{16,20},{20,16},{24,28},{28,24},{1,5},{5... | collective-permute-start | bytes 147464 | tf_op jit(solution)/shard_map/ppermute | solution.py:942
  378.3 13.9 %collective-permute-start.11 = (bf16[1,144,768]{2,1,0:T(8,128)(2,1)S(1)}, bf16[1,144,768]{2,1,0:T(8,128)(2,1)S(1)}, u32[]{:S(2)}, u32[]{:S(2)}) collective-permute-start(bf16[1,144,768]{2,1,0:T(8,128)(2,1)S(1)} %get-tuple-element.106), channel_id=1, source_target_pairs={{0,16},{4,20},{8,24},{12,28},{16,0},{20,4},{24,8},{28,12},{1,17},{... | collective-permute-start | bytes 663560 | tf_op jit(solution)/shard_map/ppermute | solution.py:942
  378.4 5.4 %collective-permute-start.10 = (f32[16,768]{1,0:T(8,128)S(1)}, f32[16,768]{1,0:T(8,128)S(1)}, u32[]{:S(2)}, u32[]{:S(2)}) collective-permute-start(f32[16,768]{1,0:T(8,128)S(1)} %add.92), channel_id=1, source_target_pairs={{0,8},{4,12},{8,0},{12,4},{16,24},{20,28},{24,16},{28,20},{1,9},{5... | collective-permute-start | bytes 147464 | tf_op jit(solution)/shard_map/ppermute | solution.py:942
  383.8 28.2 %copy-start = (bf16[1,432,768]{2,1,0:T(8,128)(2,1)S(1)}, bf16[1,432,768]{2,1,0:T(8,128)(2,1)}, u32[]{:S(2)}) copy-start(bf16[1,432,768]{2,1,0:T(8,128)(2,1)} %reduce-scatter.2.cloned.1.call-done) | copy-start | bytes 1990660
  383.8 28.2 %collective-permute-start.15 = (bf16[432,768]{1,0:T(8,128)(2,1)}, bf16[432,768]{1,0:T(8,128)(2,1)S(1)}, u32[]{:S(2)}, u32[]{:S(2)}) collective-permute-start(bf16[432,768]{1,0:T(8,128)(2,1)} %bitcast.28), channel_id=1, source_target_pairs={{0,2},{1,3},{2,0},{3,1},{4,6},{5,7},{6,4},{7,5},{8,10},{9,11},{10,... | collective-permute-start | bytes 1990664 | tf_op jit(solution)/shard_map/ppermute | solution.py:942
  392.3 19.6 %collective-permute-start.13 = (bf16[144,768]{1,0:T(8,128)(2,1)S(1)}, bf16[144,768]{1,0:T(8,128)(2,1)S(1)}, u32[]{:S(2)}, u32[]{:S(2)}) collective-permute-start(bf16[144,768]{1,0:T(8,128)(2,1)S(1)} %fusion), channel_id=1, source_target_pairs={{0,2},{1,3},{2,0},{3,1},{4,6},{5,7},{6,4},{7,5},{8,10},{9,11},{10,... | collective-permute-start | bytes 663560 | tf_op jit(solution)/shard_map/ppermute | solution.py:942
  398.3 5.0 %collective-permute-start.12 = (f32[16,768]{1,0:T(8,128)S(1)}, f32[16,768]{1,0:T(8,128)S(1)}, u32[]{:S(2)}, u32[]{:S(2)}) collective-permute-start(f32[16,768]{1,0:T(8,128)S(1)} %add.101), channel_id=1, source_target_pairs={{0,16},{4,20},{8,24},{12,28},{16,0},{20,4},{24,8},{28,12},{1,17},{... | collective-permute-start | bytes 147464 | tf_op jit(solution)/shard_map/ppermute | solution.py:942
  411.9 1.5 collective-permute-start.14
  412.2 2.3 collective-permute-start.16
Sparse Core Ops, SparseCore 0:
  247.2 133.0 reduce-scatter.1

commit v4 on v3

--- a/solution.py
+++ b/solution.py
@@ -1107,9 +1107,9 @@
             vectors = doubled(vectors, n)
         block = added(after(keep, vectors), crossing)
         keep, crossing = start_fold(block, 4)
-        vectors = doubled(after(vectors, block), rounds - 2)
         across_two = swap(share_two, "bal", 2)
-        block = added(after(keep, vectors, share_two), crossing).reshape(sum_one.shape[-2:])
+        vectors = doubled(after(vectors, block, share_two), rounds - 2)
+        block = added(after(keep, vectors), crossing).reshape(sum_one.shape[-2:])
         across_one = swap(block, "bal", 2)
         vectors = doubled(after(vectors, block), rounds - 1)
         full_one = added(after(block, vectors), across_one)

time: 426 us -> 415 us (0.974)
  Pallas kernels: 296 us -> 250 us
  starting transfers between devices: 55.7 us -> 78.4 us
  waiting for transfers between devices: 40.5 us -> 54.8 us
    pallas_call x1, Pallas kernels: 137 us -> 114 us  [mlp(): pl.pallas_call(functools.partial(mlp_kernel, CHUNK, length), out_shape=(j...]
    ppermute x14, starting transfers between devices: 40.7 us -> 63.4 us  [swap(): return lax.ppermute(block, axis, [(n, n ^ bit) for n in range(size)])]
    ppermute x14, waiting for transfers between devices: 27.3 us -> 43.5 us  [swap(): return lax.ppermute(block, axis, [(n, n ^ bit) for n in range(size)])]
    pallas_call x2, Pallas kernels: 42.7 us -> 31.8 us  [attend_back(): pl.pallas_call(functools.partial(attend_back_kernel, first, per), out_sha...]
    pallas_call x1, Pallas kernels: 19.1 us -> 14.7 us  [qkv_grad(): pl.pallas_call(qkv_grad_kernel, out_shape=(jax.ShapeDtypeStruct((BLOCKS,...]
    pallas_call x1, Pallas kernels: 23.1 us -> 18.7 us  [token_grad(): pl.pallas_call(token_grad_kernel, out_shape=(jax.ShapeDtypeStruct((steps,...]
  transfers between devices with their start and end apart: 20 -> 20, of which waited for: 12 -> 14; matrix products, arithmetic and copies ran while one was open for 1% -> 1% of each run, Pallas kernels for 35% -> 30%
where the time goes in v4:
time: 415 us
  Pallas kernels  250 us (60%)
  starting transfers between devices  78.4 us (19%)
  waiting for transfers between devices  54.8 us (13%)
  other arithmetic  15 us (4%)
  between operations  14.5 us (3%)
    pallas_call x1, Pallas kernels, mlp(): pl.pallas_call(functools.partial(mlp_kernel, CHUNK, length), out_shape=(j...  114 us
    ppermute x14, starting transfers between devices, swap(): return lax.ppermute(block, axis, [(n, n ^ bit) for n in range(size)])  63.4 us
    pallas_call x1, Pallas kernels, first_half(): pl.pallas_call(attend_kernel, out_shape=(jax.ShapeDtypeStruct((total, wid...  54.1 us
    ppermute x14, waiting for transfers between devices, swap(): return lax.ppermute(block, axis, [(n, n ^ bit) for n in range(size)])  43.5 us
    pallas_call x2, Pallas kernels, attend_back(): pl.pallas_call(functools.partial(attend_back_kernel, first, per), out_sha...  31.8 us
    pallas_call x1, Pallas kernels, token_grad(): pl.pallas_call(token_grad_kernel, out_shape=(jax.ShapeDtypeStruct((steps,...  18.7 us
    pallas_call x1, Pallas kernels, qkv_grad(): pl.pallas_call(qkv_grad_kernel, out_shape=(jax.ShapeDtypeStruct((BLOCKS,...  14.7 us
    all_to_all x2, starting transfers between devices, exchange(): return lax.all_to_all(flat, 'bal', split_axis=0, concat_axis=0, tiled=True)  10.5 us
  transfers between devices with their start and end apart: 20, of which 14 were waited for; matrix products, arithmetic and copies ran while one was open for 1% of the time, Pallas kernels for 30%

profile of v4, /device:TPU:0, one launch (start us, length us, event | category | flops | bytes accessed | tf_op | source)
XLA Modules:
  0.0 415.3 jit_solution(17504050816979844838)
XLA Ops:
  7.2 0.5 collective-permute-start
  7.7 2.6 collective-permute-start.1
  10.3 1.4 collective-permute-start.2
  12.0 1.1 collective-permute-done.2.rest_2_
  13.2 0.6 copy-done.4
  13.7 9.6 %shard_map.307 = (s32[128]{0:T(128)}, s32[16]{0:T(128)}, f32[16,768]{1,0:T(8,128)}, bf16[4,4,232,768]{3,2,1,0:T(8,128)(2,1)}) custom-call(s32[4,4]{1,0:T(4,128)} %counts.1, s32[4,4]{1,0:T(4,128)} %present.1, s32[4,4]{1,0:T(4,128)} %slots.1, s32[1]{0:T(128)} %bitcast.me, bf16[4,225,4,768]{3,2,1,0:T(4,128)(2,1)} %bitcast.26, s32[4,4]{1,0:T(4,128)} %copy-done.2, ...), custom_call_target="tpu_custom_call" | custom-call | tf_op jit(solution)/shard_map/pallas_call | solution.py:650
  23.3 5.1 %all-to-all-start = ((bf16[4,928,768]{2,1,0:T(8,128)(2,1)}), bf16[4,928,768]{2,1,0:T(8,128)(2,1)}, u32[]{:S(2)}, u32[]{:S(2)}) async-start(bf16[4,928,768]{2,1,0:T(8,128)(2,1)} %bitcast.24), calls=%async_computation | async-start | bytes 11403264 | tf_op jit(solution)/shard_map/all_to_all | solution.py:1051
  28.5 0.5 multiply_exponential_fusion.slopes
  29.0 54.1 %shard_map.308 = (bf16[4096,768]{1,0:T(8,128)(2,1)}, bf16[4096,2304]{1,0:T(8,128)(2,1)}, bf16[4096,768]{1,0:T(8,128)(2,1)}, f32[16,6,8,256]{3,2,1,0:T(8,128)}) custom-call(s32[128]{0:T(128)} %get-tuple-element.67.meta, f32[16]{0:T(128)} %multiply_exponential_fusion.slopes, bf16[4,225,4,768]{3,2,1,0:T(4,128)(2,1)} %bitcast.30, s32[4,4,225]{2,1,0:T(4,128)} %rows_in.5, ...), custom_call_target="tpu_custom_call" | custom-call | flops 40000000000 | bytes 4000000 | tf_op jit(solution)/shard_map/pallas_call | solution.py:694
  83.1 9.7 %all-to-all-done = bf16[4,928,768]{2,1,0:T(8,128)(2,1)} async-done(((bf16[4,928,768]{2,1,0:T(8,128)(2,1)}), bf16[4,928,768]{2,1,0:T(8,128)(2,1)}, u32[]{:S(2)}, u32[]{:S(2)}) %all-to-all-start) | async-done | bytes 5701664 | tf_op jit(solution)/shard_map/all_to_all | solution.py:1051
  92.8 114.0 %shard_map.309 = (bf16[4,4,232,768]{3,2,1,0:T(8,128)(2,1)}, f32[4096,768]{1,0:T(8,128)}, bf16[4096,768]{1,0:T(8,128)(2,1)}, bf16[8,432,768]{2,1,0:T(8,128)(2,1)}...) custom-call(s32[128]{0:T(128)} %get-tuple-element.67.meta, ...), custom_call_target="tpu_custom_call" | custom-call | flops 109999996928 | bytes 11000000 | tf_op jit(solution)/shard_map/pallas_call | solution.py:751
  206.8 17.8 %collective-permute-start.3 = (bf16[8,432,768]{2,1,0:T(8,128)(2,1)}, bf16[8,432,768]{2,1,0:T(8,128)(2,1)}, u32[]{:S(2)}, u32[]{:S(2)}) collective-permute-start(bf16[8,432,768]{2,1,0:T(8,128)(2,1)} %get-tuple-element.59), channel_id=1, source_target_pairs={{0,1},{1,0},{2,3},{3,2},{4,5},{5,4},{6,7},{7,6},{8,9},{9,8},{10,11... | collective-permute-start | bytes 15925256 | tf_op jit(solution)/shard_map/ppermute | solution.py:942
  224.6 7.9 %shard_map.310.rest_0_ = bf16[4096,2304]{1,0:T(8,128)(2,1)} custom-call(s32[128]{0:T(128)} %get-tuple-element.67.meta, f32[16]{0:T(128)} %multiply_exponential_fusion.slopes, bf16[4096,2304]{1,0:T(8,128)(2,1)} %get-tuple-element.55.qkv, bf16[4096,768]{1,0:T(8,128)(2,1)} %get-tuple-element.56.att_grad, f32[16,6,8,256]{3,2,1,0:T(8,128)} %get-tuple-element.57.totals, ...), custom_call_target="tpu_custom_call" | custom-call | flops 15000000512 | bytes 1500000 | tf_op jit(solution)/shard_map/pallas_call | solution.py:827
  232.5 0.8 collective-permute-done.3
  233.3 7.8 %add_convert_fusion = bf16[8,432,768]{2,1,0:T(8,128)(2,1)} fusion(bf16[8,432,768]{2,1,0:T(8,128)(2,1)} %collective-permute-done.3, bf16[8,432,768]{2,1,0:T(8,128)(2,1)} %get-tuple-element.58), kind=kLoop, calls=%fused_computation | loop fusion | flops 10616832 | bytes 15925248 | tf_op jit(solution)/shard_map/convert_element_type | solution.py:950
  241.2 5.3 %all-to-all-start.1 = ((bf16[4,928,768]{2,1,0:T(8,128)(2,1)}), bf16[4,928,768]{2,1,0:T(8,128)(2,1)}, u32[]{:S(2)}, u32[]{:S(2)}) async-start(bf16[4,928,768]{2,1,0:T(8,128)(2,1)} %bitcast.23), calls=%async_computation.1 | async-start | bytes 11403264 | tf_op jit(solution)/shard_map/all_to_all | solution.py:1051
  246.5 23.9 %shard_map.311.packed_grad = bf16[4096,2304]{1,0:T(8,128)(2,1)} custom-call(s32[128]{0:T(128)} %get-tuple-element.67.meta, f32[16]{0:T(128)} %multiply_exponential_fusion.slopes, bf16[4096,2304]{1,0:T(8,128)(2,1)} %get-tuple-element.55.qkv, bf16[4096,768]{1,0:T(8,128)(2,1)} %get-tuple-element.56.att_grad, ...), custom_call_target="tpu_custom_call", output_to_operand_aliasing={{}: (7, {})} | custom-call | flops 499999997952 | bytes 50000000 | tf_op jit(solution)/shard_map/pallas_call | solution.py:827
  270.4 14.7 %shard_map.312 = (bf16[8,144,768]{2,1,0:T(8,128)(2,1)}, bf16[8,144,768]{2,1,0:T(8,128)(2,1)}, f32[8,2304]{1,0:T(8,128)}) custom-call(s32[128]{0:T(128)} %get-tuple-element.67.meta, bf16[4096,2304]{1,0:T(8,128)(2,1)} %shard_map.311.packed_grad, bf16[4096,768]{1,0:T(8,128)(2,1)} %get-tuple-element.53.tokens_in.tokens, f32[16,768]{1,0:T(8,128)} %get-tuple-element.51.vecs), custom_call_target="tpu_custom_call" | custom-call | flops 15000000512 | bytes 1500000 | tf_op jit(solution)/shard_map/pallas_call | solution.py:865
  285.2 16.5 %collective-permute-start.4 = (bf16[8,144,768]{2,1,0:T(8,128)(2,1)}, bf16[8,144,768]{2,1,0:T(8,128)(2,1)S(1)}, u32[]{:S(2)}, u32[]{:S(2)}) collective-permute-start(bf16[8,144,768]{2,1,0:T(8,128)(2,1)} %get-tuple-element.66), channel_id=1, source_target_pairs={{0,1},{1,0},{2,3},{3,2},{4,5},{5,4},{6,7},{7,6},{8,9},{9,8},{10,11... | collective-permute-start | bytes 5308424 | tf_op jit(solution)/shard_map/ppermute | solution.py:942
  301.6 3.5 collective-permute-done.4
  305.2 2.0 add_convert_fusion.1
  307.3 14.2 %collective-permute-start.8 = (bf16[4,144,768]{2,1,0:T(8,128)(2,1)S(1)}, bf16[4,144,768]{2,1,0:T(8,128)(2,1)S(1)}, u32[]{:S(2)}, u32[]{:S(2)}) collective-permute-start(bf16[4,144,768]{2,1,0:T(8,128)(2,1)S(1)} %get-tuple-element.90), channel_id=1, source_target_pairs={{0,4},{4,0},{8,12},{12,8},{16,20},{20,16},{24,28},{28,24},{1,5},{5... | collective-permute-start | bytes 2654216 | tf_op jit(solution)/shard_map/ppermute | solution.py:942
  321.5 7.0 %shard_map.313 = bf16[4,225,4,768]{3,2,1,0:T(4,128)(2,1)} custom-call(s32[16]{0:T(128)} %get-tuple-element.62.take, bf16[4,4,232,768]{3,2,1,0:T(8,128)(2,1)} %bitcast.6.got), custom_call_target="tpu_custom_call" | custom-call | tf_op jit(solution)/shard_map/pallas_call | solution.py:675
  328.5 18.7 %shard_map.314 = (f32[4,225,4,768]{3,2,1,0:T(4,128)}, f32[16,768]{1,0:T(8,128)}) custom-call(s32[128]{0:T(128)} %get-tuple-element.67.meta, bf16[4096,2304]{1,0:T(8,128)(2,1)} %shard_map.311.packed_grad, bf16[4096,768]{1,0:T(8,128)(2,1)} %get-tuple-element.53.tokens_in.tokens, f32[4096,768]{1,0:T(8,128)} %get-tuple-element.68.mid_grad, ...), custom_call_target="tpu_custom_call" | custom-call | flops 20000000000 | bytes 2000000 | tf_op jit(solution)/shard_map/pallas_call | solution.py:901
  347.6 0.4 copy-done.1
  348.0 4.4 %collective-permute-start.5 = (f32[16,768]{1,0:T(8,128)S(1)}, f32[16,768]{1,0:T(8,128)S(1)}, u32[]{:S(2)}, u32[]{:S(2)}) collective-permute-start(f32[16,768]{1,0:T(8,128)S(1)} %copy-done.1), channel_id=1, source_target_pairs={{0,1},{1,0},{2,3},{3,2},{4,5},{5,4},{6,7},{7,6},{8,9},{9,8},{10,11... | collective-permute-start | bytes 147464 | tf_op jit(solution)/shard_map/ppermute | solution.py:942
  352.5 0.9 collective-permute-done.5
  353.3 1.6 collective-permute-start.6
  355.0 2.5 collective-permute-done.6
  357.4 2.0 collective-permute-start.7
  359.4 2.2 collective-permute-done.7
  361.6 15.9 %collective-permute-done.9 = bf16[2,144,768]{2,1,0:T(8,128)(2,1)S(1)} collective-permute-done((bf16[2,144,768]{2,1,0:T(8,128)(2,1)S(1)}, bf16[2,144,768]{2,1,0:T(8,128)(2,1)S(1)}, u32[]{:S(2)}, u32[]{:S(2)}) %collective-permute-start.9) | collective-permute-done | bytes 442400 | tf_op jit(solution)/shard_map/ppermute | solution.py:942
  377.7 1.0 collective-permute-start.11
  378.7 2.5 collective-permute-start.10
  381.2 1.3 collective-permute-start.15
  382.5 2.1 collective-permute-done.10
  384.6 6.3 %collective-permute-done.11 = bf16[1,144,768]{2,1,0:T(8,128)(2,1)S(1)} collective-permute-done((bf16[1,144,768]{2,1,0:T(8,128)(2,1)S(1)}, bf16[1,144,768]{2,1,0:T(8,128)(2,1)S(1)}, u32[]{:S(2)}, u32[]{:S(2)}) %collective-permute-start.11) | collective-permute-done | bytes 221216 | tf_op jit(solution)/shard_map/ppermute | solution.py:942
  390.9 1.5 collective-permute-start.13
  392.5 5.0 %collective-permute-done.12 = f32[16,768]{1,0:T(8,128)S(1)} collective-permute-done((f32[16,768]{1,0:T(8,128)S(1)}, f32[16,768]{1,0:T(8,128)S(1)}, u32[]{:S(2)}, u32[]{:S(2)}) %collective-permute-start.12) | collective-permute-done | bytes 49184 | tf_op jit(solution)/shard_map/ppermute | solution.py:942
  397.5 0.6 reshape.70
  398.1 0.7 slice_reduce_fusion
  398.7 3.6 collective-permute-done.13
  402.7 0.5 collective-permute-start.16
  403.2 0.7 collective-permute-done.14
  404.0 1.0 maximum_convert_fusion.2
  405.2 0.7 maximum_convert_fusion.3
  406.0 1.1 maximum_convert_fusion
  407.1 1.1 maximum_convert_fusion.1
  (41 shorter events, 1.8 us)
Async XLA Ops:
  7.2 4.5 %collective-permute-start = (s32[4,4]{1,0:T(4,128)}, s32[4,4]{1,0:T(4,128)S(1)}, u32[]{:S(2)}, u32[]{:S(2)}) collective-permute-start(s32[4,4]{1,0:T(4,128)} %slots.1), channel_id=1, source_target_pairs={{0,1},{1,2},{2,3},{3,0},{4,5},{5,6},{6,7},{7,4},{8,9},{9,10},{10,1... | collective-permute-start | bytes 200 | tf_op jit(solution)/shard_map/ppermute | solution.py:1058
  7.7 4.3 %collective-permute-start.1 = (s32[4,4]{1,0:T(4,128)}, s32[4,4]{1,0:T(4,128)S(1)}, u32[]{:S(2)}, u32[]{:S(2)}) collective-permute-start(s32[4,4]{1,0:T(4,128)} %slots.1), channel_id=1, source_target_pairs={{0,2},{1,3},{2,0},{3,1},{4,6},{5,7},{6,4},{7,5},{8,10},{9,11},{10,... | collective-permute-start | bytes 200 | tf_op jit(solution)/shard_map/ppermute | solution.py:1058
  10.3 2.9 collective-permute-start.2
  11.6 1.5 copy-start.2
  12.0 1.1 copy-start.3
  13.2 0.6 copy-start.4
  23.3 69.5 %all-to-all-start = ((bf16[4,928,768]{2,1,0:T(8,128)(2,1)}), bf16[4,928,768]{2,1,0:T(8,128)(2,1)}, u32[]{:S(2)}, u32[]{:S(2)}) async-start(bf16[4,928,768]{2,1,0:T(8,128)(2,1)} %bitcast.24), calls=%async_computation | async-start | bytes 11403264 | tf_op jit(solution)/shard_map/all_to_all | solution.py:1051
  28.4 350.2 %reduce-scatter.2.cloned.1.call-start = ((), (), s32[]{:S(2)}) async-start(), calls=%async_computation.3 | async-start | bytes 5971968 | tf_op jit(solution)/shard_map/reduce_scatter | solution.py:1086
  206.8 26.5 %collective-permute-start.3 = (bf16[8,432,768]{2,1,0:T(8,128)(2,1)}, bf16[8,432,768]{2,1,0:T(8,128)(2,1)}, u32[]{:S(2)}, u32[]{:S(2)}) collective-permute-start(bf16[8,432,768]{2,1,0:T(8,128)(2,1)} %get-tuple-element.59), channel_id=1, source_target_pairs={{0,1},{1,0},{2,3},{3,2},{4,5},{5,4},{6,7},{7,6},{8,9},{9,8},{10,11... | collective-permute-start | bytes 15925256 | tf_op jit(solution)/shard_map/ppermute | solution.py:942
  241.2 80.3 %all-to-all-start.1 = ((bf16[4,928,768]{2,1,0:T(8,128)(2,1)}), bf16[4,928,768]{2,1,0:T(8,128)(2,1)}, u32[]{:S(2)}, u32[]{:S(2)}) async-start(bf16[4,928,768]{2,1,0:T(8,128)(2,1)} %bitcast.23), calls=%async_computation.1 | async-start | bytes 11403264 | tf_op jit(solution)/shard_map/all_to_all | solution.py:1051
  285.2 20.0 %collective-permute-start.4 = (bf16[8,144,768]{2,1,0:T(8,128)(2,1)}, bf16[8,144,768]{2,1,0:T(8,128)(2,1)S(1)}, u32[]{:S(2)}, u32[]{:S(2)}) collective-permute-start(bf16[8,144,768]{2,1,0:T(8,128)(2,1)} %get-tuple-element.66), channel_id=1, source_target_pairs={{0,1},{1,0},{2,3},{3,2},{4,5},{5,4},{6,7},{7,6},{8,9},{9,8},{10,11... | collective-permute-start | bytes 5308424 | tf_op jit(solution)/shard_map/ppermute | solution.py:942
  307.3 40.0 %collective-permute-start.8 = (bf16[4,144,768]{2,1,0:T(8,128)(2,1)S(1)}, bf16[4,144,768]{2,1,0:T(8,128)(2,1)S(1)}, u32[]{:S(2)}, u32[]{:S(2)}) collective-permute-start(bf16[4,144,768]{2,1,0:T(8,128)(2,1)S(1)} %get-tuple-element.90), channel_id=1, source_target_pairs={{0,4},{4,0},{8,12},{12,8},{16,20},{20,16},{24,28},{28,24},{1,5},{5... | collective-permute-start | bytes 2654216 | tf_op jit(solution)/shard_map/ppermute | solution.py:942
  347.2 0.8 copy-start.1
  347.5 30.0 %collective-permute-start.9 = (bf16[2,144,768]{2,1,0:T(8,128)(2,1)S(1)}, bf16[2,144,768]{2,1,0:T(8,128)(2,1)S(1)}, u32[]{:S(2)}, u32[]{:S(2)}) collective-permute-start(bf16[2,144,768]{2,1,0:T(8,128)(2,1)S(1)} %get-tuple-element.94), channel_id=1, source_target_pairs={{0,8},{4,12},{8,0},{12,4},{16,24},{20,28},{24,16},{28,20},{1,9},{5... | collective-permute-start | bytes 1327112 | tf_op jit(solution)/shard_map/ppermute | solution.py:942
  348.0 5.3 %collective-permute-start.5 = (f32[16,768]{1,0:T(8,128)S(1)}, f32[16,768]{1,0:T(8,128)S(1)}, u32[]{:S(2)}, u32[]{:S(2)}) collective-permute-start(f32[16,768]{1,0:T(8,128)S(1)} %copy-done.1), channel_id=1, source_target_pairs={{0,1},{1,0},{2,3},{3,2},{4,5},{5,4},{6,7},{7,6},{8,9},{9,8},{10,11... | collective-permute-start | bytes 147464 | tf_op jit(solution)/shard_map/ppermute | solution.py:942
  353.3 4.1 collective-permute-start.6
  357.4 4.2 collective-permute-start.7
  377.7 13.2 %collective-permute-start.11 = (bf16[1,144,768]{2,1,0:T(8,128)(2,1)S(1)}, bf16[1,144,768]{2,1,0:T(8,128)(2,1)S(1)}, u32[]{:S(2)}, u32[]{:S(2)}) collective-permute-start(bf16[1,144,768]{2,1,0:T(8,128)(2,1)S(1)} %get-tuple-element.106), channel_id=1, source_target_pairs={{0,16},{4,20},{8,24},{12,28},{16,0},{20,4},{24,8},{28,12},{1,17},{... | collective-permute-start | bytes 663560 | tf_op jit(solution)/shard_map/ppermute | solution.py:942
  378.7 23.8 %copy-start = (bf16[1,432,768]{2,1,0:T(8,128)(2,1)S(1)}, bf16[1,432,768]{2,1,0:T(8,128)(2,1)}, u32[]{:S(2)}) copy-start(bf16[1,432,768]{2,1,0:T(8,128)(2,1)} %reduce-scatter.2.cloned.1.call-done) | copy-start | bytes 1990660
  378.7 5.9 %collective-permute-start.10 = (f32[16,768]{1,0:T(8,128)S(1)}, f32[16,768]{1,0:T(8,128)S(1)}, u32[]{:S(2)}, u32[]{:S(2)}) collective-permute-start(f32[16,768]{1,0:T(8,128)S(1)} %add.92), channel_id=1, source_target_pairs={{0,8},{4,12},{8,0},{12,4},{16,24},{20,28},{24,16},{28,20},{1,9},{5... | collective-permute-start | bytes 147464 | tf_op jit(solution)/shard_map/ppermute | solution.py:942
  381.2 21.3 %collective-permute-start.15 = (bf16[432,768]{1,0:T(8,128)(2,1)}, bf16[432,768]{1,0:T(8,128)(2,1)S(1)}, u32[]{:S(2)}, u32[]{:S(2)}) collective-permute-start(bf16[432,768]{1,0:T(8,128)(2,1)} %bitcast.28), channel_id=1, source_target_pairs={{0,2},{1,3},{2,0},{3,1},{4,6},{5,7},{6,4},{7,5},{8,10},{9,11},{10,... | collective-permute-start | bytes 1990664 | tf_op jit(solution)/shard_map/ppermute | solution.py:942
  390.9 11.4 %collective-permute-start.13 = (bf16[144,768]{1,0:T(8,128)(2,1)S(1)}, bf16[144,768]{1,0:T(8,128)(2,1)S(1)}, u32[]{:S(2)}, u32[]{:S(2)}) collective-permute-start(bf16[144,768]{1,0:T(8,128)(2,1)S(1)} %fusion), channel_id=1, source_target_pairs={{0,2},{1,3},{2,0},{3,1},{4,6},{5,7},{6,4},{7,5},{8,10},{9,11},{10,... | collective-permute-start | bytes 663560 | tf_op jit(solution)/shard_map/ppermute | solution.py:942
  392.4 5.0 %collective-permute-start.12 = (f32[16,768]{1,0:T(8,128)S(1)}, f32[16,768]{1,0:T(8,128)S(1)}, u32[]{:S(2)}, u32[]{:S(2)}) collective-permute-start(f32[16,768]{1,0:T(8,128)S(1)} %add.101), channel_id=1, source_target_pairs={{0,16},{4,20},{8,24},{12,28},{16,0},{20,4},{24,8},{28,12},{1,17},{... | collective-permute-start | bytes 147464 | tf_op jit(solution)/shard_map/ppermute | solution.py:942
  402.4 1.5 collective-permute-start.14
  402.7 2.3 collective-permute-start.16
Sparse Core Ops, SparseCore 0:
  241.3 136.6 reduce-scatter.1

commit v5 on v4

--- a/solution.py
+++ b/solution.py
@@ -937,6 +937,23 @@
     )
 
 
+def add_kernel(a, b, out):
+    out[...] = (a[...].astype(F32) + b[...].astype(F32)).astype(BF16)
+
+
+def added_parcels(a, b):
+    block = pl.BlockSpec((1,) + a.shape[1:], lambda n: (n, 0, 0))
+    return pl.pallas_call(
+        add_kernel,
+        out_shape=jax.ShapeDtypeStruct(a.shape, BF16),
+        grid=a.shape[:1],
+        in_specs=[block, block],
+        out_specs=block,
+        compiler_params=params(),
+        cost_estimate=cost(5),
+    )(a, b)
+
+
 def swap(block, axis, bit):
     size = lax.axis_size(axis)
     return lax.ppermute(block, axis, [(n, n ^ bit) for n in range(size)])
@@ -1082,7 +1099,7 @@
     packed_grad = back(0, lead, 15, meta, ())
     table = meta
     if direct:
-        sum_two = added(after(keep_two, packed_grad), swap(send_two, "bal", 1))
+        sum_two = added_parcels(after(keep_two, packed_grad), swap(send_two, "bal", 1))
         share_two = lax.psum_scatter(sum_two, "dp", scatter_dimension=0, tiled=True)[0]
         table = after(meta, sum_two)
         y_send = after(y_send, sum_two)

time: 415 us -> 412 us (level)
  Pallas kernels: 250 us -> 280 us
  starting transfers between devices: 78.4 us -> 55 us
  other arithmetic: 15 us -> 7.1 us
    ppermute x14, starting transfers between devices: 63.4 us -> 40.1 us  [swap(): return lax.ppermute(block, axis, [(n, n ^ bit) for n in range(size)])]
    pallas_call x0 -> x1, Pallas kernels: none -> 8.69 us  [added_parcels(): pl.pallas_call(add_kernel, out_shape=jax.ShapeDtypeStruct(a.shape, BF16),...]
    pallas_call x2, Pallas kernels: 31.8 us -> 40.4 us  [attend_back(): pl.pallas_call(functools.partial(attend_back_kernel, first, per), out_sha...]
    convert_element_type x6 -> x5, other arithmetic: 10.3 us -> 2.45 us  [added(): return (a.astype(F32) + b.astype(F32)).astype(BF16)]
    pallas_call x1, Pallas kernels: 114 us -> 121 us  [mlp(): pl.pallas_call(functools.partial(mlp_kernel, CHUNK, length), out_shape=(j...]
    ppermute x14, waiting for transfers between devices: 43.5 us -> 39.2 us  [swap(): return lax.ppermute(block, axis, [(n, n ^ bit) for n in range(size)])]
  transfers between devices with their start and end apart: 20 -> 20, of which waited for: 14 -> 14; matrix products, arithmetic and copies ran while one was open for 1% -> 1% of each run, Pallas kernels for 30% -> 34%
where the time goes in v5:
time: 412 us; the launch traced here: 411 us
  Pallas kernels  280 us (68%)
  starting transfers between devices  55 us (13%)
  waiting for transfers between devices  51.6 us (13%)
  between operations  14.6 us (4%)
  other arithmetic  7.1 us (2%)
    pallas_call x1, Pallas kernels, mlp(): pl.pallas_call(functools.partial(mlp_kernel, CHUNK, length), out_shape=(j...  121 us
    pallas_call x1, Pallas kernels, first_half(): pl.pallas_call(attend_kernel, out_shape=(jax.ShapeDtypeStruct((total, wid...  52.9 us
    pallas_call x2, Pallas kernels, attend_back(): pl.pallas_call(functools.partial(attend_back_kernel, first, per), out_sha...  40.4 us
    ppermute x14, starting transfers between devices, swap(): return lax.ppermute(block, axis, [(n, n ^ bit) for n in range(size)])  40.1 us
    ppermute x14, waiting for transfers between devices, swap(): return lax.ppermute(block, axis, [(n, n ^ bit) for n in range(size)])  39.2 us
    pallas_call x1, Pallas kernels, token_grad(): pl.pallas_call(token_grad_kernel, out_shape=(jax.ShapeDtypeStruct((steps,...  22 us
    pallas_call x1, Pallas kernels, qkv_grad(): pl.pallas_call(qkv_grad_kernel, out_shape=(jax.ShapeDtypeStruct((BLOCKS,...  17.6 us
    all_to_all x2, waiting for transfers between devices, exchange(): return lax.all_to_all(flat, 'bal', split_axis=0, concat_axis=0, tiled=True)  10.9 us
  transfers between devices with their start and end apart: 20, of which 14 were waited for; matrix products, arithmetic and copies ran while one was open for 1% of the time, Pallas kernels for 34%

profile of v5, /device:TPU:0, one launch (start us, length us, event | category | flops | bytes accessed | tf_op | source)
XLA Modules:
  0.0 410.6 jit_solution(14830103895998627933)
XLA Ops:
  7.2 0.5 collective-permute-start
  7.7 2.6 collective-permute-start.1
  10.3 1.4 collective-permute-start.2
  11.6 0.4 collective-permute-done.1.rest_1_
  12.0 1.1 collective-permute-done.2.rest_2_
  13.2 0.6 copy-done.4
  13.7 9.6 %shard_map.307 = (s32[128]{0:T(128)}, s32[16]{0:T(128)}, f32[16,768]{1,0:T(8,128)}, bf16[4,4,232,768]{3,2,1,0:T(8,128)(2,1)}) custom-call(s32[4,4]{1,0:T(4,128)} %counts.1, s32[4,4]{1,0:T(4,128)} %present.1, s32[4,4]{1,0:T(4,128)} %slots.1, s32[1]{0:T(128)} %bitcast.me, bf16[4,225,4,768]{3,2,1,0:T(4,128)(2,1)} %bitcast.26, s32[4,4]{1,0:T(4,128)} %copy-done.2, ...), custom_call_target="tpu_custom_call" | custom-call | tf_op jit(solution)/shard_map/pallas_call | solution.py:650
  23.3 5.1 %all-to-all-start = ((bf16[4,928,768]{2,1,0:T(8,128)(2,1)}), bf16[4,928,768]{2,1,0:T(8,128)(2,1)}, u32[]{:S(2)}, u32[]{:S(2)}) async-start(bf16[4,928,768]{2,1,0:T(8,128)(2,1)} %bitcast.24), calls=%async_computation | async-start | bytes 11403264 | tf_op jit(solution)/shard_map/all_to_all | solution.py:1068
  28.5 0.5 multiply_exponential_fusion.slopes
  29.0 52.9 %shard_map.308 = (bf16[4096,768]{1,0:T(8,128)(2,1)}, bf16[4096,2304]{1,0:T(8,128)(2,1)}, bf16[4096,768]{1,0:T(8,128)(2,1)}, f32[16,6,8,256]{3,2,1,0:T(8,128)}) custom-call(s32[128]{0:T(128)} %get-tuple-element.67.meta, f32[16]{0:T(128)} %multiply_exponential_fusion.slopes, bf16[4,225,4,768]{3,2,1,0:T(4,128)(2,1)} %bitcast.30, s32[4,4,225]{2,1,0:T(4,128)} %rows_in.5, ...), custom_call_target="tpu_custom_call" | custom-call | flops 40000000000 | bytes 4000000 | tf_op jit(solution)/shard_map/pallas_call | solution.py:694
  81.9 10.9 %all-to-all-done = bf16[4,928,768]{2,1,0:T(8,128)(2,1)} async-done(((bf16[4,928,768]{2,1,0:T(8,128)(2,1)}), bf16[4,928,768]{2,1,0:T(8,128)(2,1)}, u32[]{:S(2)}, u32[]{:S(2)}) %all-to-all-start) | async-done | bytes 5701664 | tf_op jit(solution)/shard_map/all_to_all | solution.py:1068
  92.8 121.5 %shard_map.309 = (bf16[4,4,232,768]{3,2,1,0:T(8,128)(2,1)}, f32[4096,768]{1,0:T(8,128)}, bf16[4096,768]{1,0:T(8,128)(2,1)}, bf16[8,432,768]{2,1,0:T(8,128)(2,1)}...) custom-call(s32[128]{0:T(128)} %get-tuple-element.67.meta, ...), custom_call_target="tpu_custom_call" | custom-call | flops 109999996928 | bytes 11000000 | tf_op jit(solution)/shard_map/pallas_call | solution.py:751
  214.3 21.1 %collective-permute-start.3 = (bf16[8,432,768]{2,1,0:T(8,128)(2,1)}, bf16[8,432,768]{2,1,0:T(8,128)(2,1)}, u32[]{:S(2)}, u32[]{:S(2)}) collective-permute-start(bf16[8,432,768]{2,1,0:T(8,128)(2,1)} %get-tuple-element.59), channel_id=1, source_target_pairs={{0,1},{1,0},{2,3},{3,2},{4,5},{5,4},{6,7},{7,6},{8,9},{9,8},{10,11... | collective-permute-start | bytes 15925256 | tf_op jit(solution)/shard_map/ppermute | solution.py:959
  235.4 7.8 %shard_map.310.rest_0_ = bf16[4096,2304]{1,0:T(8,128)(2,1)} custom-call(s32[128]{0:T(128)} %get-tuple-element.67.meta, f32[16]{0:T(128)} %multiply_exponential_fusion.slopes, bf16[4096,2304]{1,0:T(8,128)(2,1)} %get-tuple-element.55.qkv, bf16[4096,768]{1,0:T(8,128)(2,1)} %get-tuple-element.56.att_grad, f32[16,6,8,256]{3,2,1,0:T(8,128)} %get-tuple-element.57.totals, ...), custom_call_target="tpu_custom_call" | custom-call | flops 15000000512 | bytes 1500000 | tf_op jit(solution)/shard_map/pallas_call | solution.py:827
  243.2 0.9 collective-permute-done.3.b
  244.1 8.7 %shard_map.311 = bf16[8,432,768]{2,1,0:T(8,128)(2,1)} custom-call(bf16[8,432,768]{2,1,0:T(8,128)(2,1)} %get-tuple-element.58.a, bf16[8,432,768]{2,1,0:T(8,128)(2,1)} %collective-permute-done.3.b), custom_call_target="tpu_custom_call" | custom-call | flops 5000000000 | bytes 500000 | tf_op jit(solution)/shard_map/pallas_call | solution.py:946
  252.8 5.3 %all-to-all-start.1 = ((bf16[4,928,768]{2,1,0:T(8,128)(2,1)}), bf16[4,928,768]{2,1,0:T(8,128)(2,1)}, u32[]{:S(2)}, u32[]{:S(2)}) async-start(bf16[4,928,768]{2,1,0:T(8,128)(2,1)} %bitcast.23), calls=%async_computation.1 | async-start | bytes 11403264 | tf_op jit(solution)/shard_map/all_to_all | solution.py:1068
  258.2 32.5 %shard_map.312.packed_grad = bf16[4096,2304]{1,0:T(8,128)(2,1)} custom-call(s32[128]{0:T(128)} %get-tuple-element.67.meta, f32[16]{0:T(128)} %multiply_exponential_fusion.slopes, bf16[4096,2304]{1,0:T(8,128)(2,1)} %get-tuple-element.55.qkv, bf16[4096,768]{1,0:T(8,128)(2,1)} %get-tuple-element.56.att_grad, ...), custom_call_target="tpu_custom_call", output_to_operand_aliasing={{}: (7, {})} | custom-call | flops 499999997952 | bytes 50000000 | tf_op jit(solution)/shard_map/pallas_call | solution.py:827
  290.7 17.6 %shard_map.313 = (bf16[8,144,768]{2,1,0:T(8,128)(2,1)}, bf16[8,144,768]{2,1,0:T(8,128)(2,1)}, f32[8,2304]{1,0:T(8,128)}) custom-call(s32[128]{0:T(128)} %get-tuple-element.67.meta, bf16[4096,2304]{1,0:T(8,128)(2,1)} %shard_map.312.packed_grad, bf16[4096,768]{1,0:T(8,128)(2,1)} %get-tuple-element.53.tokens_in.tokens, f32[16,768]{1,0:T(8,128)} %get-tuple-element.51.vecs), custom_call_target="tpu_custom_call" | custom-call | flops 15000000512 | bytes 1500000 | tf_op jit(solution)/shard_map/pallas_call | solution.py:865
  308.3 9.7 %collective-permute-start.4 = (bf16[8,144,768]{2,1,0:T(8,128)(2,1)}, bf16[8,144,768]{2,1,0:T(8,128)(2,1)S(1)}, u32[]{:S(2)}, u32[]{:S(2)}) collective-permute-start(bf16[8,144,768]{2,1,0:T(8,128)(2,1)} %get-tuple-element.66), channel_id=1, source_target_pairs={{0,1},{1,0},{2,3},{3,2},{4,5},{5,4},{6,7},{7,6},{8,9},{9,8},{10,11... | collective-permute-start | bytes 5308424 | tf_op jit(solution)/shard_map/ppermute | solution.py:959
  318.1 3.5 collective-permute-done.4
  321.6 1.9 add_convert_fusion
  323.5 0.1 dynamic-slice_bitcast_fusion.1
  323.7 7.0 %shard_map.314 = bf16[4,225,4,768]{3,2,1,0:T(4,128)(2,1)} custom-call(s32[16]{0:T(128)} %get-tuple-element.62.take, bf16[4,4,232,768]{3,2,1,0:T(8,128)(2,1)} %bitcast.6.got), custom_call_target="tpu_custom_call" | custom-call | tf_op jit(solution)/shard_map/pallas_call | solution.py:675
  330.8 22.0 %shard_map.315 = (f32[4,225,4,768]{3,2,1,0:T(4,128)}, f32[16,768]{1,0:T(8,128)}) custom-call(s32[128]{0:T(128)} %get-tuple-element.67.meta, bf16[4096,2304]{1,0:T(8,128)(2,1)} %shard_map.312.packed_grad, bf16[4096,768]{1,0:T(8,128)(2,1)} %get-tuple-element.53.tokens_in.tokens, f32[4096,768]{1,0:T(8,128)} %get-tuple-element.68.mid_grad, ...), custom_call_target="tpu_custom_call" | custom-call | flops 20000000000 | bytes 2000000 | tf_op jit(solution)/shard_map/pallas_call | solution.py:901
  352.7 0.2 add_convert_fusion.1
  353.1 0.4 copy-done.1
  353.5 3.2 collective-permute-start.5
  356.8 0.9 collective-permute-done.5
  357.6 0.4 collective-permute-start.6
  358.0 3.7 collective-permute-done.6
  361.9 4.0 collective-permute-done.7
  365.9 8.6 %collective-permute-done.9 = bf16[2,144,768]{2,1,0:T(8,128)(2,1)S(1)} collective-permute-done((bf16[2,144,768]{2,1,0:T(8,128)(2,1)S(1)}, bf16[2,144,768]{2,1,0:T(8,128)(2,1)S(1)}, u32[]{:S(2)}, u32[]{:S(2)}) %collective-permute-start.9) | collective-permute-done | bytes 442400 | tf_op jit(solution)/shard_map/ppermute | solution.py:959
  374.8 2.6 collective-permute-start.15
  377.5 3.8 collective-permute-done.10
  381.3 6.3 %collective-permute-done.11 = bf16[1,144,768]{2,1,0:T(8,128)(2,1)S(1)} collective-permute-done((bf16[1,144,768]{2,1,0:T(8,128)(2,1)S(1)}, bf16[1,144,768]{2,1,0:T(8,128)(2,1)S(1)}, u32[]{:S(2)}, u32[]{:S(2)}) %collective-permute-start.11) | collective-permute-done | bytes 221216 | tf_op jit(solution)/shard_map/ppermute | solution.py:959
  387.7 2.0 collective-permute-start.13
  389.7 5.0 %collective-permute-done.12 = f32[16,768]{1,0:T(8,128)S(1)} collective-permute-done((f32[16,768]{1,0:T(8,128)S(1)}, f32[16,768]{1,0:T(8,128)S(1)}, u32[]{:S(2)}, u32[]{:S(2)}) %collective-permute-start.12) | collective-permute-done | bytes 49184 | tf_op jit(solution)/shard_map/ppermute | solution.py:959
  394.7 0.6 reshape.70
  395.3 0.7 slice_reduce_fusion
  396.0 1.7 collective-permute-done.13
  397.8 0.2 add_convert_fusion.2
  398.0 0.5 collective-permute-start.16
  398.5 0.7 collective-permute-done.14
  399.3 1.0 maximum_convert_fusion.2
  400.6 0.7 maximum_convert_fusion.3
  401.3 1.1 maximum_convert_fusion
  402.4 1.1 maximum_convert_fusion.1
  (41 shorter events, 1.2 us)
Async XLA Ops:
  7.2 4.5 %collective-permute-start = (s32[4,4]{1,0:T(4,128)}, s32[4,4]{1,0:T(4,128)S(1)}, u32[]{:S(2)}, u32[]{:S(2)}) collective-permute-start(s32[4,4]{1,0:T(4,128)} %slots.1), channel_id=1, source_target_pairs={{0,1},{1,2},{2,3},{3,0},{4,5},{5,6},{6,7},{7,4},{8,9},{9,10},{10,1... | collective-permute-start | bytes 200 | tf_op jit(solution)/shard_map/ppermute | solution.py:1075
  7.7 4.3 %collective-permute-start.1 = (s32[4,4]{1,0:T(4,128)}, s32[4,4]{1,0:T(4,128)S(1)}, u32[]{:S(2)}, u32[]{:S(2)}) collective-permute-start(s32[4,4]{1,0:T(4,128)} %slots.1), channel_id=1, source_target_pairs={{0,2},{1,3},{2,0},{3,1},{4,6},{5,7},{6,4},{7,5},{8,10},{9,11},{10,... | collective-permute-start | bytes 200 | tf_op jit(solution)/shard_map/ppermute | solution.py:1075
  10.3 2.9 collective-permute-start.2
  11.6 1.5 copy-start.2
  12.0 1.1 copy-start.3
  13.2 0.6 copy-start.4
  23.3 69.5 %all-to-all-start = ((bf16[4,928,768]{2,1,0:T(8,128)(2,1)}), bf16[4,928,768]{2,1,0:T(8,128)(2,1)}, u32[]{:S(2)}, u32[]{:S(2)}) async-start(bf16[4,928,768]{2,1,0:T(8,128)(2,1)} %bitcast.24), calls=%async_computation | async-start | bytes 11403264 | tf_op jit(solution)/shard_map/all_to_all | solution.py:1068
  28.4 346.3 %reduce-scatter.2.cloned.1.call-start = ((), (), s32[]{:S(2)}) async-start(), calls=%async_computation.3 | async-start | bytes 5971968 | tf_op jit(solution)/shard_map/reduce_scatter | solution.py:1103
  214.3 29.8 %collective-permute-start.3 = (bf16[8,432,768]{2,1,0:T(8,128)(2,1)}, bf16[8,432,768]{2,1,0:T(8,128)(2,1)}, u32[]{:S(2)}, u32[]{:S(2)}) collective-permute-start(bf16[8,432,768]{2,1,0:T(8,128)(2,1)} %get-tuple-element.59), channel_id=1, source_target_pairs={{0,1},{1,0},{2,3},{3,2},{4,5},{5,4},{6,7},{7,6},{8,9},{9,8},{10,11... | collective-permute-start | bytes 15925256 | tf_op jit(solution)/shard_map/ppermute | solution.py:959
  252.8 70.9 %all-to-all-start.1 = ((bf16[4,928,768]{2,1,0:T(8,128)(2,1)}), bf16[4,928,768]{2,1,0:T(8,128)(2,1)}, u32[]{:S(2)}, u32[]{:S(2)}) async-start(bf16[4,928,768]{2,1,0:T(8,128)(2,1)} %bitcast.23), calls=%async_computation.1 | async-start | bytes 11403264 | tf_op jit(solution)/shard_map/all_to_all | solution.py:1068
  308.3 13.3 %collective-permute-start.4 = (bf16[8,144,768]{2,1,0:T(8,128)(2,1)}, bf16[8,144,768]{2,1,0:T(8,128)(2,1)S(1)}, u32[]{:S(2)}, u32[]{:S(2)}) collective-permute-start(bf16[8,144,768]{2,1,0:T(8,128)(2,1)} %get-tuple-element.66), channel_id=1, source_target_pairs={{0,1},{1,0},{2,3},{3,2},{4,5},{5,4},{6,7},{7,6},{8,9},{9,8},{10,11... | collective-permute-start | bytes 5308424 | tf_op jit(solution)/shard_map/ppermute | solution.py:959
  323.6 29.1 %collective-permute-start.8 = (bf16[4,144,768]{2,1,0:T(8,128)(2,1)S(1)}, bf16[4,144,768]{2,1,0:T(8,128)(2,1)S(1)}, u32[]{:S(2)}, u32[]{:S(2)}) collective-permute-start(bf16[4,144,768]{2,1,0:T(8,128)(2,1)S(1)} %get-tuple-element.90), channel_id=1, source_target_pairs={{0,4},{4,0},{8,12},{12,8},{16,20},{20,16},{24,28},{28,24},{1,5},{5... | collective-permute-start | bytes 2654216 | tf_op jit(solution)/shard_map/ppermute | solution.py:959
  352.7 0.8 copy-start.1
  353.0 21.4 %collective-permute-start.9 = (bf16[2,144,768]{2,1,0:T(8,128)(2,1)S(1)}, bf16[2,144,768]{2,1,0:T(8,128)(2,1)S(1)}, u32[]{:S(2)}, u32[]{:S(2)}) collective-permute-start(bf16[2,144,768]{2,1,0:T(8,128)(2,1)S(1)} %get-tuple-element.94), channel_id=1, source_target_pairs={{0,8},{4,12},{8,0},{12,4},{16,24},{20,28},{24,16},{28,20},{1,9},{5... | collective-permute-start | bytes 1327112 | tf_op jit(solution)/shard_map/ppermute | solution.py:959
  353.5 4.1 collective-permute-start.5
  357.6 4.1 collective-permute-start.6
  361.7 4.2 %collective-permute-start.7 = (f32[16,768]{1,0:T(8,128)S(1)}, f32[16,768]{1,0:T(8,128)S(1)}, u32[]{:S(2)}, u32[]{:S(2)}) collective-permute-start(f32[16,768]{1,0:T(8,128)S(1)} %add.87), channel_id=1, source_target_pairs={{0,4},{4,0},{8,12},{12,8},{16,20},{20,16},{24,28},{28,24},{1,5},{5... | collective-permute-start | bytes 147464 | tf_op jit(solution)/shard_map/ppermute | solution.py:959
  374.6 13.0 %collective-permute-start.11 = (bf16[1,144,768]{2,1,0:T(8,128)(2,1)S(1)}, bf16[1,144,768]{2,1,0:T(8,128)(2,1)S(1)}, u32[]{:S(2)}, u32[]{:S(2)}) collective-permute-start(bf16[1,144,768]{2,1,0:T(8,128)(2,1)S(1)} %get-tuple-element.106), channel_id=1, source_target_pairs={{0,16},{4,20},{8,24},{12,28},{16,0},{20,4},{24,8},{28,12},{1,17},{... | collective-permute-start | bytes 663560 | tf_op jit(solution)/shard_map/ppermute | solution.py:959
  374.7 23.1 %copy-start = (bf16[1,432,768]{2,1,0:T(8,128)(2,1)S(1)}, bf16[1,432,768]{2,1,0:T(8,128)(2,1)}, u32[]{:S(2)}) copy-start(bf16[1,432,768]{2,1,0:T(8,128)(2,1)} %reduce-scatter.2.cloned.1.call-done) | copy-start | bytes 1990660
  374.7 6.6 %collective-permute-start.10 = (f32[16,768]{1,0:T(8,128)S(1)}, f32[16,768]{1,0:T(8,128)S(1)}, u32[]{:S(2)}, u32[]{:S(2)}) collective-permute-start(f32[16,768]{1,0:T(8,128)S(1)} %add.88), channel_id=1, source_target_pairs={{0,8},{4,12},{8,0},{12,4},{16,24},{20,28},{24,16},{28,20},{1,9},{5... | collective-permute-start | bytes 147464 | tf_op jit(solution)/shard_map/ppermute | solution.py:959
  374.8 23.0 %collective-permute-start.15 = (bf16[432,768]{1,0:T(8,128)(2,1)}, bf16[432,768]{1,0:T(8,128)(2,1)S(1)}, u32[]{:S(2)}, u32[]{:S(2)}) collective-permute-start(bf16[432,768]{1,0:T(8,128)(2,1)} %bitcast.28), channel_id=1, source_target_pairs={{0,2},{1,3},{2,0},{3,1},{4,6},{5,7},{6,4},{7,5},{8,10},{9,11},{10,... | collective-permute-start | bytes 1990664 | tf_op jit(solution)/shard_map/ppermute | solution.py:959
  387.7 10.0 %collective-permute-start.13 = (bf16[144,768]{1,0:T(8,128)(2,1)S(1)}, bf16[144,768]{1,0:T(8,128)(2,1)S(1)}, u32[]{:S(2)}, u32[]{:S(2)}) collective-permute-start(bf16[144,768]{1,0:T(8,128)(2,1)S(1)} %fusion), channel_id=1, source_target_pairs={{0,2},{1,3},{2,0},{3,1},{4,6},{5,7},{6,4},{7,5},{8,10},{9,11},{10,... | collective-permute-start | bytes 663560 | tf_op jit(solution)/shard_map/ppermute | solution.py:959
  389.7 5.0 %collective-permute-start.12 = (f32[16,768]{1,0:T(8,128)S(1)}, f32[16,768]{1,0:T(8,128)S(1)}, u32[]{:S(2)}, u32[]{:S(2)}) collective-permute-start(f32[16,768]{1,0:T(8,128)S(1)} %add.97), channel_id=1, source_target_pairs={{0,16},{4,20},{8,24},{12,28},{16,0},{20,4},{24,8},{28,12},{1,17},{... | collective-permute-start | bytes 147464 | tf_op jit(solution)/shard_map/ppermute | solution.py:959
  397.7 1.5 collective-permute-start.14
  398.0 2.3 collective-permute-start.16
Sparse Core Ops, SparseCore 0:
  252.9 120.3 reduce-scatter.1
